TPU v7x, 256 devices: a whole 4x4x8 slice. The times are simulated.
256 devices in a mesh: grp: 8 (over z), seq: 32 (over x, y, core).
Axes of the slice: x: 4, y: 4, z: 8, core: 2. Of those that a mesh axis runs over, the one named last changes fastest.
Arguments:
- query_gate: bfloat16 [8, 32, 131072], P('grp', None, 'seq'), may hold values from -6 to 6
- key_stream: bfloat16 [8, 32, 131072], P('grp', None, 'seq'), may hold values from -6 to 6
- value_stream: bfloat16 [8, 32, 131072], P('grp', None, 'seq'), may hold values from -6 to 6
- filter_taps: float32 [32, 131072], P(None, 'seq')
- skip_gain: float32 [32], replicated, may hold values from -3 to 3
- page_pool: bfloat16 [8, 32, 16, 32, 512], P('grp', 'seq'), may hold values from -6 to 6
- page_owner: int32 [8, 256], P('grp', 'seq'), may hold values from 0 to 7, as said below
- page_slot: int32 [8, 256], P('grp', 'seq'), may hold values from 0 to 15, as said below
- suffix_blocks: int32 [8], P('grp'), may hold values from 1 to 64, as said below
Outputs:
- gated_output: bfloat16 [8, 32, 131072], P('grp', None, 'seq')
Inputs may be any that keep to these rules, and one draw needn't show every extreme that they name: `page_owner`: for a block b below 256 - suffix_blocks[s], entry [s, b] is the index along grp of the device holding that block's page; that device stands at index b // 8 along seq. Of one session's blocks in one range of 8 blocks, at most 2 share an owner, and some owner holds exactly 2 in every draw. Entries of later blocks are not used. `page_slot`: entry [s, b] is the block's slot in its owner's pool: session s's pages lie in slots s * 2 to s * 2 + 1, distinct among one owner's pages of one session and range. Entries of blocks at or past 256 - suffix_blocks[s] are not used. The last suffix_blocks[s] blocks of session s are fresh; the earlier ones are cached.
All inputs are finite; a program needn't handle non-finite values.
Results may differ from a plain program's by a relative error of at most 0.012.
Values may be sent and summed in bfloat16 or wider, within the bound.
No kernel may reach another device: no remote copies, remote signals or barrier semaphores. Data moves between devices by JAX's collectives and lax.ppermute only.
A program may use at most 64 MiB of HBM per device.

v0:
```python
import functools

import jax
import jax.numpy as jnp
import ml_dtypes
import numpy as np
from jax import lax
from jax.experimental import pallas as pl
from jax.experimental.pallas import tpu as pltpu
from jax.sharding import PartitionSpec as P

N1 = 256
N2 = 512
HALF = N2 // 2
TOTAL = N1 * N2
BF16 = jnp.bfloat16
F32 = jnp.float32


def split_table(table):
    high = table.astype(ml_dtypes.bfloat16)
    low = (table - high.astype(np.float64)).astype(ml_dtypes.bfloat16)
    return high, low


@functools.cache
def tables():
    k1 = np.arange(N1)[:, None] + 0.25
    n1 = np.arange(N1)[None, :]
    rows = np.exp(-2j * np.pi * k1 * n1 / N1)
    high, low = split_table(np.concatenate([rows.real, rows.imag], axis=0))
    first = np.concatenate([high, low], axis=0)
    twiddle = np.exp(-2j * np.pi * k1 * np.arange(N2)[None, :] / TOTAL)
    m = np.arange(HALF)[:, None]
    l = np.arange(HALF)[None, :]
    second_high, second_low = [], []
    for p in range(2):
        f = np.exp(-2j * np.pi * m * (l + 0.5 * p) / HALF)
        full = np.block([[f.real, f.imag], [-f.imag, f.real]])
        high, low = split_table(full)
        second_high.append(high)
        second_low.append(low)
    back = rows.conj().T / TOTAL
    high, low = split_table(np.concatenate([back.real, -back.imag], axis=1))
    last = np.concatenate([high, low], axis=0)
    return (
        first,
        twiddle.real.astype(np.float32),
        twiddle.imag.astype(np.float32),
        np.stack(second_high),
        np.stack(second_low),
        last,
    )


def dot(a, b):
    return jnp.dot(a, b, preferred_element_type=F32)


def dot_t(a, b):
    return lax.dot_general(a, b, (((1,), (1,)), ((), ())), preferred_element_type=F32)


def scatter_block(ref, a, block):
    for t in range(4):
        ref[t, pl.ds(a, 32, stride=8), :] = block[:, t * 128 : (t + 1) * 128]


def stage_kernel(key_ref, value_ref, taps_ref, send_ref, signal_ref, scratch_ref):
    for a in range(8):
        cols = slice(a * N2, (a + 1) * N2)
        fresh = key_ref[:, cols].astype(F32) * value_ref[:, cols].astype(F32)
        scatter_block(signal_ref, a, fresh)
        scatter_block(scratch_ref, a, taps_ref[:, cols])
    for t in range(4):
        send_ref[:, N2 + t * 128 : N2 + (t + 1) * 128] = scratch_ref[t].astype(BF16)


def select_kernel(index_ref, cached_ref, pages_ref, send_in_ref, signal_in_ref, send_ref, signal_ref):
    send_ref[:, N2:] = send_in_ref[:, N2:]
    signal_ref[...] = signal_in_ref[...]
    for a in range(8):

        @pl.when(cached_ref[a] != 0)
        def _():
            scatter_block(signal_ref, a, pages_ref[index_ref[a]].astype(F32))

    for t in range(4):
        send_ref[:, t * 128 : (t + 1) * 128] = signal_ref[t].astype(BF16)


def conv_kernel(x_ref, first_ref, cos_ref, sin_ref, high_ref, low_ref, last_ref, out_ref):
    part = dot(first_ref[...], x_ref[...])
    real = part[:N1] + part[2 * N1 : 3 * N1]
    imag = part[N1 : 2 * N1] + part[3 * N1 :]
    cosine = cos_ref[...]
    sine = sin_ref[...]
    sums, gaps = [], []
    for item in range(2):
        cols = slice(item * N2, (item + 1) * N2)
        r, i = real[:, cols], imag[:, cols]
        br = r * cosine - i * sine
        bi = r * sine + i * cosine
        sums.append(
            jnp.concatenate([br[:, :HALF] + br[:, HALF:], bi[:, :HALF] + bi[:, HALF:]], axis=1)
        )
        gaps.append(
            jnp.concatenate([br[:, :HALF] - br[:, HALF:], bi[:, :HALF] - bi[:, HALF:]], axis=1)
        )
    turned = []
    for p, pieces in enumerate((sums, gaps)):
        c = jnp.concatenate(pieces, axis=0).astype(BF16)
        spec = dot(c, high_ref[p]) + dot(c, low_ref[p])
        xr, xi = spec[:N1, :HALF], spec[:N1, HALF:]
        hr, hi = spec[N1:, :HALF], spec[N1:, HALF:]
        prod = jnp.concatenate([xr * hr - xi * hi, xr * hi + xi * hr], axis=1).astype(BF16)
        turned.append(dot_t(prod, high_ref[p]) + dot_t(prod, low_ref[p]))
    plus = turned[0] + turned[1]
    minus = turned[0] - turned[1]
    dr = jnp.concatenate([plus[:, :HALF], minus[:, :HALF]], axis=1)
    di = jnp.concatenate([plus[:, HALF:], minus[:, HALF:]], axis=1)
    er = (dr * cosine + di * sine).astype(BF16)
    ei = (di * cosine - dr * sine).astype(BF16)
    part = dot(last_ref[...], jnp.concatenate([er, ei], axis=0))
    out_ref[...] = (part[:N1] + part[N1:]).astype(BF16)


def gate_kernel(conv_ref, signal_ref, gain_ref, query_ref, out_ref, scratch_ref):
    gain = gain_ref[...]
    for t in range(4):
        conv = conv_ref[:, t * 128 : (t + 1) * 128].astype(F32)
        scratch_ref[t] = conv + gain * signal_ref[t]
    for a in range(8):
        for t in range(4):
            cols = slice(a * N2 + t * 128, a * N2 + (t + 1) * 128)
            total = scratch_ref[t, pl.ds(a, 32, stride=8), :]
            out_ref[:, cols] = (query_ref[:, cols].astype(F32) * total).astype(BF16)


def params():
    return pltpu.CompilerParams(vmem_limit_bytes=48 * 1024 * 1024)


def cost(flops, moved):
    return pl.CostEstimate(flops=flops, bytes_accessed=moved, transcendentals=0)


VMEM = pl.BlockSpec(memory_space=pltpu.VMEM)
SMEM = pl.BlockSpec(memory_space=pltpu.SMEM)


def shards(
    query_gate,
    key_stream,
    value_stream,
    filter_taps,
    skip_gain,
    page_pool,
    page_owner,
    page_slot,
    suffix_blocks,
):
    seq_index = lax.axis_index("seq")
    grp_index = lax.axis_index("grp")
    outgoing = page_pool.reshape(8, 2, 32, N2)
    arrived = lax.all_to_all(outgoing, "grp", split_axis=0, concat_axis=0, tiled=True)
    arrived = arrived.reshape(16, 32, N2)

    index = jnp.clip(page_owner[0] * 2 + page_slot[0] - grp_index * 2, 0, 15)
    block_ids = seq_index * 8 + jnp.arange(8, dtype=jnp.int32)
    cached = (block_ids < 256 - suffix_blocks[0]).astype(jnp.int32)
    gain = jnp.repeat(skip_gain, 8)[:, None]

    send, signal = pl.pallas_call(
        stage_kernel,
        out_shape=(
            jax.ShapeDtypeStruct((N1, 2 * N2), BF16),
            jax.ShapeDtypeStruct((4, N1, 128), F32),
        ),
        in_specs=[VMEM] * 3,
        out_specs=(VMEM, VMEM),
        scratch_shapes=[pltpu.VMEM((4, N1, 128), F32)],
        compiler_params=params(),
        cost_estimate=cost(1 << 18, 1 << 21),
        name="stage",
    )(key_stream[0], value_stream[0], filter_taps)

    send, signal = pl.pallas_call(
        select_kernel,
        out_shape=(
            jax.ShapeDtypeStruct((N1, 2 * N2), BF16),
            jax.ShapeDtypeStruct((4, N1, 128), F32),
        ),
        in_specs=[SMEM, SMEM, VMEM, VMEM, VMEM],
        out_specs=(VMEM, VMEM),
        compiler_params=params(),
        cost_estimate=cost(1 << 18, 1 << 21),
        name="select",
    )(index, cached, arrived, send, signal)

    columns = lax.all_to_all(
        send.reshape(32, 8, 2 * N2), "seq", split_axis=0, concat_axis=0, tiled=True
    ).reshape(N1, 2 * N2)

    convolved = pl.pallas_call(
        conv_kernel,
        out_shape=jax.ShapeDtypeStruct((N1, N2), BF16),
        in_specs=[VMEM] * 7,
        out_specs=VMEM,
        compiler_params=params(),
        cost_estimate=cost(1 << 31, 1 << 23),
        name="conv",
    )(columns, *[jnp.asarray(t) for t in tables()])

    back = lax.all_to_all(
        convolved.reshape(32, 8, N2), "seq", split_axis=0, concat_axis=0, tiled=True
    ).reshape(N1, N2)

    gated = pl.pallas_call(
        gate_kernel,
        out_shape=jax.ShapeDtypeStruct((32, 8 * N2), BF16),
        in_specs=[VMEM] * 4,
        out_specs=VMEM,
        scratch_shapes=[pltpu.VMEM((4, N1, 128), F32)],
        compiler_params=params(),
        cost_estimate=cost(1 << 18, 1 << 21),
        name="gate",
    )(back, signal, gain, query_gate[0])
    return gated[None]


def solution(mesh):
    return jax.shard_map(
        shards,
        mesh=mesh,
        in_specs=(
            P("grp", None, "seq"),
            P("grp", None, "seq"),
            P("grp", None, "seq"),
            P(None, "seq"),
            P(),
            P("grp", "seq", None, None, None),
            P("grp", "seq"),
            P("grp", "seq"),
            P("grp"),
        ),
        out_specs=P("grp", None, "seq"),
        check_vma=False,
    )
```

profile of v0, /device:TPU:1, one launch (start us, length us, event | category | flops | bytes accessed | tf_op | source)
XLA Modules:
  0.0 66.8 jit_solution(8745420593932692812)
XLA Ops:
  0.0 0.0 copy-start
  0.0 0.0 copy-start.1
  0.0 0.0 copy-start.2
  0.0 9.2 %all-to-all-start = ((bf16[8,2,32,512]{3,2,1,0:T(8,128)(2,1)}), bf16[8,2,32,512]{3,2,1,0:T(8,128)(2,1)S(1)}, u32[]{:S(2)}, u32[]{:S(2)}) async-start(bf16[8,2,32,512]{3,2,1,0:T(8,128)(2,1)} %bitcast.20), calls=%async_computation | async-start | bytes 1048576 | tf_op jit(solution)/shard_map/all_to_all | solution.py:166
  9.2 0.0 copy-done
  9.2 0.0 copy-done.1
  9.2 0.0 copy-done.2
  9.2 0.0 copy-start.7
  9.2 0.3 stage.1
  10.2 0.0 copy-start.11
  10.2 0.0 copy-start.12
  10.2 0.6 copy-done.11
  10.8 0.0 copy-done.12
  10.9 16.3 %all-to-all-done = bf16[8,2,32,512]{3,2,1,0:T(8,128)(2,1)S(1)} async-done(((bf16[8,2,32,512]{3,2,1,0:T(8,128)(2,1)}), bf16[8,2,32,512]{3,2,1,0:T(8,128)(2,1)S(1)}, u32[]{:S(2)}, u32[]{:S(2)}) %all-to-all-start) | async-done | bytes 524320 | tf_op jit(solution)/shard_map/all_to_all | solution.py:166
  27.1 0.8 %select.1 = (bf16[256,1024]{1,0:T(8,128)(2,1)S(1)}, f32[4,256,128]{2,1,0:T(8,128)S(1)}) custom-call(s32[8]{0:T(128)S(1)} %clamp_bitcast_fusion.index_ref, s32[8]{0:T(128)S(1)} %compare_convert_fusion.cached_ref, bf16[16,32,512]{2,1,0:T(8,128)(2,1)S(1)} %bitcast.13, bf16[256,1024]{1,0:T(8,128)(2,1)S(1)} %get-tuple-element.9.send_in_ref, ...), custom_call_target="tpu_custom_call" | custom-call | flops 262144 | bytes 2097152 | tf_op jit(solution)/shard_map/select/pallas_call | solution.py:188
  27.9 0.0 copy-start.6
  27.9 19.1 %all_to_all.15 = bf16[32,8,1024]{2,1,0:T(8,128)(2,1)S(1)} all-to-all(bf16[32,8,1024]{2,1,0:T(8,128)(2,1)S(1)} %bitcast.15), channel_id=1, replica_groups=mesh['grp'=8,'seq'=32] {'seq'}, dimensions={0} | all-to-all | bytes 1048576 | tf_op jit(solution)/shard_map/all_to_all | solution.py:201
  47.1 0.0 copy-done.7
  47.1 0.0 copy-done.4
  47.1 0.0 copy-done.5
  47.1 0.0 copy-done.6
  47.1 0.0 copy-start.8
  47.1 1.0 %copy-done.8 = f32[256,512]{1,0:T(8,128)S(1)} copy-done((f32[256,512]{1,0:T(8,128)S(1)}, f32[256,512]{1,0:T(8,128)}, u32[]{:S(2)}) %copy-start.8) | copy-done | bytes 524312
  48.1 1.0 %copy-done.9 = bf16[512,512]{1,0:T(8,128)(2,1)S(1)} copy-done((bf16[512,512]{1,0:T(8,128)(2,1)S(1)}, bf16[512,512]{1,0:T(8,128)(2,1)}, u32[]{:S(2)}) %copy-start.9) | copy-done | bytes 524312
  49.2 3.9 %conv.1 = bf16[256,512]{1,0:T(8,128)(2,1)} custom-call(bf16[256,1024]{1,0:T(8,128)(2,1)S(1)} %bitcast.16, bf16[1024,256]{1,0:T(8,128)(2,1)S(1)} %copy-done.6, f32[256,512]{1,0:T(8,128)S(1)} %copy-done.7, f32[256,512]{1,0:T(8,128)S(1)} %copy-done.8, bf16[2,512,512]{2,1,0:T(8,128)(2,1)S(1)} %copy-done.4, bf16[2,512,512]{2,1,0:T(8,128)(2,1)S(1)} %copy-done.5, ...), custom_call_target="tpu_custom_call" | custom-call | flops 2147483648 | bytes 8388608 | tf_op jit(solution)/shard_map/conv/pallas_call | solution.py:205
  53.1 3.8 %all-to-all-start.2 = ((bf16[32,8,512]{2,1,0:T(8,128)(2,1)}), bf16[32,8,512]{2,1,0:T(8,128)(2,1)S(1)}, u32[]{:S(2)}, u32[]{:S(2)}) async-start(bf16[32,8,512]{2,1,0:T(8,128)(2,1)} %bitcast.8), calls=%async_computation.2 | async-start | bytes 524288 | tf_op jit(solution)/shard_map/all_to_all | solution.py:215
  56.9 0.0 copy-done.10
  56.9 0.1 broadcast_in_dim.6
  57.0 0.1 broadcast_in_dim_reshape.4.gain_ref
  57.1 8.8 %all-to-all-done.2 = bf16[32,8,512]{2,1,0:T(8,128)(2,1)S(1)} async-done(((bf16[32,8,512]{2,1,0:T(8,128)(2,1)}), bf16[32,8,512]{2,1,0:T(8,128)(2,1)S(1)}, u32[]{:S(2)}, u32[]{:S(2)}) %all-to-all-start.2) | async-done | bytes 262176 | tf_op jit(solution)/shard_map/all_to_all | solution.py:215
  65.8 0.0 copy-done.3
  65.8 0.9 %gate.1 = bf16[32,4096]{1,0:T(8,128)(2,1)} custom-call(bf16[256,512]{1,0:T(8,128)(2,1)S(1)} %bitcast.14, f32[4,256,128]{2,1,0:T(8,128)S(1)} %get-tuple-element.12.signal_ref, f32[256,1]{1,0:T(8,128)S(1)} %broadcast_in_dim_reshape.4.gain_ref, bf16[32,4096]{1,0:T(8,128)(2,1)S(1)} %bitcast.19), custom_call_target="tpu_custom_call" | custom-call | flops 262144 | bytes 2097152 | tf_op jit(solution)/shard_map/gate/pallas_call | solution.py:219
  (7 shorter events, 0.0 us)
Async XLA Ops:
  0.0 9.2 %copy-start = (f32[32,4096]{1,0:T(8,128)S(1)}, f32[32,4096]{1,0:T(8,128)}, u32[]{:S(2)}) copy-start(f32[32,4096]{1,0:T(8,128)} %taps_ref.1) | copy-start | bytes 1572868
  0.0 9.2 %copy-start.1 = (bf16[1,32,4096]{2,1,0:T(8,128)(2,1)S(1)}, bf16[1,32,4096]{2,1,0:T(8,128)(2,1)}, u32[]{:S(2)}) copy-start(bf16[1,32,4096]{2,1,0:T(8,128)(2,1)} %param.16) | copy-start | bytes 786436
  0.0 9.2 %copy-start.2 = (bf16[1,32,4096]{2,1,0:T(8,128)(2,1)S(1)}, bf16[1,32,4096]{2,1,0:T(8,128)(2,1)}, u32[]{:S(2)}) copy-start(bf16[1,32,4096]{2,1,0:T(8,128)(2,1)} %param.17) | copy-start | bytes 786436
  0.0 27.1 %all-to-all-start = ((bf16[8,2,32,512]{3,2,1,0:T(8,128)(2,1)}), bf16[8,2,32,512]{3,2,1,0:T(8,128)(2,1)S(1)}, u32[]{:S(2)}, u32[]{:S(2)}) async-start(bf16[8,2,32,512]{3,2,1,0:T(8,128)(2,1)} %bitcast.20), calls=%async_computation | async-start | bytes 1048576 | tf_op jit(solution)/shard_map/all_to_all | solution.py:166
  9.2 37.9 %copy-start.7 = (f32[256,512]{1,0:T(8,128)S(1)}, f32[256,512]{1,0:T(8,128)}, u32[]{:S(2)}) copy-start(f32[256,512]{1,0:T(8,128)} %constant.34.clone.cos_ref) | copy-start | bytes 1572868
  10.2 0.7 copy-start.11
  10.2 0.7 copy-start.12
  27.1 20.0 %copy-start.4 = (bf16[2,512,512]{2,1,0:T(8,128)(2,1)S(1)}, bf16[2,512,512]{2,1,0:T(8,128)(2,1)}, u32[]{:S(2)}) copy-start(bf16[2,512,512]{2,1,0:T(8,128)(2,1)} %constant.36.clone.high_ref) | copy-start | bytes 3145732
  27.1 20.0 %copy-start.5 = (bf16[2,512,512]{2,1,0:T(8,128)(2,1)S(1)}, bf16[2,512,512]{2,1,0:T(8,128)(2,1)}, u32[]{:S(2)}) copy-start(bf16[2,512,512]{2,1,0:T(8,128)(2,1)} %constant.37.clone.low_ref) | copy-start | bytes 3145732
  27.9 19.2 %copy-start.6 = (bf16[1024,256]{1,0:T(8,128)(2,1)S(1)}, bf16[1024,256]{1,0:T(8,128)(2,1)}, u32[]{:S(2)}) copy-start(bf16[1024,256]{1,0:T(8,128)(2,1)} %constant.33.clone.first_ref) | copy-start | bytes 1572868
  47.1 1.0 %copy-start.8 = (f32[256,512]{1,0:T(8,128)S(1)}, f32[256,512]{1,0:T(8,128)}, u32[]{:S(2)}) copy-start(f32[256,512]{1,0:T(8,128)} %constant.35.clone.sin_ref) | copy-start | bytes 1572868
  48.1 1.0 %copy-start.9 = (bf16[512,512]{1,0:T(8,128)(2,1)S(1)}, bf16[512,512]{1,0:T(8,128)(2,1)}, u32[]{:S(2)}) copy-start(bf16[512,512]{1,0:T(8,128)(2,1)} %constant.38.clone.last_ref) | copy-start | bytes 1572868
  53.1 3.8 %copy-start.10 = (f32[32]{0:T(128)S(1)}, f32[32]{0:T(128)}, u32[]{:S(2)}) copy-start(f32[32]{0:T(128)} %param.19) | copy-start | bytes 388
  53.1 12.8 %copy-start.3 = (bf16[1,32,4096]{2,1,0:T(8,128)(2,1)S(1)}, bf16[1,32,4096]{2,1,0:T(8,128)(2,1)}, u32[]{:S(2)}) copy-start(bf16[1,32,4096]{2,1,0:T(8,128)(2,1)} %param.15) | copy-start | bytes 786436
  53.1 12.7 %all-to-all-start.2 = ((bf16[32,8,512]{2,1,0:T(8,128)(2,1)}), bf16[32,8,512]{2,1,0:T(8,128)(2,1)S(1)}, u32[]{:S(2)}, u32[]{:S(2)}) async-start(bf16[32,8,512]{2,1,0:T(8,128)(2,1)} %bitcast.8), calls=%async_computation.2 | async-start | bytes 524288 | tf_op jit(solution)/shard_map/all_to_all | solution.py:215
where the time goes:
time: 67.2 us; the launch traced here: 66.8 us
  waiting for transfers between devices  25 us (37%)
  blocking collectives  19.1 us (28%)
  starting transfers between devices  12.9 us (19%)
  Pallas kernels  5.92 us (9%)
  local copies, waits for them, and re-layouts  2.93 us (4%)
  between operations  0.79 us (1%)
    all_to_all x1, blocking collectives, shards(): lax.all_to_all(send.reshape(32, 8, 2 * N2), 'seq', split_axis=0, concat_a...  19.1 us
    all_to_all x1, waiting for transfers between devices, shards(): lax.all_to_all(outgoing, 'grp', split_axis=0, concat_axis=0, tiled=True)  16.3 us
    all_to_all x1, starting transfers between devices, shards(): lax.all_to_all(outgoing, 'grp', split_axis=0, concat_axis=0, tiled=True)  9.16 us
    all_to_all x1, waiting for transfers between devices, shards(): lax.all_to_all(convolved.reshape(32, 8, N2), 'seq', split_axis=0, concat_...  8.77 us
    pallas_call x1, Pallas kernels, shards(): pl.pallas_call(conv_kernel, out_shape=jax.ShapeDtypeStruct((N1, N2), BF16...  3.89 us
    all_to_all x1, starting transfers between devices, shards(): lax.all_to_all(convolved.reshape(32, 8, N2), 'seq', split_axis=0, concat_...  3.79 us
    unnamed x26, local copies, waits for them, and re-layouts  2.76 us
  transfers between devices with their start and end apart: 2, of which 2 were waited for; matrix products, arithmetic and copies ran while one was open for 0% of the time, Pallas kernels for 0%

commit v1 on v0

--- a/solution.py
+++ b/solution.py
@@ -36,8 +36,7 @@
     second_high, second_low = [], []
     for p in range(2):
         f = np.exp(-2j * np.pi * m * (l + 0.5 * p) / HALF)
-        full = np.block([[f.real, f.imag], [-f.imag, f.real]])
-        high, low = split_table(full)
+        high, low = split_table(np.concatenate([f.real, f.imag], axis=1))
         second_high.append(high)
         second_low.append(low)
     back = rows.conj().T / TOTAL
@@ -66,6 +65,24 @@
         ref[t, pl.ds(a, 32, stride=8), :] = block[:, t * 128 : (t + 1) * 128]
 
 
+def whole_table(half):
+    return jnp.concatenate(
+        [half, jnp.concatenate([-half[:, HALF:], half[:, :HALF]], axis=1)], axis=0
+    )
+
+
+def cut_kernel(grp_ref, pool_ref, *rest):
+    outs, sems = rest[:7], rest[7]
+    copies = []
+    for d in range(1, 8):
+        slab = lax.rem(grp_ref[0] + d, 8)
+        copy = pltpu.make_async_copy(pool_ref.at[slab], outs[d - 1], sems.at[d - 1])
+        copy.start()
+        copies.append(copy)
+    for copy in copies:
+        copy.wait()
+
+
 def stage_kernel(key_ref, value_ref, taps_ref, send_ref, signal_ref, scratch_ref):
     for a in range(8):
         cols = slice(a * N2, (a + 1) * N2)
@@ -76,14 +93,16 @@
         send_ref[:, N2 + t * 128 : N2 + (t + 1) * 128] = scratch_ref[t].astype(BF16)
 
 
-def select_kernel(index_ref, cached_ref, pages_ref, send_in_ref, signal_in_ref, send_ref, signal_ref):
+def select_kernel(row_ref, *rest):
+    pages, (send_in_ref, signal_in_ref, send_ref, signal_ref) = rest[:8], rest[8:]
     send_ref[:, N2:] = send_in_ref[:, N2:]
     signal_ref[...] = signal_in_ref[...]
-    for a in range(8):
-
-        @pl.when(cached_ref[a] != 0)
+    for j in range(16):
+        row = row_ref[j]
+
+        @pl.when(row >= 0)
         def _():
-            scatter_block(signal_ref, a, pages_ref[index_ref[a]].astype(F32))
+            scatter_block(signal_ref, row, pages[j // 2][j % 2].astype(F32))
 
     for t in range(4):
         send_ref[:, t * 128 : (t + 1) * 128] = signal_ref[t].astype(BF16)
@@ -110,11 +129,13 @@
     turned = []
     for p, pieces in enumerate((sums, gaps)):
         c = jnp.concatenate(pieces, axis=0).astype(BF16)
-        spec = dot(c, high_ref[p]) + dot(c, low_ref[p])
+        high = whole_table(high_ref[p])
+        low = whole_table(low_ref[p])
+        spec = dot(c, high) + dot(c, low)
         xr, xi = spec[:N1, :HALF], spec[:N1, HALF:]
         hr, hi = spec[N1:, :HALF], spec[N1:, HALF:]
         prod = jnp.concatenate([xr * hr - xi * hi, xr * hi + xi * hr], axis=1).astype(BF16)
-        turned.append(dot_t(prod, high_ref[p]) + dot_t(prod, low_ref[p]))
+        turned.append(dot_t(prod, high) + dot_t(prod, low))
     plus = turned[0] + turned[1]
     minus = turned[0] - turned[1]
     dr = jnp.concatenate([plus[:, :HALF], minus[:, :HALF]], axis=1)
@@ -162,13 +183,26 @@
 ):
     seq_index = lax.axis_index("seq")
     grp_index = lax.axis_index("grp")
-    outgoing = page_pool.reshape(8, 2, 32, N2)
-    arrived = lax.all_to_all(outgoing, "grp", split_axis=0, concat_axis=0, tiled=True)
-    arrived = arrived.reshape(16, 32, N2)
-
-    index = jnp.clip(page_owner[0] * 2 + page_slot[0] - grp_index * 2, 0, 15)
+    pool = page_pool.reshape(8, 2, 32, N2)
+    parts = pl.pallas_call(
+        cut_kernel,
+        out_shape=[jax.ShapeDtypeStruct((2, 32, N2), BF16)] * 7,
+        in_specs=[SMEM, pl.BlockSpec(memory_space=pl.ANY)],
+        out_specs=[VMEM] * 7,
+        scratch_shapes=[pltpu.SemaphoreType.DMA((7,))],
+        compiler_params=params(),
+        cost_estimate=cost(0, 1 << 20),
+        name="cut",
+    )(grp_index[None], pool)
+    arrived = [lax.dynamic_index_in_dim(pool, grp_index, 0, keepdims=False)]
+    for d in range(1, 8):
+        arrived.append(lax.ppermute(parts[d - 1], "grp", [(z, (z + d) % 8) for z in range(8)]))
+
     block_ids = seq_index * 8 + jnp.arange(8, dtype=jnp.int32)
-    cached = (block_ids < 256 - suffix_blocks[0]).astype(jnp.int32)
+    cached = block_ids < 256 - suffix_blocks[0]
+    index = ((grp_index - page_owner[0]) & 7) * 2 + page_slot[0] - grp_index * 2
+    hits = (index[None, :] == jnp.arange(16, dtype=jnp.int32)[:, None]) & cached[None, :]
+    rows = jnp.max(jnp.where(hits, jnp.arange(8, dtype=jnp.int32)[None, :], -1), axis=1)
     gain = jnp.repeat(skip_gain, 8)[:, None]
 
     send, signal = pl.pallas_call(
@@ -191,12 +225,12 @@
             jax.ShapeDtypeStruct((N1, 2 * N2), BF16),
             jax.ShapeDtypeStruct((4, N1, 128), F32),
         ),
-        in_specs=[SMEM, SMEM, VMEM, VMEM, VMEM],
+        in_specs=[SMEM] + [VMEM] * 10,
         out_specs=(VMEM, VMEM),
         compiler_params=params(),
         cost_estimate=cost(1 << 18, 1 << 21),
         name="select",
-    )(index, cached, arrived, send, signal)
+    )(rows, *arrived, send, signal)
 
     columns = lax.all_to_all(
         send.reshape(32, 8, 2 * N2), "seq", split_axis=0, concat_axis=0, tiled=True

time: 67.2 us -> 66.3 us (0.987)
  waiting for transfers between devices: 25 us -> 12.1 us
  starting transfers between devices: 12.9 us -> 21.2 us
  local copies, waits for them, and re-layouts: 2.93 us -> 4.63 us
  blocking collectives: 19.1 us -> 20.4 us
  Pallas kernels: 5.92 us -> 6.63 us
    ppermute x0 -> x7, starting transfers between devices: none -> 17.4 us  [shards(): lax.ppermute(parts[d - 1], 'grp', [(z, (z + d) % 8) for z in range(8)])]
    all_to_all x1 -> x0, waiting for transfers between devices: 16.3 us -> none  [shards(): lax.all_to_all(outgoing, 'grp', split_axis=0, concat_axis=0, tiled=True)]
    all_to_all x1 -> x0, starting transfers between devices: 9.16 us -> none  [shards(): lax.all_to_all(outgoing, 'grp', split_axis=0, concat_axis=0, tiled=True)]
    ppermute x0 -> x7, waiting for transfers between devices: none -> 3.37 us  [shards(): lax.ppermute(parts[d - 1], 'grp', [(z, (z + d) % 8) for z in range(8)])]
    all_to_all x1, blocking collectives: 19.1 us -> 20.4 us  [shards(): lax.all_to_all(send.reshape(32, 8, 2 * N2), 'seq', split_axis=0, concat_a...]
    unnamed x26 -> x28, local copies, waits for them, and re-layouts: 2.76 us -> 3.62 us
    squeeze x0 -> x1, local copies, waits for them, and re-layouts: none -> 0.84 us  [shards(): arrived = [lax.dynamic_index_in_dim(pool, grp_index, 0, keepdims=False)]]
    pallas_call x0 -> x1, Pallas kernels: none -> 0.67 us  [shards(): pl.pallas_call(cut_kernel, out_shape=[jax.ShapeDtypeStruct((2, 32, N2), B...]
  transfers between devices with their start and end apart: 2 -> 8, of which waited for: 2 -> 3; matrix products, arithmetic and copies ran while one was open for 0% -> 2% of each run, Pallas kernels for 0% -> 0%
where the time goes in v1:
time: 66.3 us; the launch traced here: 65.9 us
  starting transfers between devices  21.2 us (32%)
  blocking collectives  20.4 us (31%)
  waiting for transfers between devices  12.1 us (18%)
  Pallas kernels  6.63 us (10%)
  local copies, waits for them, and re-layouts  4.63 us (7%)
  between operations  0.8 us (1%)
    all_to_all x1, blocking collectives, shards(): lax.all_to_all(send.reshape(32, 8, 2 * N2), 'seq', split_axis=0, concat_a...  20.4 us
    ppermute x7, starting transfers between devices, shards(): lax.ppermute(parts[d - 1], 'grp', [(z, (z + d) % 8) for z in range(8)])  17.4 us
    all_to_all x1, waiting for transfers between devices, shards(): lax.all_to_all(convolved.reshape(32, 8, N2), 'seq', split_axis=0, concat_...  8.77 us
    pallas_call x1, Pallas kernels, shards(): pl.pallas_call(conv_kernel, out_shape=jax.ShapeDtypeStruct((N1, N2), BF16...  3.89 us
    all_to_all x1, starting transfers between devices, shards(): lax.all_to_all(convolved.reshape(32, 8, N2), 'seq', split_axis=0, concat_...  3.79 us
    unnamed x28, local copies, waits for them, and re-layouts  3.62 us
    ppermute x7, waiting for transfers between devices, shards(): lax.ppermute(parts[d - 1], 'grp', [(z, (z + d) % 8) for z in range(8)])  3.37 us
  transfers between devices with their start and end apart: 8, of which 3 were waited for; matrix products, arithmetic and copies ran while one was open for 2% of the time, Pallas kernels for 0%

profile of v1, /device:TPU:1, one launch (start us, length us, event | category | flops | bytes accessed | tf_op | source)
XLA Modules:
  0.0 65.9 jit_solution(13768841910841901767)
XLA Ops:
  0.0 1.0 %copy-done = bf16[1,1,16,32,512]{4,3,2,1,0:T(8,128)(2,1)S(1)} copy-done((bf16[1,1,16,32,512]{4,3,2,1,0:T(8,128)(2,1)S(1)}, bf16[1,1,16,32,512]{4,3,2,1,0:T(8,128)(2,1)}, u32[]{:S(2)}) %copy-start) | copy-done | bytes 524312
  1.0 0.7 %cut.1 = (bf16[2,32,512]{2,1,0:T(8,128)(2,1)S(1)}, bf16[2,32,512]{2,1,0:T(8,128)(2,1)S(1)}, bf16[2,32,512]{2,1,0:T(8,128)(2,1)S(1)}, bf16[2,32,512]{2,1,0:T(8,12...) custom-call(s32[1]{0:T(128)} %bitcast.4.grp_ref, ...), custom_call_target="tpu_custom_call" | custom-call | bytes 1048576 | tf_op jit(solution)/shard_map/cut/pallas_call | solution.py:187
  1.7 2.5 %collective-permute-start = (bf16[2,32,512]{2,1,0:T(8,128)(2,1)S(1)}, bf16[2,32,512]{2,1,0:T(8,128)(2,1)S(1)}, u32[]{:S(2)}, u32[]{:S(2)}) collective-permute-start(bf16[2,32,512]{2,1,0:T(8,128)(2,1)S(1)} %get-tuple-element.16), channel_id=1, source_target_pairs={{0,32},{32,64},{64,96},{96,128},{128,160},{160,192},{192,224},{224... | collective-permute-start | bytes 196616 | tf_op jit(solution)/shard_map/ppermute | solution.py:199
  4.3 3.0 %collective-permute-start.1 = (bf16[2,32,512]{2,1,0:T(8,128)(2,1)S(1)}, bf16[2,32,512]{2,1,0:T(8,128)(2,1)S(1)}, u32[]{:S(2)}, u32[]{:S(2)}) collective-permute-start(bf16[2,32,512]{2,1,0:T(8,128)(2,1)S(1)} %get-tuple-element.17), channel_id=1, source_target_pairs={{0,64},{32,96},{64,128},{96,160},{128,192},{160,224},{192,0},{224,... | collective-permute-start | bytes 196616 | tf_op jit(solution)/shard_map/ppermute | solution.py:199
  7.3 3.8 %collective-permute-start.2 = (bf16[2,32,512]{2,1,0:T(8,128)(2,1)S(1)}, bf16[2,32,512]{2,1,0:T(8,128)(2,1)S(1)}, u32[]{:S(2)}, u32[]{:S(2)}) collective-permute-start(bf16[2,32,512]{2,1,0:T(8,128)(2,1)S(1)} %get-tuple-element.18), channel_id=1, source_target_pairs={{0,96},{32,128},{64,160},{96,192},{128,224},{160,0},{192,32},{224,... | collective-permute-start | bytes 196616 | tf_op jit(solution)/shard_map/ppermute | solution.py:199
  11.0 0.5 collective-permute-start.3
  11.5 4.5 %collective-permute-start.4 = (bf16[2,32,512]{2,1,0:T(8,128)(2,1)S(1)}, bf16[2,32,512]{2,1,0:T(8,128)(2,1)S(1)}, u32[]{:S(2)}, u32[]{:S(2)}) collective-permute-start(bf16[2,32,512]{2,1,0:T(8,128)(2,1)S(1)} %get-tuple-element.20), channel_id=1, source_target_pairs={{0,160},{32,192},{64,224},{96,0},{128,32},{160,64},{192,96},{224,1... | collective-permute-start | bytes 196616 | tf_op jit(solution)/shard_map/ppermute | solution.py:199
  16.6 0.0 copy-start.11
  16.6 0.0 copy-start.12
  16.6 0.6 copy-done.11
  17.3 0.0 copy-done.12
  17.3 0.9 %copy-done.2 = bf16[1,32,4096]{2,1,0:T(8,128)(2,1)S(1)} copy-done((bf16[1,32,4096]{2,1,0:T(8,128)(2,1)S(1)}, bf16[1,32,4096]{2,1,0:T(8,128)(2,1)}, u32[]{:S(2)}) %copy-start.2) | copy-done | bytes 262168
  18.2 0.9 %copy-done.3 = bf16[1,32,4096]{2,1,0:T(8,128)(2,1)S(1)} copy-done((bf16[1,32,4096]{2,1,0:T(8,128)(2,1)S(1)}, bf16[1,32,4096]{2,1,0:T(8,128)(2,1)}, u32[]{:S(2)}) %copy-start.3) | copy-done | bytes 262168
  19.2 0.3 stage.1
  19.5 0.1 select_reduce_fusion.row_ref
  19.6 0.0 collective-permute-done.rest_1_
  19.6 2.5 %collective-permute-start.5 = (bf16[2,32,512]{2,1,0:T(8,128)(2,1)S(1)}, bf16[2,32,512]{2,1,0:T(8,128)(2,1)S(1)}, u32[]{:S(2)}, u32[]{:S(2)}) collective-permute-start(bf16[2,32,512]{2,1,0:T(8,128)(2,1)S(1)} %get-tuple-element.21), channel_id=1, source_target_pairs={{0,192},{32,224},{64,0},{96,32},{128,64},{160,96},{192,128},{224,1... | collective-permute-start | bytes 196616 | tf_op jit(solution)/shard_map/ppermute | solution.py:199
  22.1 0.0 collective-permute-done.1.rest_2_
  22.1 0.7 %collective-permute-start.6 = (bf16[2,32,512]{2,1,0:T(8,128)(2,1)S(1)}, bf16[2,32,512]{2,1,0:T(8,128)(2,1)S(1)}, u32[]{:S(2)}, u32[]{:S(2)}) collective-permute-start(bf16[2,32,512]{2,1,0:T(8,128)(2,1)S(1)} %get-tuple-element.22), channel_id=1, source_target_pairs={{0,224},{32,0},{64,32},{96,64},{128,96},{160,128},{192,160},{224,1... | collective-permute-start | bytes 196616 | tf_op jit(solution)/shard_map/ppermute | solution.py:199
  22.8 0.8 %dynamic-slice_bitcast_fusion.rest_0_ = bf16[2,32,512]{2,1,0:T(8,128)(2,1)S(1)} fusion(bf16[8,2,32,512]{3,2,1,0:T(8,128)(2,1)} %bitcast.16, s32[]{:T(128)S(6)} %select_n.9), kind=kLoop, calls=%fused_computation | loop fusion | bytes 131076 | tf_op jit(solution)/shard_map/jit(dynamic_index_in_dim)/squeeze | solution.py:197
  23.7 1.7 %collective-permute-done.5.rest_6_ = bf16[2,32,512]{2,1,0:T(8,128)(2,1)S(1)} collective-permute-done((bf16[2,32,512]{2,1,0:T(8,128)(2,1)S(1)}, bf16[2,32,512]{2,1,0:T(8,128)(2,1)S(1)}, u32[]{:S(2)}, u32[]{:S(2)}) %collective-permute-start.5) | collective-permute-done | bytes 65568 | tf_op jit(solution)/shard_map/ppermute | solution.py:199
  25.3 1.7 %collective-permute-done.6.rest_7_ = bf16[2,32,512]{2,1,0:T(8,128)(2,1)S(1)} collective-permute-done((bf16[2,32,512]{2,1,0:T(8,128)(2,1)S(1)}, bf16[2,32,512]{2,1,0:T(8,128)(2,1)S(1)}, u32[]{:S(2)}, u32[]{:S(2)}) %collective-permute-start.6) | collective-permute-done | bytes 65568 | tf_op jit(solution)/shard_map/ppermute | solution.py:199
  27.0 0.8 %select.1 = (bf16[256,1024]{1,0:T(8,128)(2,1)S(1)}, f32[4,256,128]{2,1,0:T(8,128)S(1)}) custom-call(s32[16]{0:T(128)S(1)} %select_reduce_fusion.row_ref, bf16[2,32,512]{2,1,0:T(8,128)(2,1)S(1)} %dynamic-slice_bitcast_fusion.rest_0_, bf16[2,32,512]{2,1,0:T(8,128)(2,1)S(1)} %collective-permute-done.rest_1_, ...), custom_call_target="tpu_custom_call" | custom-call | flops 262144 | bytes 2097152 | tf_op jit(solution)/shard_map/select/pallas_call | solution.py:222
  27.9 0.0 copy-start.5
  27.9 0.0 copy-start.6
  27.9 20.4 %all_to_all.10 = bf16[32,8,1024]{2,1,0:T(8,128)(2,1)S(1)} all-to-all(bf16[32,8,1024]{2,1,0:T(8,128)(2,1)S(1)} %bitcast.18), channel_id=1, replica_groups=mesh['grp'=8,'seq'=32] {'seq'}, dimensions={0} | all-to-all | bytes 1048576 | tf_op jit(solution)/shard_map/all_to_all | solution.py:235
  48.4 3.9 %conv.1 = bf16[256,512]{1,0:T(8,128)(2,1)} custom-call(bf16[256,1024]{1,0:T(8,128)(2,1)S(1)} %bitcast.19, bf16[1024,256]{1,0:T(8,128)(2,1)S(1)} %copy-done.5, f32[256,512]{1,0:T(8,128)S(1)} %copy-done.6, f32[256,512]{1,0:T(8,128)S(1)} %copy-done.7, bf16[2,256,512]{2,1,0:T(8,128)(2,1)S(1)} %copy-done.8, bf16[2,256,512]{2,1,0:T(8,128)(2,1)S(1)} %copy-done.9, ...), custom_call_target="tpu_custom_call" | custom-call | flops 2147483648 | bytes 8388608 | tf_op jit(solution)/shard_map/conv/pallas_call | solution.py:239
  52.3 3.8 %all-to-all-start.1 = ((bf16[32,8,512]{2,1,0:T(8,128)(2,1)}), bf16[32,8,512]{2,1,0:T(8,128)(2,1)S(1)}, u32[]{:S(2)}, u32[]{:S(2)}) async-start(bf16[32,8,512]{2,1,0:T(8,128)(2,1)} %bitcast.9), calls=%async_computation.1 | async-start | bytes 524288 | tf_op jit(solution)/shard_map/all_to_all | solution.py:249
  56.1 0.1 broadcast_in_dim.28
  56.1 0.1 broadcast_in_dim_reshape.4.gain_ref
  56.2 8.8 %all-to-all-done.1 = bf16[32,8,512]{2,1,0:T(8,128)(2,1)S(1)} async-done(((bf16[32,8,512]{2,1,0:T(8,128)(2,1)}), bf16[32,8,512]{2,1,0:T(8,128)(2,1)S(1)}, u32[]{:S(2)}, u32[]{:S(2)}) %all-to-all-start.1) | async-done | bytes 262176 | tf_op jit(solution)/shard_map/all_to_all | solution.py:249
  65.0 0.9 %gate.1 = bf16[32,4096]{1,0:T(8,128)(2,1)} custom-call(bf16[256,512]{1,0:T(8,128)(2,1)S(1)} %bitcast.15, f32[4,256,128]{2,1,0:T(8,128)S(1)} %get-tuple-element.26.signal_ref, f32[256,1]{1,0:T(8,128)S(1)} %broadcast_in_dim_reshape.4.gain_ref, bf16[32,4096]{1,0:T(8,128)(2,1)S(1)} %bitcast.22), custom_call_target="tpu_custom_call" | custom-call | flops 262144 | bytes 2097152 | tf_op jit(solution)/shard_map/gate/pallas_call | solution.py:253
  (24 shorter events, 0.1 us)
Async XLA Ops:
  0.0 1.0 %copy-start = (bf16[1,1,16,32,512]{4,3,2,1,0:T(8,128)(2,1)S(1)}, bf16[1,1,16,32,512]{4,3,2,1,0:T(8,128)(2,1)}, u32[]{:S(2)}) copy-start(bf16[1,1,16,32,512]{4,3,2,1,0:T(8,128)(2,1)} %param.20) | copy-start | bytes 1572868
  1.0 16.2 %copy-start.1 = (f32[32,4096]{1,0:T(8,128)S(1)}, f32[32,4096]{1,0:T(8,128)}, u32[]{:S(2)}) copy-start(f32[32,4096]{1,0:T(8,128)} %taps_ref.1) | copy-start | bytes 1572868
  1.7 17.9 %collective-permute-start = (bf16[2,32,512]{2,1,0:T(8,128)(2,1)S(1)}, bf16[2,32,512]{2,1,0:T(8,128)(2,1)S(1)}, u32[]{:S(2)}, u32[]{:S(2)}) collective-permute-start(bf16[2,32,512]{2,1,0:T(8,128)(2,1)S(1)} %get-tuple-element.16), channel_id=1, source_target_pairs={{0,32},{32,64},{64,96},{96,128},{128,160},{160,192},{192,224},{224... | collective-permute-start | bytes 196616 | tf_op jit(solution)/shard_map/ppermute | solution.py:199
  4.3 17.8 %collective-permute-start.1 = (bf16[2,32,512]{2,1,0:T(8,128)(2,1)S(1)}, bf16[2,32,512]{2,1,0:T(8,128)(2,1)S(1)}, u32[]{:S(2)}, u32[]{:S(2)}) collective-permute-start(bf16[2,32,512]{2,1,0:T(8,128)(2,1)S(1)} %get-tuple-element.17), channel_id=1, source_target_pairs={{0,64},{32,96},{64,128},{96,160},{128,192},{160,224},{192,0},{224,... | collective-permute-start | bytes 196616 | tf_op jit(solution)/shard_map/ppermute | solution.py:199
  7.3 16.4 %collective-permute-start.2 = (bf16[2,32,512]{2,1,0:T(8,128)(2,1)S(1)}, bf16[2,32,512]{2,1,0:T(8,128)(2,1)S(1)}, u32[]{:S(2)}, u32[]{:S(2)}) collective-permute-start(bf16[2,32,512]{2,1,0:T(8,128)(2,1)S(1)} %get-tuple-element.18), channel_id=1, source_target_pairs={{0,96},{32,128},{64,160},{96,192},{128,224},{160,0},{192,32},{224,... | collective-permute-start | bytes 196616 | tf_op jit(solution)/shard_map/ppermute | solution.py:199
  11.0 12.6 %collective-permute-start.3 = (bf16[2,32,512]{2,1,0:T(8,128)(2,1)S(1)}, bf16[2,32,512]{2,1,0:T(8,128)(2,1)S(1)}, u32[]{:S(2)}, u32[]{:S(2)}) collective-permute-start(bf16[2,32,512]{2,1,0:T(8,128)(2,1)S(1)} %get-tuple-element.19), channel_id=1, source_target_pairs={{0,128},{32,160},{64,192},{96,224},{128,0},{160,32},{192,64},{224,... | collective-permute-start | bytes 196616 | tf_op jit(solution)/shard_map/ppermute | solution.py:199
  11.5 12.2 %collective-permute-start.4 = (bf16[2,32,512]{2,1,0:T(8,128)(2,1)S(1)}, bf16[2,32,512]{2,1,0:T(8,128)(2,1)S(1)}, u32[]{:S(2)}, u32[]{:S(2)}) collective-permute-start(bf16[2,32,512]{2,1,0:T(8,128)(2,1)S(1)} %get-tuple-element.20), channel_id=1, source_target_pairs={{0,160},{32,192},{64,224},{96,0},{128,32},{160,64},{192,96},{224,1... | collective-permute-start | bytes 196616 | tf_op jit(solution)/shard_map/ppermute | solution.py:199
  16.6 0.7 copy-start.11
  16.6 0.7 %copy-start.12 = (s32[1,8]{1,0:T(1,128)S(1)}, s32[1,8]{1,0:T(1,128)}, u32[]{:S(2)}) copy-start(s32[1,8]{1,0:T(1,128)} %param.21) | copy-start | bytes 100
  17.3 1.0 %copy-start.2 = (bf16[1,32,4096]{2,1,0:T(8,128)(2,1)S(1)}, bf16[1,32,4096]{2,1,0:T(8,128)(2,1)}, u32[]{:S(2)}) copy-start(bf16[1,32,4096]{2,1,0:T(8,128)(2,1)} %param.16) | copy-start | bytes 786436
  18.2 0.9 %copy-start.3 = (bf16[1,32,4096]{2,1,0:T(8,128)(2,1)S(1)}, bf16[1,32,4096]{2,1,0:T(8,128)(2,1)}, u32[]{:S(2)}) copy-start(bf16[1,32,4096]{2,1,0:T(8,128)(2,1)} %param.17) | copy-start | bytes 786436
  19.2 29.1 %copy-start.10 = (bf16[512,512]{1,0:T(8,128)(2,1)S(1)}, bf16[512,512]{1,0:T(8,128)(2,1)}, u32[]{:S(2)}) copy-start(bf16[512,512]{1,0:T(8,128)(2,1)} %constant.45.clone.last_ref) | copy-start | bytes 1572868
  19.6 5.7 %collective-permute-start.5 = (bf16[2,32,512]{2,1,0:T(8,128)(2,1)S(1)}, bf16[2,32,512]{2,1,0:T(8,128)(2,1)S(1)}, u32[]{:S(2)}, u32[]{:S(2)}) collective-permute-start(bf16[2,32,512]{2,1,0:T(8,128)(2,1)S(1)} %get-tuple-element.21), channel_id=1, source_target_pairs={{0,192},{32,224},{64,0},{96,32},{128,64},{160,96},{192,128},{224,1... | collective-permute-start | bytes 196616 | tf_op jit(solution)/shard_map/ppermute | solution.py:199
  22.1 4.9 %collective-permute-start.6 = (bf16[2,32,512]{2,1,0:T(8,128)(2,1)S(1)}, bf16[2,32,512]{2,1,0:T(8,128)(2,1)S(1)}, u32[]{:S(2)}, u32[]{:S(2)}) collective-permute-start(bf16[2,32,512]{2,1,0:T(8,128)(2,1)S(1)} %get-tuple-element.22), channel_id=1, source_target_pairs={{0,224},{32,0},{64,32},{96,64},{128,96},{160,128},{192,160},{224,1... | collective-permute-start | bytes 196616 | tf_op jit(solution)/shard_map/ppermute | solution.py:199
  27.0 21.3 %copy-start.7 = (f32[256,512]{1,0:T(8,128)S(1)}, f32[256,512]{1,0:T(8,128)}, u32[]{:S(2)}) copy-start(f32[256,512]{1,0:T(8,128)} %constant.42.clone.sin_ref) | copy-start | bytes 1572868
  27.0 21.3 %copy-start.8 = (bf16[2,256,512]{2,1,0:T(8,128)(2,1)S(1)}, bf16[2,256,512]{2,1,0:T(8,128)(2,1)}, u32[]{:S(2)}) copy-start(bf16[2,256,512]{2,1,0:T(8,128)(2,1)} %constant.43.clone.high_ref) | copy-start | bytes 1572868
  27.0 21.3 %copy-start.9 = (bf16[2,256,512]{2,1,0:T(8,128)(2,1)S(1)}, bf16[2,256,512]{2,1,0:T(8,128)(2,1)}, u32[]{:S(2)}) copy-start(bf16[2,256,512]{2,1,0:T(8,128)(2,1)} %constant.44.clone.low_ref) | copy-start | bytes 1572868
  27.9 20.5 %copy-start.5 = (bf16[1024,256]{1,0:T(8,128)(2,1)S(1)}, bf16[1024,256]{1,0:T(8,128)(2,1)}, u32[]{:S(2)}) copy-start(bf16[1024,256]{1,0:T(8,128)(2,1)} %constant.40.clone.first_ref) | copy-start | bytes 1572868
  27.9 20.5 %copy-start.6 = (f32[256,512]{1,0:T(8,128)S(1)}, f32[256,512]{1,0:T(8,128)}, u32[]{:S(2)}) copy-start(f32[256,512]{1,0:T(8,128)} %constant.41.clone.cos_ref) | copy-start | bytes 1572868
  52.2 3.8 %copy-start.13 = (f32[32]{0:T(128)S(1)}, f32[32]{0:T(128)}, u32[]{:S(2)}) copy-start(f32[32]{0:T(128)} %param.19) | copy-start | bytes 388
  52.3 12.8 %copy-start.4 = (bf16[1,32,4096]{2,1,0:T(8,128)(2,1)S(1)}, bf16[1,32,4096]{2,1,0:T(8,128)(2,1)}, u32[]{:S(2)}) copy-start(bf16[1,32,4096]{2,1,0:T(8,128)(2,1)} %param.15) | copy-start | bytes 786436
  52.3 12.8 %all-to-all-start.1 = ((bf16[32,8,512]{2,1,0:T(8,128)(2,1)}), bf16[32,8,512]{2,1,0:T(8,128)(2,1)S(1)}, u32[]{:S(2)}, u32[]{:S(2)}) async-start(bf16[32,8,512]{2,1,0:T(8,128)(2,1)} %bitcast.9), calls=%async_computation.1 | async-start | bytes 524288 | tf_op jit(solution)/shard_map/all_to_all | solution.py:249

commit v2 on v1

--- a/solution.py
+++ b/solution.py
@@ -60,52 +60,98 @@
     return lax.dot_general(a, b, (((1,), (1,)), ((), ())), preferred_element_type=F32)
 
 
-def scatter_block(ref, a, block):
-    for t in range(4):
-        ref[t, pl.ds(a, 32, stride=8), :] = block[:, t * 128 : (t + 1) * 128]
-
-
 def whole_table(half):
     return jnp.concatenate(
         [half, jnp.concatenate([-half[:, HALF:], half[:, :HALF]], axis=1)], axis=0
     )
 
 
-def cut_kernel(grp_ref, pool_ref, *rest):
-    outs, sems = rest[:7], rest[7]
-    copies = []
-    for d in range(1, 8):
-        slab = lax.rem(grp_ref[0] + d, 8)
-        copy = pltpu.make_async_copy(pool_ref.at[slab], outs[d - 1], sems.at[d - 1])
+def place_rows(key_row):
+    rows = lax.broadcasted_iota(jnp.int32, (N1, key_row.shape[1]), 0)
+    return (rows == key_row).astype(F32).astype(BF16)
+
+
+def block_order(to_send):
+    col = lax.broadcasted_iota(jnp.int32, (1, N1), 1)
+    if to_send:
+        return place_rows((col & 31) * 8 + (col >> 5))
+    return place_rows((col & 7) * 32 + (col >> 3))
+
+
+def fetch(sources, targets, sems):
+    copies = [
+        pltpu.make_async_copy(source, target, sems.at[i])
+        for i, (source, target) in enumerate(zip(sources, targets))
+    ]
+    for copy in copies:
         copy.start()
-        copies.append(copy)
     for copy in copies:
         copy.wait()
 
 
-def stage_kernel(key_ref, value_ref, taps_ref, send_ref, signal_ref, scratch_ref):
+def cut_kernel(pool_ref, *rest):
+    outs, sems = rest[:8], rest[8]
+    here = lax.axis_index("grp")
+    fetch([pool_ref.at[lax.rem(here + d, 8)] for d in range(8)], outs, sems)
+
+
+def stage_kernel(
+    owner_ref,
+    slot_ref,
+    suffix_ref,
+    gain_ref,
+    key_hbm,
+    value_hbm,
+    taps_hbm,
+    tie_ref,
+    taps_ref,
+    fresh_send_ref,
+    fresh_ref,
+    send_key_ref,
+    plain_key_ref,
+    gain_rows_ref,
+    key_ref,
+    value_ref,
+    plain_ref,
+    sems,
+):
+    del tie_ref
+    fetch([key_hbm, value_hbm, taps_hbm], [key_ref, value_ref, plain_ref], sems)
+    here = lax.axis_index("grp")
+    count = 256 - suffix_ref[0] - lax.axis_index("seq") * 8
+    column = lax.broadcasted_iota(jnp.int32, (1, 512), 1)
+    channel = column & 31
+    send_key = jnp.full((1, 512), -1, jnp.int32)
+    plain_key = jnp.full((1, 512), -1, jnp.int32)
+    taps = []
     for a in range(8):
+        page = ((here - owner_ref[0, a]) & 7) * 2 + slot_ref[0, a] - here * 2
+        hit = (column >> 5) == jnp.where(a < count, page, -1)
+        send_key = jnp.where(hit, channel * 8 + a, send_key)
+        plain_key = jnp.where(hit, channel + a * 32, plain_key)
         cols = slice(a * N2, (a + 1) * N2)
-        fresh = key_ref[:, cols].astype(F32) * value_ref[:, cols].astype(F32)
-        scatter_block(signal_ref, a, fresh)
-        scatter_block(scratch_ref, a, taps_ref[:, cols])
-    for t in range(4):
-        send_ref[:, N2 + t * 128 : N2 + (t + 1) * 128] = scratch_ref[t].astype(BF16)
-
-
-def select_kernel(row_ref, *rest):
-    pages, (send_in_ref, signal_in_ref, send_ref, signal_ref) = rest[:8], rest[8:]
-    send_ref[:, N2:] = send_in_ref[:, N2:]
-    signal_ref[...] = signal_in_ref[...]
-    for j in range(16):
-        row = row_ref[j]
-
-        @pl.when(row >= 0)
-        def _():
-            scatter_block(signal_ref, row, pages[j // 2][j % 2].astype(F32))
-
-    for t in range(4):
-        send_ref[:, t * 128 : (t + 1) * 128] = signal_ref[t].astype(BF16)
+        product = key_ref[:, cols].astype(F32) * value_ref[:, cols].astype(F32)
+        fresh_ref[a * 32 : (a + 1) * 32, :] = jnp.where(a < count, 0.0, product)
+        taps.append(plain_ref[:, cols])
+    send_key_ref[...] = send_key
+    plain_key_ref[...] = plain_key
+    lane = lax.broadcasted_iota(jnp.int32, (N1, 1), 0) & 31
+    gain = jnp.zeros((N1, 1), F32)
+    for c in range(32):
+        gain = jnp.where(lane == c, gain_ref[c], gain)
+    gain_rows_ref[...] = gain
+    order = block_order(True)
+    taps_ref[...] = dot(order, jnp.concatenate(taps, axis=0).astype(BF16)).astype(BF16)
+    fresh_send_ref[...] = dot(order, fresh_ref[...].astype(BF16)).astype(BF16)
+
+
+def select_kernel(send_key_ref, key_ref, gain_ref, taps_ref, fresh_send_ref, fresh_ref, *rest):
+    slabs, (send_ref, direct_ref) = rest[:8], rest[8:]
+    pages = jnp.concatenate([slab[...].reshape(64, N2) for slab in slabs], axis=0)
+    cached = dot(place_rows(send_key_ref[...]), pages)
+    send_ref[:, :N2] = (cached + fresh_send_ref[...].astype(F32)).astype(BF16)
+    send_ref[:, N2:] = taps_ref[...]
+    direct_ref[...] = gain_ref[...] * (dot(place_rows(key_ref[...]), pages) + fresh_ref[...])
 
 
 def conv_kernel(x_ref, first_ref, cos_ref, sin_ref, high_ref, low_ref, last_ref, out_ref):
@@ -146,28 +192,29 @@
     out_ref[...] = (part[:N1] + part[N1:]).astype(BF16)
 
 
-def gate_kernel(conv_ref, signal_ref, gain_ref, query_ref, out_ref, scratch_ref):
-    gain = gain_ref[...]
-    for t in range(4):
-        conv = conv_ref[:, t * 128 : (t + 1) * 128].astype(F32)
-        scratch_ref[t] = conv + gain * signal_ref[t]
+def gate_kernel(conv_ref, direct_ref, query_ref, out_ref):
+    total = dot(block_order(False), conv_ref[...]) + direct_ref[...]
     for a in range(8):
-        for t in range(4):
-            cols = slice(a * N2 + t * 128, a * N2 + (t + 1) * 128)
-            total = scratch_ref[t, pl.ds(a, 32, stride=8), :]
-            out_ref[:, cols] = (query_ref[:, cols].astype(F32) * total).astype(BF16)
+        cols = slice(a * N2, (a + 1) * N2)
+        query = query_ref[:, cols].astype(F32)
+        out_ref[:, cols] = (query * total[a * 32 : (a + 1) * 32, :]).astype(BF16)
 
 
 def params():
     return pltpu.CompilerParams(vmem_limit_bytes=48 * 1024 * 1024)
 
 
+def in_hbm(array):
+    return pltpu.with_memory_space_constraint(array, pltpu.HBM)
+
+
 def cost(flops, moved):
     return pl.CostEstimate(flops=flops, bytes_accessed=moved, transcendentals=0)
 
 
 VMEM = pl.BlockSpec(memory_space=pltpu.VMEM)
 SMEM = pl.BlockSpec(memory_space=pltpu.SMEM)
+HBM = pl.BlockSpec(memory_space=pltpu.HBM)
 
 
 def shards(
@@ -181,56 +228,64 @@
     page_slot,
     suffix_blocks,
 ):
-    seq_index = lax.axis_index("seq")
-    grp_index = lax.axis_index("grp")
-    pool = page_pool.reshape(8, 2, 32, N2)
-    parts = pl.pallas_call(
+    slabs = pl.pallas_call(
         cut_kernel,
-        out_shape=[jax.ShapeDtypeStruct((2, 32, N2), BF16)] * 7,
-        in_specs=[SMEM, pl.BlockSpec(memory_space=pl.ANY)],
-        out_specs=[VMEM] * 7,
-        scratch_shapes=[pltpu.SemaphoreType.DMA((7,))],
+        out_shape=[jax.ShapeDtypeStruct((2, 32, N2), BF16)] * 8,
+        in_specs=[HBM],
+        out_specs=[VMEM] * 8,
+        scratch_shapes=[pltpu.SemaphoreType.DMA((8,))],
         compiler_params=params(),
         cost_estimate=cost(0, 1 << 20),
         name="cut",
-    )(grp_index[None], pool)
-    arrived = [lax.dynamic_index_in_dim(pool, grp_index, 0, keepdims=False)]
+    )(in_hbm(page_pool.reshape(8, 2, 32, N2)))
+    slabs = list(slabs)
     for d in range(1, 8):
-        arrived.append(lax.ppermute(parts[d - 1], "grp", [(z, (z + d) % 8) for z in range(8)]))
-
-    block_ids = seq_index * 8 + jnp.arange(8, dtype=jnp.int32)
-    cached = block_ids < 256 - suffix_blocks[0]
-    index = ((grp_index - page_owner[0]) & 7) * 2 + page_slot[0] - grp_index * 2
-    hits = (index[None, :] == jnp.arange(16, dtype=jnp.int32)[:, None]) & cached[None, :]
-    rows = jnp.max(jnp.where(hits, jnp.arange(8, dtype=jnp.int32)[None, :], -1), axis=1)
-    gain = jnp.repeat(skip_gain, 8)[:, None]
-
-    send, signal = pl.pallas_call(
+        slabs[d] = lax.ppermute(slabs[d], "grp", [(z, (z + d) % 8) for z in range(8)])
+
+    taps, fresh_send, fresh, send_key, plain_key, gain = pl.pallas_call(
         stage_kernel,
         out_shape=(
-            jax.ShapeDtypeStruct((N1, 2 * N2), BF16),
-            jax.ShapeDtypeStruct((4, N1, 128), F32),
+            jax.ShapeDtypeStruct((N1, N2), BF16),
+            jax.ShapeDtypeStruct((N1, N2), BF16),
+            jax.ShapeDtypeStruct((N1, N2), F32),
+            jax.ShapeDtypeStruct((1, 512), jnp.int32),
+            jax.ShapeDtypeStruct((1, 512), jnp.int32),
+            jax.ShapeDtypeStruct((N1, 1), F32),
         ),
-        in_specs=[VMEM] * 3,
-        out_specs=(VMEM, VMEM),
-        scratch_shapes=[pltpu.VMEM((4, N1, 128), F32)],
+        in_specs=[SMEM] * 4 + [HBM] * 3 + [pl.BlockSpec(memory_space=pl.ANY)],
+        out_specs=(VMEM,) * 6,
+        scratch_shapes=[
+            pltpu.VMEM((32, 8 * N2), BF16),
+            pltpu.VMEM((32, 8 * N2), BF16),
+            pltpu.VMEM((32, 8 * N2), F32),
+            pltpu.SemaphoreType.DMA((3,)),
+        ],
         compiler_params=params(),
         cost_estimate=cost(1 << 18, 1 << 21),
         name="stage",
-    )(key_stream[0], value_stream[0], filter_taps)
-
-    send, signal = pl.pallas_call(
+    )(
+        page_owner,
+        page_slot,
+        suffix_blocks,
+        skip_gain,
+        in_hbm(key_stream[0]),
+        in_hbm(value_stream[0]),
+        in_hbm(filter_taps),
+        slabs[1],
+    )
+
+    send, direct = pl.pallas_call(
         select_kernel,
         out_shape=(
             jax.ShapeDtypeStruct((N1, 2 * N2), BF16),
-            jax.ShapeDtypeStruct((4, N1, 128), F32),
+            jax.ShapeDtypeStruct((N1, N2), F32),
         ),
-        in_specs=[SMEM] + [VMEM] * 10,
+        in_specs=[VMEM] * 14,
         out_specs=(VMEM, VMEM),
         compiler_params=params(),
         cost_estimate=cost(1 << 18, 1 << 21),
         name="select",
-    )(rows, *arrived, send, signal)
+    )(send_key, plain_key, gain, taps, fresh_send, fresh, *slabs)
 
     columns = lax.all_to_all(
         send.reshape(32, 8, 2 * N2), "seq", split_axis=0, concat_axis=0, tiled=True
@@ -253,13 +308,12 @@
     gated = pl.pallas_call(
         gate_kernel,
         out_shape=jax.ShapeDtypeStruct((32, 8 * N2), BF16),
-        in_specs=[VMEM] * 4,
+        in_specs=[VMEM] * 3,
         out_specs=VMEM,
-        scratch_shapes=[pltpu.VMEM((4, N1, 128), F32)],
         compiler_params=params(),
         cost_estimate=cost(1 << 18, 1 << 21),
         name="gate",
-    )(back, signal, gain, query_gate[0])
+    )(back, direct, query_gate[0])
     return gated[None]
 
 

time: 66.3 us -> 62.9 us (0.949)
  blocking collectives: 20.4 us -> 32.5 us
  waiting for transfers between devices: 12.1 us -> 3.39 us
  local copies, waits for them, and re-layouts: 4.63 us -> 0.7 us
  starting transfers between devices: 21.2 us -> 17.3 us
  Pallas kernels: 6.63 us -> 7.91 us
    all_to_all x0 -> x1, blocking collectives: none -> 12.5 us  [shards(): lax.all_to_all(convolved.reshape(32, 8, N2), 'seq', split_axis=0, concat_...]
    all_to_all x1 -> x0, waiting for transfers between devices: 8.77 us -> none  [shards(): lax.all_to_all(convolved.reshape(32, 8, N2), 'seq', split_axis=0, concat_...]
    all_to_all x1 -> x0, starting transfers between devices: 3.79 us -> none  [shards(): lax.all_to_all(convolved.reshape(32, 8, N2), 'seq', split_axis=0, concat_...]
    unnamed x28 -> x20, local copies, waits for them, and re-layouts: 3.62 us -> 0.7 us
    pallas_call x1, Pallas kernels: 0.31 us -> 2.21 us  [shards(): pl.pallas_call(stage_kernel, out_shape=(jax.ShapeDtypeStruct((N1, N2), BF...]
    squeeze x1 -> x0, local copies, waits for them, and re-layouts: 0.84 us -> none  [shards(): arrived = [lax.dynamic_index_in_dim(pool, grp_index, 0, keepdims=False)]]
    pallas_call x1, Pallas kernels: 3.89 us -> 3.19 us  [shards(): pl.pallas_call(conv_kernel, out_shape=jax.ShapeDtypeStruct((N1, N2), BF16...]
  transfers between devices with their start and end apart: 8 -> 7, of which waited for: 3 -> 1; matrix products, arithmetic and copies ran while one was open for 2% -> 0% of each run, Pallas kernels for 0% -> 4%
where the time goes in v2:
time: 62.9 us; the launch traced here: 62.7 us
  blocking collectives  32.5 us (52%)
  starting transfers between devices  17.3 us (28%)
  Pallas kernels  7.91 us (13%)
  waiting for transfers between devices  3.39 us (5%)
  between operations  0.8 us (1%)
  local copies, waits for them, and re-layouts  0.7 us (1%)
    all_to_all x1, blocking collectives, shards(): lax.all_to_all(send.reshape(32, 8, 2 * N2), 'seq', split_axis=0, concat_a...  20 us
    ppermute x7, starting transfers between devices, shards(): lax.ppermute(slabs[d], 'grp', [(z, (z + d) % 8) for z in range(8)])  17.3 us
    all_to_all x1, blocking collectives, shards(): lax.all_to_all(convolved.reshape(32, 8, N2), 'seq', split_axis=0, concat_...  12.5 us
    ppermute x7, waiting for transfers between devices, shards(): lax.ppermute(slabs[d], 'grp', [(z, (z + d) % 8) for z in range(8)])  3.39 us
    pallas_call x1, Pallas kernels, shards(): pl.pallas_call(conv_kernel, out_shape=jax.ShapeDtypeStruct((N1, N2), BF16...  3.19 us
    pallas_call x1, Pallas kernels, shards(): pl.pallas_call(stage_kernel, out_shape=(jax.ShapeDtypeStruct((N1, N2), BF...  2.21 us
  transfers between devices with their start and end apart: 7, of which 1 were waited for; matrix products, arithmetic and copies ran while one was open for 0% of the time, Pallas kernels for 4%

profile of v2, /device:TPU:1, one launch (start us, length us, event | category | flops | bytes accessed | tf_op | source)
XLA Modules:
  0.0 62.7 jit_solution(7039620251319467949)
XLA Ops:
  0.0 1.1 %cut.1 = (bf16[2,32,512]{2,1,0:T(8,128)(2,1)S(1)}, bf16[2,32,512]{2,1,0:T(8,128)(2,1)S(1)}, bf16[2,32,512]{2,1,0:T(8,128)(2,1)S(1)}, bf16[2,32,512]{2,1,0:T(8,12...) custom-call(bf16[8,2,32,512]{3,2,1,0:T(8,128)(2,1)} %bitcast.14), custom_call_target="tpu_custom_call" | custom-call | bytes 1048576 | tf_op jit(solution)/shard_map/cut/pallas_call | solution.py:231
  1.1 2.5 %collective-permute-start = (bf16[2,32,512]{2,1,0:T(8,128)(2,1)S(1)}, bf16[2,32,512]{2,1,0:T(8,128)(2,1)S(1)}, u32[]{:S(2)}, u32[]{:S(2)}) collective-permute-start(bf16[2,32,512]{2,1,0:T(8,128)(2,1)S(1)} %get-tuple-element.21), channel_id=1, source_target_pairs={{0,32},{32,64},{64,96},{96,128},{128,160},{160,192},{192,224},{224... | collective-permute-start | bytes 196616 | tf_op jit(solution)/shard_map/ppermute | solution.py:243
  3.7 3.0 %collective-permute-start.1 = (bf16[2,32,512]{2,1,0:T(8,128)(2,1)S(1)}, bf16[2,32,512]{2,1,0:T(8,128)(2,1)S(1)}, u32[]{:S(2)}, u32[]{:S(2)}) collective-permute-start(bf16[2,32,512]{2,1,0:T(8,128)(2,1)S(1)} %get-tuple-element.29), channel_id=1, source_target_pairs={{0,64},{32,96},{64,128},{96,160},{128,192},{160,224},{192,0},{224,... | collective-permute-start | bytes 196616 | tf_op jit(solution)/shard_map/ppermute | solution.py:243
  6.7 3.8 %collective-permute-start.2 = (bf16[2,32,512]{2,1,0:T(8,128)(2,1)S(1)}, bf16[2,32,512]{2,1,0:T(8,128)(2,1)S(1)}, u32[]{:S(2)}, u32[]{:S(2)}) collective-permute-start(bf16[2,32,512]{2,1,0:T(8,128)(2,1)S(1)} %get-tuple-element.30), channel_id=1, source_target_pairs={{0,96},{32,128},{64,160},{96,192},{128,224},{160,0},{192,32},{224,... | collective-permute-start | bytes 196616 | tf_op jit(solution)/shard_map/ppermute | solution.py:243
  10.4 0.5 collective-permute-start.3
  10.9 4.5 %collective-permute-start.4 = (bf16[2,32,512]{2,1,0:T(8,128)(2,1)S(1)}, bf16[2,32,512]{2,1,0:T(8,128)(2,1)S(1)}, u32[]{:S(2)}, u32[]{:S(2)}) collective-permute-start(bf16[2,32,512]{2,1,0:T(8,128)(2,1)S(1)} %get-tuple-element.32), channel_id=1, source_target_pairs={{0,160},{32,192},{64,224},{96,0},{128,32},{160,64},{192,96},{224,1... | collective-permute-start | bytes 196616 | tf_op jit(solution)/shard_map/ppermute | solution.py:243
  15.4 0.0 collective-permute-done.tie_ref.rest_1_
  15.4 2.4 %collective-permute-start.5 = (bf16[2,32,512]{2,1,0:T(8,128)(2,1)S(1)}, bf16[2,32,512]{2,1,0:T(8,128)(2,1)S(1)}, u32[]{:S(2)}, u32[]{:S(2)}) collective-permute-start(bf16[2,32,512]{2,1,0:T(8,128)(2,1)S(1)} %get-tuple-element.33), channel_id=1, source_target_pairs={{0,192},{32,224},{64,0},{96,32},{128,64},{160,96},{192,128},{224,1... | collective-permute-start | bytes 196616 | tf_op jit(solution)/shard_map/ppermute | solution.py:243
  17.7 0.0 collective-permute-done.1.rest_2_
  17.7 0.7 %collective-permute-start.6 = (bf16[2,32,512]{2,1,0:T(8,128)(2,1)S(1)}, bf16[2,32,512]{2,1,0:T(8,128)(2,1)S(1)}, u32[]{:S(2)}, u32[]{:S(2)}) collective-permute-start(bf16[2,32,512]{2,1,0:T(8,128)(2,1)S(1)} %get-tuple-element.34), channel_id=1, source_target_pairs={{0,224},{32,0},{64,32},{96,64},{128,96},{160,128},{192,160},{224,1... | collective-permute-start | bytes 196616 | tf_op jit(solution)/shard_map/ppermute | solution.py:243
  19.1 0.0 copy-start.1
  19.1 0.0 copy-start.2
  19.2 0.0 copy-start.3
  19.2 0.6 copy-done.1
  19.8 0.0 copy-done.2
  19.8 0.0 copy-done.3
  19.8 2.2 %stage.1 = (bf16[256,512]{1,0:T(8,128)(2,1)S(1)}, bf16[256,512]{1,0:T(8,128)(2,1)S(1)}, f32[256,512]{1,0:T(8,128)S(1)}, s32[1,512]{1,0:T(1,128)S(1)}, s32[1,512]{1,0:T(1,128)S(1)}, /*index=5*/f32[256,1]{1,0:T(8,128)S(1)}) custom-call(s32[1,8]{1,0:T(1,128)S(1)} %copy-done.1, s32[1,8]{1,0:T(1,128)S(1)} %copy-done.2, s32[1]{0:T(128)S(6)} %copy.16.suffix_ref, ...), custom_call_target="tpu_custom_call" | custom-call | flops 262144 | bytes 2097152 | tf_op jit(solution)/shard_map/stage/pallas_call | solution.py:245
  22.0 0.0 collective-permute-done.2.rest_3_
  22.0 0.0 collective-permute-done.3.rest_4_
  22.1 0.0 collective-permute-done.4.rest_5_
  22.1 3.4 %collective-permute-done.5.rest_6_ = bf16[2,32,512]{2,1,0:T(8,128)(2,1)S(1)} collective-permute-done((bf16[2,32,512]{2,1,0:T(8,128)(2,1)S(1)}, bf16[2,32,512]{2,1,0:T(8,128)(2,1)S(1)}, u32[]{:S(2)}, u32[]{:S(2)}) %collective-permute-start.5) | collective-permute-done | bytes 65568 | tf_op jit(solution)/shard_map/ppermute | solution.py:243
  25.4 0.0 collective-permute-done.6.rest_7_
  25.5 0.4 select.1
  25.9 0.0 copy-start.4
  25.9 0.0 copy-start.5
  25.9 20.0 %all_to_all.10 = bf16[32,8,1024]{2,1,0:T(8,128)(2,1)S(1)} all-to-all(bf16[32,8,1024]{2,1,0:T(8,128)(2,1)S(1)} %bitcast.10), channel_id=1, replica_groups=mesh['grp'=8,'seq'=32] {'seq'}, dimensions={0} | all-to-all | bytes 1048576 | tf_op jit(solution)/shard_map/all_to_all | solution.py:290
  45.9 0.0 copy-done.9
  46.0 3.2 %conv.1 = bf16[256,512]{1,0:T(8,128)(2,1)S(1)} custom-call(bf16[256,1024]{1,0:T(8,128)(2,1)S(1)} %bitcast.11, bf16[1024,256]{1,0:T(8,128)(2,1)S(1)} %copy-done.9, f32[256,512]{1,0:T(8,128)S(1)} %copy-done.8, f32[256,512]{1,0:T(8,128)S(1)} %copy-done.7, bf16[2,256,512]{2,1,0:T(8,128)(2,1)S(1)} %copy-done.6, bf16[2,256,512]{2,1,0:T(8,128)(2,1)S(1)} %copy-done.5, ...), custom_call_target="tpu_custom_call" | custom-call | flops 2147483648 | bytes 8388608 | tf_op jit(solution)/shard_map/conv/pallas_call | solution.py:294
  49.2 0.0 copy-start
  49.2 12.5 %all_to_all.11 = bf16[32,8,512]{2,1,0:T(8,128)(2,1)S(1)} all-to-all(bf16[32,8,512]{2,1,0:T(8,128)(2,1)S(1)} %bitcast.13), channel_id=1, replica_groups=mesh['grp'=8,'seq'=32] {'seq'}, dimensions={0} | all-to-all | bytes 524288 | tf_op jit(solution)/shard_map/all_to_all | solution.py:304
  61.7 0.0 copy-done
  61.7 0.9 %gate.1 = bf16[32,4096]{1,0:T(8,128)(2,1)} custom-call(bf16[256,512]{1,0:T(8,128)(2,1)S(1)} %bitcast.9, f32[256,512]{1,0:T(8,128)S(1)} %get-tuple-element.36.direct_ref, bf16[32,4096]{1,0:T(8,128)(2,1)S(1)} %bitcast.12), custom_call_target="tpu_custom_call" | custom-call | flops 262144 | bytes 2097152 | tf_op jit(solution)/shard_map/gate/pallas_call | solution.py:308
  (9 shorter events, 0.0 us)
Async XLA Ops:
  1.1 14.2 %collective-permute-start = (bf16[2,32,512]{2,1,0:T(8,128)(2,1)S(1)}, bf16[2,32,512]{2,1,0:T(8,128)(2,1)S(1)}, u32[]{:S(2)}, u32[]{:S(2)}) collective-permute-start(bf16[2,32,512]{2,1,0:T(8,128)(2,1)S(1)} %get-tuple-element.21), channel_id=1, source_target_pairs={{0,32},{32,64},{64,96},{96,128},{128,160},{160,192},{192,224},{224... | collective-permute-start | bytes 196616 | tf_op jit(solution)/shard_map/ppermute | solution.py:243
  3.7 14.1 %collective-permute-start.1 = (bf16[2,32,512]{2,1,0:T(8,128)(2,1)S(1)}, bf16[2,32,512]{2,1,0:T(8,128)(2,1)S(1)}, u32[]{:S(2)}, u32[]{:S(2)}) collective-permute-start(bf16[2,32,512]{2,1,0:T(8,128)(2,1)S(1)} %get-tuple-element.29), channel_id=1, source_target_pairs={{0,64},{32,96},{64,128},{96,160},{128,192},{160,224},{192,0},{224,... | collective-permute-start | bytes 196616 | tf_op jit(solution)/shard_map/ppermute | solution.py:243
  6.7 15.4 %collective-permute-start.2 = (bf16[2,32,512]{2,1,0:T(8,128)(2,1)S(1)}, bf16[2,32,512]{2,1,0:T(8,128)(2,1)S(1)}, u32[]{:S(2)}, u32[]{:S(2)}) collective-permute-start(bf16[2,32,512]{2,1,0:T(8,128)(2,1)S(1)} %get-tuple-element.30), channel_id=1, source_target_pairs={{0,96},{32,128},{64,160},{96,192},{128,224},{160,0},{192,32},{224,... | collective-permute-start | bytes 196616 | tf_op jit(solution)/shard_map/ppermute | solution.py:243
  10.4 11.6 %collective-permute-start.3 = (bf16[2,32,512]{2,1,0:T(8,128)(2,1)S(1)}, bf16[2,32,512]{2,1,0:T(8,128)(2,1)S(1)}, u32[]{:S(2)}, u32[]{:S(2)}) collective-permute-start(bf16[2,32,512]{2,1,0:T(8,128)(2,1)S(1)} %get-tuple-element.31), channel_id=1, source_target_pairs={{0,128},{32,160},{64,192},{96,224},{128,0},{160,32},{192,64},{224,... | collective-permute-start | bytes 196616 | tf_op jit(solution)/shard_map/ppermute | solution.py:243
  10.9 11.2 %collective-permute-start.4 = (bf16[2,32,512]{2,1,0:T(8,128)(2,1)S(1)}, bf16[2,32,512]{2,1,0:T(8,128)(2,1)S(1)}, u32[]{:S(2)}, u32[]{:S(2)}) collective-permute-start(bf16[2,32,512]{2,1,0:T(8,128)(2,1)S(1)} %get-tuple-element.32), channel_id=1, source_target_pairs={{0,160},{32,192},{64,224},{96,0},{128,32},{160,64},{192,96},{224,1... | collective-permute-start | bytes 196616 | tf_op jit(solution)/shard_map/ppermute | solution.py:243
  15.4 10.1 %collective-permute-start.5 = (bf16[2,32,512]{2,1,0:T(8,128)(2,1)S(1)}, bf16[2,32,512]{2,1,0:T(8,128)(2,1)S(1)}, u32[]{:S(2)}, u32[]{:S(2)}) collective-permute-start(bf16[2,32,512]{2,1,0:T(8,128)(2,1)S(1)} %get-tuple-element.33), channel_id=1, source_target_pairs={{0,192},{32,224},{64,0},{96,32},{128,64},{160,96},{192,128},{224,1... | collective-permute-start | bytes 196616 | tf_op jit(solution)/shard_map/ppermute | solution.py:243
  17.7 7.7 %collective-permute-start.6 = (bf16[2,32,512]{2,1,0:T(8,128)(2,1)S(1)}, bf16[2,32,512]{2,1,0:T(8,128)(2,1)S(1)}, u32[]{:S(2)}, u32[]{:S(2)}) collective-permute-start(bf16[2,32,512]{2,1,0:T(8,128)(2,1)S(1)} %get-tuple-element.34), channel_id=1, source_target_pairs={{0,224},{32,0},{64,32},{96,64},{128,96},{160,128},{192,160},{224,1... | collective-permute-start | bytes 196616 | tf_op jit(solution)/shard_map/ppermute | solution.py:243
  19.1 0.7 %copy-start.1 = (s32[1,8]{1,0:T(1,128)S(1)}, s32[1,8]{1,0:T(1,128)}, u32[]{:S(2)}) copy-start(s32[1,8]{1,0:T(1,128)} %owner_ref.1) | copy-start | bytes 100
  19.1 0.7 %copy-start.2 = (s32[1,8]{1,0:T(1,128)S(1)}, s32[1,8]{1,0:T(1,128)}, u32[]{:S(2)}) copy-start(s32[1,8]{1,0:T(1,128)} %slot_ref.1) | copy-start | bytes 100
  19.2 0.7 %copy-start.3 = (f32[32]{0:T(128)S(1)}, f32[32]{0:T(128)}, u32[]{:S(2)}) copy-start(f32[32]{0:T(128)} %gain_ref.1) | copy-start | bytes 388
  19.8 26.1 %copy-start.9 = (bf16[1024,256]{1,0:T(8,128)(2,1)S(1)}, bf16[1024,256]{1,0:T(8,128)(2,1)}, u32[]{:S(2)}) copy-start(bf16[1024,256]{1,0:T(8,128)(2,1)} %constant.12.clone.first_ref) | copy-start | bytes 1572868
  25.4 20.5 %copy-start.6 = (bf16[2,256,512]{2,1,0:T(8,128)(2,1)S(1)}, bf16[2,256,512]{2,1,0:T(8,128)(2,1)}, u32[]{:S(2)}) copy-start(bf16[2,256,512]{2,1,0:T(8,128)(2,1)} %constant.15.clone.high_ref) | copy-start | bytes 1572868
  25.4 20.5 %copy-start.7 = (f32[256,512]{1,0:T(8,128)S(1)}, f32[256,512]{1,0:T(8,128)}, u32[]{:S(2)}) copy-start(f32[256,512]{1,0:T(8,128)} %constant.14.clone.sin_ref) | copy-start | bytes 1572868
  25.4 20.5 %copy-start.8 = (f32[256,512]{1,0:T(8,128)S(1)}, f32[256,512]{1,0:T(8,128)}, u32[]{:S(2)}) copy-start(f32[256,512]{1,0:T(8,128)} %constant.13.clone.cos_ref) | copy-start | bytes 1572868
  25.9 20.0 %copy-start.4 = (bf16[512,512]{1,0:T(8,128)(2,1)S(1)}, bf16[512,512]{1,0:T(8,128)(2,1)}, u32[]{:S(2)}) copy-start(bf16[512,512]{1,0:T(8,128)(2,1)} %constant.17.clone.last_ref) | copy-start | bytes 1572868
  25.9 20.0 %copy-start.5 = (bf16[2,256,512]{2,1,0:T(8,128)(2,1)S(1)}, bf16[2,256,512]{2,1,0:T(8,128)(2,1)}, u32[]{:S(2)}) copy-start(bf16[2,256,512]{2,1,0:T(8,128)(2,1)} %constant.16.clone.low_ref) | copy-start | bytes 1572868
  49.2 12.6 %copy-start = (bf16[1,32,4096]{2,1,0:T(8,128)(2,1)S(1)}, bf16[1,32,4096]{2,1,0:T(8,128)(2,1)}, u32[]{:S(2)}) copy-start(bf16[1,32,4096]{2,1,0:T(8,128)(2,1)} %param.15) | copy-start | bytes 786436

commit v3 on v2

v3 whole, which is shorter than its diff:
```python
import functools

import jax
import jax.numpy as jnp
import ml_dtypes
import numpy as np
from jax import lax
from jax.experimental import pallas as pl
from jax.experimental.pallas import tpu as pltpu
from jax.sharding import PartitionSpec as P

N1 = 256
N2 = 512
HALF = N2 // 2
TOTAL = N1 * N2
BF16 = jnp.bfloat16
F32 = jnp.float32


def split_table(table):
    high = table.astype(ml_dtypes.bfloat16)
    low = (table - high.astype(np.float64)).astype(ml_dtypes.bfloat16)
    return high, low


@functools.cache
def tables():
    k1 = np.arange(N1)[:, None] + 0.25
    n1 = np.arange(N1)[None, :]
    rows = np.exp(-2j * np.pi * k1 * n1 / N1)
    high, low = split_table(np.concatenate([rows.real, rows.imag], axis=0))
    first = np.concatenate([high, low], axis=0)
    twiddle = np.exp(-2j * np.pi * k1 * np.arange(128)[None, :] / TOTAL)
    m = np.arange(HALF)[:, None]
    l = np.arange(HALF)[None, :]
    second_high, second_low = [], []
    for p in range(2):
        f = np.exp(-2j * np.pi * m * (l + 0.5 * p) / HALF)
        high, low = split_table(np.concatenate([f.real, f.imag], axis=1))
        second_high.append(high)
        second_low.append(low)
    back = rows.conj().T / TOTAL
    high, low = split_table(np.concatenate([back.real, -back.imag], axis=1))
    last = np.concatenate([high, low], axis=0)
    return (
        first,
        twiddle.real.astype(np.float32),
        twiddle.imag.astype(np.float32),
        np.stack(second_high),
        np.stack(second_low),
        last,
    )


def dot(a, b):
    return jnp.dot(a, b, preferred_element_type=F32)


def dot_t(a, b):
    return lax.dot_general(a, b, (((1,), (1,)), ((), ())), preferred_element_type=F32)


def whole_table(half):
    return jnp.concatenate(
        [half, jnp.concatenate([-half[:, HALF:], half[:, :HALF]], axis=1)], axis=0
    )


def place_rows(key_row):
    rows = lax.broadcasted_iota(jnp.int32, (N1, key_row.shape[1]), 0)
    return (rows == key_row).astype(F32).astype(BF16)


def send_order():
    col = lax.broadcasted_iota(jnp.int32, (1, N1), 1)
    return (col & 31) * 8 + (col >> 5)


def block_order():
    col = lax.broadcasted_iota(jnp.int32, (1, N1), 1)
    return (col & 7) * 32 + (col >> 3)


def fetch(sources, targets, sems):
    copies = [
        pltpu.make_async_copy(source, target, sems.at[i])
        for i, (source, target) in enumerate(zip(sources, targets))
    ]
    for copy in copies:
        copy.start()
    for copy in copies:
        copy.wait()


def place():
    seq = lax.axis_index("seq")
    return seq >> 3, (seq >> 1) & 3, seq & 1


def reorder(key_row, rows):
    return dot(place_rows(key_row), rows).astype(BF16)


def taps_core_kernel(taps_ref, keep_ref, send_ref):
    _, _, core = place()
    rows = jnp.concatenate([taps_ref[:, a * N2 : (a + 1) * N2] for a in range(8)], axis=0)
    col = lax.broadcasted_iota(jnp.int32, (1, N1), 1)
    channel, block = col & 31, col >> 5
    other = (channel & 1) ^ core
    key = other * 128 + ((channel >> 1) & 3) * 32 + (channel >> 3) * 8 + block
    full = reorder(key, rows.astype(BF16))
    keep_ref[...] = full[:128]
    send_ref[...] = full[128:]


def taps_y_kernel(keep_ref, came_ref, *outs):
    _, y, core = place()
    col = lax.broadcasted_iota(jnp.int32, (1, N1), 1)
    step = (((col >> 5) & 3) - y) & 3
    key = step * 64 + ((col >> 3) & 3) * 16 + ((col >> 7) ^ core) * 8 + (col & 7)
    full = reorder(key, jnp.concatenate([keep_ref[...], came_ref[...]], axis=0))
    for d in range(4):
        outs[d][...] = full[d * 64 : (d + 1) * 64]


def taps_x_kernel(*refs):
    ins, outs = refs[:4], refs[-4:]
    x, y, _ = place()
    col = lax.broadcasted_iota(jnp.int32, (1, N1), 1)
    step = (((col >> 4) & 3) - x) & 3
    key = step * 64 + ((y - (col >> 6)) & 3) * 16 + (col & 15)
    full = reorder(key, jnp.concatenate([ref[...] for ref in ins], axis=0))
    for d in range(4):
        outs[d][...] = full[d * 64 : (d + 1) * 64]


def stage_kernel(
    owner_hbm,
    slot_hbm,
    suffix_ref,
    key_hbm,
    value_hbm,
    tie_ref,
    fresh_ref,
    row_key_ref,
    owner_ref,
    slot_ref,
    key_ref,
    value_ref,
    sems,
):
    del tie_ref
    fetch(
        [owner_hbm, slot_hbm, key_hbm, value_hbm],
        [owner_ref, slot_ref, key_ref, value_ref],
        sems,
    )
    owner, slot = owner_ref[...], slot_ref[...]
    count = 256 - lax.axis_index("seq") * 8 - suffix_ref[0]
    column = lax.broadcasted_iota(jnp.int32, (1, 512), 1)
    row_key = jnp.full((1, 512), -1, jnp.int32)
    page = owner * 2 + slot - lax.axis_index("grp") * 2
    fresh = []
    for a in range(8):
        hit = ((column >> 5) == page[:, a : a + 1]) & (count > a)
        row_key = jnp.where(hit, (column & 31) * 8 + a, row_key)
        cols = slice(a * N2, (a + 1) * N2)
        product = key_ref[:, cols].astype(F32) * value_ref[:, cols].astype(F32)
        fresh.append(jnp.where(count > a, 0.0, product))
    row_key_ref[...] = row_key
    fresh_ref[...] = reorder(send_order(), jnp.concatenate(fresh, axis=0).astype(BF16))


def select_kernel(row_key_ref, fresh_ref, pages_ref, send_ref):
    cached = dot(place_rows(row_key_ref[...]), pages_ref[...])
    send_ref[...] = (cached + fresh_ref[...].astype(F32)).astype(BF16)


def twiddles(cos_ref, sin_ref):
    c, s = cos_ref[...], sin_ref[...]
    half_c, half_s = c[:, 64:65], s[:, 64:65]
    step_c, step_s = half_c * half_c - half_s * half_s, 2.0 * half_c * half_s
    cosines, sines = [c], [s]
    for _ in range(3):
        c, s = c * step_c - s * step_s, c * step_s + s * step_c
        cosines.append(c)
        sines.append(s)
    return jnp.concatenate(cosines, axis=1), jnp.concatenate(sines, axis=1)


def forward(rows, first_ref, cosine, sine, high_ref, low_ref):
    part = dot(first_ref[...], rows)
    r = part[:N1] + part[2 * N1 : 3 * N1]
    i = part[N1 : 2 * N1] + part[3 * N1 :]
    br = r * cosine - i * sine
    bi = r * sine + i * cosine
    spectra = []
    for p, sign in enumerate((1.0, -1.0)):
        cr = br[:, :HALF] + sign * br[:, HALF:]
        ci = bi[:, :HALF] + sign * bi[:, HALF:]
        c = jnp.concatenate([cr, ci], axis=1).astype(BF16)
        spectra.append(dot(c, whole_table(high_ref[p])) + dot(c, whole_table(low_ref[p])))
    return spectra


def filter_kernel(*refs):
    taps, refs = refs[:4], refs[4:]
    gain_ref, first_hbm, cos_ref, sin_ref, high_ref, low_ref, *refs = refs
    out_ref, first_ref, mine_ref, rows_ref, sems = refs
    fetch([first_hbm], [first_ref], sems)
    x, _, _ = place()
    for d in range(4):
        start = pl.multiple_of(((x - d) & 3) * 64, 64)
        rows_ref[pl.ds(start, 64), :] = taps[d][...]
    lane = lax.broadcasted_iota(jnp.int32, (1, 32), 1)
    mine = jnp.where(lane == lax.axis_index("seq"), gain_ref[...], 0.0)
    mine_ref[...] = jnp.broadcast_to(jnp.sum(mine, axis=1, keepdims=True), (1, N2))
    cosine, sine = twiddles(cos_ref, sin_ref)
    spectra = forward(rows_ref[...], first_ref, cosine, sine, high_ref, low_ref)
    for p, spec in enumerate(spectra):
        out_ref[p] = spec


def conv_kernel(x_ref, filter_ref, gain_ref, *refs):
    first_ref, cos_ref, sin_ref, high_ref, low_ref, last_hbm, out_ref, last_ref, sem = refs
    copy = pltpu.make_async_copy(last_hbm, last_ref, sem)
    copy.start()
    turned = []
    cosine, sine = twiddles(cos_ref, sin_ref)
    spectra = forward(x_ref[...], first_ref, cosine, sine, high_ref, low_ref)
    for p, spec in enumerate(spectra):
        xr, xi = spec[:, :HALF], spec[:, HALF:]
        hr, hi = filter_ref[p, :, :HALF], filter_ref[p, :, HALF:]
        prod = jnp.concatenate([xr * hr - xi * hi, xr * hi + xi * hr], axis=1).astype(BF16)
        high, low = whole_table(high_ref[p]), whole_table(low_ref[p])
        turned.append(dot_t(prod, high) + dot_t(prod, low))
    plus = turned[0] + turned[1]
    minus = turned[0] - turned[1]
    dr = jnp.concatenate([plus[:, :HALF], minus[:, :HALF]], axis=1)
    di = jnp.concatenate([plus[:, HALF:], minus[:, HALF:]], axis=1)
    er = (dr * cosine + di * sine).astype(BF16)
    ei = (di * cosine - dr * sine).astype(BF16)
    copy.wait()
    part = dot(last_ref[...], jnp.concatenate([er, ei], axis=0))
    direct = gain_ref[...] * x_ref[...].astype(F32)
    out_ref[...] = (part[:N1] + part[N1:] + direct).astype(BF16)


def gate_kernel(total_ref, query_ref, out_ref):
    total = dot(place_rows(block_order()), total_ref[...])
    for a in range(8):
        cols = slice(a * N2, (a + 1) * N2)
        query = query_ref[:, cols].astype(F32)
        out_ref[:, cols] = (query * total[a * 32 : (a + 1) * 32, :]).astype(BF16)


def params():
    return pltpu.CompilerParams(vmem_limit_bytes=24 * 1024 * 1024)


def in_hbm(array):
    return pltpu.with_memory_space_constraint(array, pltpu.HBM)


def cost(flops, moved):
    return pl.CostEstimate(flops=flops, bytes_accessed=moved, transcendentals=0)


VMEM = pl.BlockSpec(memory_space=pltpu.VMEM)
ANY = pl.BlockSpec(memory_space=pl.ANY)
HBM = pl.BlockSpec(memory_space=pltpu.HBM)
SMEM = pl.BlockSpec(memory_space=pltpu.SMEM)


def hops(dx, dy, dcore):
    pairs = []
    for x in range(4):
        for y in range(4):
            for core in range(2):
                to = (((x + dx) % 4) * 4 + (y + dy) % 4) * 2 + (core + dcore) % 2
                pairs.append(((x * 4 + y) * 2 + core, to))
    return pairs


def shards(
    query_gate,
    key_stream,
    value_stream,
    filter_taps,
    skip_gain,
    page_pool,
    page_owner,
    page_slot,
    suffix_blocks,
):
    pages = lax.all_to_all(
        page_pool.reshape(8, 2, 32, N2), "grp", split_axis=0, concat_axis=0, tiled=True
    ).reshape(512, N2)

    rows_of = lambda rows: jax.ShapeDtypeStruct((rows, N2), BF16)
    call = functools.partial(
        pl.pallas_call, compiler_params=params(), cost_estimate=cost(0, 1 << 20)
    )
    keep, other = call(
        taps_core_kernel,
        out_shape=(rows_of(128),) * 2,
        in_specs=[VMEM],
        out_specs=(VMEM,) * 2,
        name="taps_core",
    )(filter_taps)
    came = lax.ppermute(other, "seq", hops(0, 0, 1))
    along_y = call(
        taps_y_kernel,
        out_shape=(rows_of(64),) * 4,
        in_specs=[VMEM] * 2,
        out_specs=(VMEM,) * 4,
        name="taps_y",
    )(keep, came)
    moved_y = [lax.ppermute(along_y[d], "seq", hops(0, d, 0)) for d in range(1, 4)]

    fresh, row_key = call(
        stage_kernel,
        out_shape=(rows_of(N1), jax.ShapeDtypeStruct((1, 512), jnp.int32)),
        in_specs=[HBM, HBM, SMEM, HBM, HBM, ANY],
        out_specs=(VMEM,) * 2,
        scratch_shapes=[
            pltpu.VMEM((1, 8), jnp.int32),
            pltpu.VMEM((1, 8), jnp.int32),
            pltpu.VMEM((32, 8 * N2), BF16),
            pltpu.VMEM((32, 8 * N2), BF16),
            pltpu.SemaphoreType.DMA((4,)),
        ],
        name="stage",
    )(
        in_hbm(page_owner),
        in_hbm(page_slot),
        suffix_blocks,
        in_hbm(key_stream[0]),
        in_hbm(value_stream[0]),
        along_y[0],
    )

    along_x = call(
        taps_x_kernel,
        out_shape=(rows_of(64),) * 4,
        in_specs=[VMEM] * 4 + [ANY],
        out_specs=(VMEM,) * 4,
        name="taps_x",
    )(along_y[0], *moved_y, row_key)
    moved_x = [lax.ppermute(along_x[d], "seq", hops(d, 0, 0)) for d in range(1, 4)]

    send = call(
        select_kernel,
        out_shape=rows_of(N1),
        in_specs=[VMEM] * 3,
        out_specs=VMEM,
        cost_estimate=cost(1 << 34, 1 << 28),
        name="select",
    )(row_key, fresh, pages)

    columns = lax.all_to_all(
        send.reshape(32, 8, N2), "seq", split_axis=0, concat_axis=0, tiled=True
    ).reshape(N1, N2)

    first, *middle, last = [jnp.asarray(t) for t in tables()]
    spectrum, first, gain = call(
        filter_kernel,
        out_shape=(
            jax.ShapeDtypeStruct((2, N1, N2), F32),
            jax.ShapeDtypeStruct(first.shape, BF16),
            jax.ShapeDtypeStruct((1, N2), F32),
        ),
        in_specs=[VMEM] * 5 + [HBM] + [VMEM] * 4,
        out_specs=(VMEM,) * 3,
        scratch_shapes=[pltpu.VMEM((N1, N2), BF16), pltpu.SemaphoreType.DMA((1,))],
        cost_estimate=cost(1 << 34, 1 << 28),
        name="filter",
    )(along_x[0], *moved_x, skip_gain.reshape(1, 32), in_hbm(first), *middle)
    convolved = call(
        conv_kernel,
        out_shape=rows_of(N1),
        in_specs=[VMEM] * 8 + [HBM],
        out_specs=VMEM,
        scratch_shapes=[pltpu.VMEM((2 * N1, N2), BF16), pltpu.SemaphoreType.DMA],
        cost_estimate=cost(0, 1 << 23),
        name="conv",
    )(columns, spectrum, gain, first, *middle, in_hbm(last))

    back = lax.all_to_all(
        convolved.reshape(32, 8, N2), "seq", split_axis=0, concat_axis=0, tiled=True
    ).reshape(N1, N2)

    gated = call(
        gate_kernel,
        out_shape=jax.ShapeDtypeStruct((32, 8 * N2), BF16),
        in_specs=[VMEM] * 2,
        out_specs=VMEM,
        name="gate",
    )(back, query_gate[0])
    return gated[None]


def solution(mesh):
    return jax.shard_map(
        shards,
        mesh=mesh,
        in_specs=(
            P("grp", None, "seq"),
            P("grp", None, "seq"),
            P("grp", None, "seq"),
            P(None, "seq"),
            P(),
            P("grp", "seq", None, None, None),
            P("grp", "seq"),
            P("grp", "seq"),
            P("grp"),
        ),
        out_specs=P("grp", None, "seq"),
        check_vma=False,
    )
```

time: 62.9 us -> 61 us (0.970)
  blocking collectives: 32.5 us -> 12.6 us
  starting transfers between devices: 17.3 us -> 27.9 us
  waiting for transfers between devices: 3.39 us -> 10.3 us
    all_to_all x1 -> x0, blocking collectives: 20 us -> none  [shards(): lax.all_to_all(send.reshape(32, 8, 2 * N2), 'seq', split_axis=0, concat_a...]
    all_to_all x0 -> x2, starting transfers between devices: none -> 16.9 us  [the longest x1 9.15 us: shards(): lax.all_to_all(page_pool.reshape(8, 2, 32, N2), 'grp', split_axis=0, conc...]
    all_to_all x0 -> x2, waiting for transfers between devices: none -> 8.98 us  [the longest x1 6.05 us: shards(): lax.all_to_all(send.reshape(32, 8, N2), 'seq', split_axis=0, concat_axis=...]
    ppermute x7, starting transfers between devices: 17.3 us -> 11 us  [the longest x3 5.07 us: shards(): lax.ppermute(along_y[d], 'seq', hops(0, d, 0))]
    ppermute x7, waiting for transfers between devices: 3.39 us -> 1.3 us  [the longest x1 0.99 us: shards(): came = lax.ppermute(other, 'seq', hops(0, 0, 1))]
    pallas_call x5 -> x8, Pallas kernels: 7.91 us -> 8.48 us  [the longest x1 2.27 us: shards(): call(conv_kernel, out_shape=rows_of(N1), in_specs=[VMEM] * 8 + [HBM], out...]
  transfers between devices with their start and end apart: 7 -> 9, of which waited for: 1 -> 5; matrix products, arithmetic and copies ran while one was open for 0% -> 0% of each run, Pallas kernels for 4% -> 9%
where the time goes in v3:
time: 61 us; the launch traced here: 60.6 us
  starting transfers between devices  27.9 us (46%)
  blocking collectives  12.6 us (21%)
  waiting for transfers between devices  10.3 us (17%)
  Pallas kernels  8.48 us (14%)
  between operations  0.8 us (1%)
  local copies, waits for them, and re-layouts  0.64 us (1%)
    all_to_all x1, blocking collectives, shards(): lax.all_to_all(convolved.reshape(32, 8, N2), 'seq', split_axis=0, concat_...  12.6 us
    all_to_all x1, starting transfers between devices, shards(): lax.all_to_all(page_pool.reshape(8, 2, 32, N2), 'grp', split_axis=0, conc...  9.15 us
    all_to_all x1, starting transfers between devices, shards(): lax.all_to_all(send.reshape(32, 8, N2), 'seq', split_axis=0, concat_axis=...  7.71 us
    all_to_all x1, waiting for transfers between devices, shards(): lax.all_to_all(send.reshape(32, 8, N2), 'seq', split_axis=0, concat_axis=...  6.05 us
    ppermute x3, starting transfers between devices, shards(): lax.ppermute(along_y[d], 'seq', hops(0, d, 0))  5.07 us
    ppermute x3, starting transfers between devices, shards(): lax.ppermute(along_x[d], 'seq', hops(d, 0, 0))  4.89 us
    all_to_all x1, waiting for transfers between devices, shards(): lax.all_to_all(page_pool.reshape(8, 2, 32, N2), 'grp', split_axis=0, conc...  2.93 us
    pallas_call x1, Pallas kernels, shards(): call(conv_kernel, out_shape=rows_of(N1), in_specs=[VMEM] * 8 + [HBM], out...  2.27 us
  transfers between devices with their start and end apart: 9, of which 5 were waited for; matrix products, arithmetic and copies ran while one was open for 0% of the time, Pallas kernels for 9%

profile of v3, /device:TPU:1, one launch (start us, length us, event | category | flops | bytes accessed | tf_op | source)
XLA Modules:
  0.0 60.6 jit_solution(6477764624757163974)
XLA Ops:
  0.0 9.1 %all-to-all-start = ((bf16[8,2,32,512]{3,2,1,0:T(8,128)(2,1)}), bf16[8,2,32,512]{3,2,1,0:T(8,128)(2,1)S(1)}, u32[]{:S(2)}, u32[]{:S(2)}) async-start(bf16[8,2,32,512]{3,2,1,0:T(8,128)(2,1)} %bitcast.17), calls=%async_computation | async-start | bytes 1048576 | tf_op jit(solution)/shard_map/all_to_all | solution.py:296
  9.1 0.0 copy-done.2
  9.2 0.2 taps_core.1
  9.4 1.0 %collective-permute-start = (bf16[128,512]{1,0:T(8,128)(2,1)S(1)}, bf16[128,512]{1,0:T(8,128)(2,1)S(1)}, u32[]{:S(2)}, u32[]{:S(2)}) collective-permute-start(bf16[128,512]{1,0:T(8,128)(2,1)S(1)} %get-tuple-element.21), channel_id=1, source_target_pairs={{0,1},{1,0},{2,3},{3,2},{4,5},{5,4},{6,7},{7,6},{8,9},{9,8},{10,11... | collective-permute-start | bytes 393224 | tf_op jit(solution)/shard_map/ppermute | solution.py:311
  10.4 1.0 %collective-permute-done.came_ref = bf16[128,512]{1,0:T(8,128)(2,1)S(1)} collective-permute-done((bf16[128,512]{1,0:T(8,128)(2,1)S(1)}, bf16[128,512]{1,0:T(8,128)(2,1)S(1)}, u32[]{:S(2)}, u32[]{:S(2)}) %collective-permute-start) | collective-permute-done | bytes 131104 | tf_op jit(solution)/shard_map/ppermute | solution.py:311
  11.4 0.2 taps_y.1
  11.6 1.4 %collective-permute-start.1 = (bf16[64,512]{1,0:T(8,128)(2,1)S(1)}, bf16[64,512]{1,0:T(8,128)(2,1)S(1)}, u32[]{:S(2)}, u32[]{:S(2)}) collective-permute-start(bf16[64,512]{1,0:T(8,128)(2,1)S(1)} %get-tuple-element.25), channel_id=1, source_target_pairs={{0,2},{1,3},{2,4},{3,5},{4,6},{5,7},{6,0},{7,1},{8,10},{9,11},{10,... | collective-permute-start | bytes 196616 | tf_op jit(solution)/shard_map/ppermute | solution.py:319
  13.0 2.6 %collective-permute-start.2 = (bf16[64,512]{1,0:T(8,128)(2,1)S(1)}, bf16[64,512]{1,0:T(8,128)(2,1)S(1)}, u32[]{:S(2)}, u32[]{:S(2)}) collective-permute-start(bf16[64,512]{1,0:T(8,128)(2,1)S(1)} %get-tuple-element.26), channel_id=1, source_target_pairs={{0,4},{1,5},{2,6},{3,7},{4,0},{5,1},{6,2},{7,3},{8,12},{9,13},{10,... | collective-permute-start | bytes 196616 | tf_op jit(solution)/shard_map/ppermute | solution.py:319
  15.7 1.1 %collective-permute-start.3 = (bf16[64,512]{1,0:T(8,128)(2,1)S(1)}, bf16[64,512]{1,0:T(8,128)(2,1)S(1)}, u32[]{:S(2)}, u32[]{:S(2)}) collective-permute-start(bf16[64,512]{1,0:T(8,128)(2,1)S(1)} %get-tuple-element.27), channel_id=1, source_target_pairs={{0,6},{1,7},{2,0},{3,1},{4,2},{5,3},{6,4},{7,5},{8,14},{9,15},{10,... | collective-permute-start | bytes 196616 | tf_op jit(solution)/shard_map/ppermute | solution.py:319
  17.4 1.4 %stage.1 = (bf16[256,512]{1,0:T(8,128)(2,1)S(1)}, s32[1,512]{1,0:T(1,128)S(1)}) custom-call(s32[1,8]{1,0:T(1,128)} %owner_hbm.1, s32[1,8]{1,0:T(1,128)} %slot_hbm.1, s32[1]{0:T(128)S(6)} %copy.16.suffix_ref, bf16[32,4096]{1,0:T(8,128)(2,1)} %bitcast.18, bf16[32,4096]{1,0:T(8,128)(2,1)} %bitcast.19, bf16[64,512]{1,0:T(8,128)(2,1)S(1)} %get-tuple-element.22.tie_ref.refs_0_), custom_call_target="tpu_custom_call" | custom-call | bytes 1048576 | tf_op jit(solution)/shard_map/stage/pallas_call | solution.py:321
  18.7 0.0 collective-permute-done.1.refs_1_
  18.8 0.2 collective-permute-done.2.refs_2_
  18.9 0.2 collective-permute-done.3.refs_3_
  19.1 0.2 taps_x.1
  19.3 1.3 %collective-permute-start.4 = (bf16[64,512]{1,0:T(8,128)(2,1)S(1)}, bf16[64,512]{1,0:T(8,128)(2,1)S(1)}, u32[]{:S(2)}, u32[]{:S(2)}) collective-permute-start(bf16[64,512]{1,0:T(8,128)(2,1)S(1)} %get-tuple-element.29), channel_id=1, source_target_pairs={{0,8},{1,9},{2,10},{3,11},{4,12},{5,13},{6,14},{7,15},{8,16},{9,17... | collective-permute-start | bytes 196616 | tf_op jit(solution)/shard_map/ppermute | solution.py:350
  20.6 2.5 %collective-permute-start.5 = (bf16[64,512]{1,0:T(8,128)(2,1)S(1)}, bf16[64,512]{1,0:T(8,128)(2,1)S(1)}, u32[]{:S(2)}, u32[]{:S(2)}) collective-permute-start(bf16[64,512]{1,0:T(8,128)(2,1)S(1)} %get-tuple-element.30), channel_id=1, source_target_pairs={{0,16},{1,17},{2,18},{3,19},{4,20},{5,21},{6,22},{7,23},{8,24},{9,... | collective-permute-start | bytes 196616 | tf_op jit(solution)/shard_map/ppermute | solution.py:350
  23.0 1.1 %collective-permute-start.6 = (bf16[64,512]{1,0:T(8,128)(2,1)S(1)}, bf16[64,512]{1,0:T(8,128)(2,1)S(1)}, u32[]{:S(2)}, u32[]{:S(2)}) collective-permute-start(bf16[64,512]{1,0:T(8,128)(2,1)S(1)} %get-tuple-element.31), channel_id=1, source_target_pairs={{0,24},{1,25},{2,26},{3,27},{4,28},{5,29},{6,30},{7,31},{8,0},{9,1... | collective-permute-start | bytes 196616 | tf_op jit(solution)/shard_map/ppermute | solution.py:350
  24.2 2.9 %all-to-all-done = bf16[8,2,32,512]{3,2,1,0:T(8,128)(2,1)S(1)} async-done(((bf16[8,2,32,512]{3,2,1,0:T(8,128)(2,1)}), bf16[8,2,32,512]{3,2,1,0:T(8,128)(2,1)S(1)}, u32[]{:S(2)}, u32[]{:S(2)}) %all-to-all-start) | async-done | bytes 524320 | tf_op jit(solution)/shard_map/all_to_all | solution.py:296
  27.1 1.0 %select.1 = bf16[256,512]{1,0:T(8,128)(2,1)} custom-call(s32[1,512]{1,0:T(1,128)S(1)} %get-tuple-element.23.row_key_ref.refs_4_, bf16[256,512]{1,0:T(8,128)(2,1)S(1)} %get-tuple-element.24.fresh_ref, bf16[512,512]{1,0:T(8,128)(2,1)S(1)} %bitcast.14), custom_call_target="tpu_custom_call" | custom-call | flops 17179869184 | bytes 268435456 | tf_op jit(solution)/shard_map/select/pallas_call | solution.py:352
  28.1 7.7 %all-to-all-start.1 = ((bf16[32,8,512]{2,1,0:T(8,128)(2,1)}), bf16[32,8,512]{2,1,0:T(8,128)(2,1)S(1)}, u32[]{:S(2)}, u32[]{:S(2)}) async-start(bf16[32,8,512]{2,1,0:T(8,128)(2,1)} %bitcast.4), calls=%async_computation.1 | async-start | bytes 524288 | tf_op jit(solution)/shard_map/all_to_all | solution.py:361
  35.8 0.0 collective-permute-done.4.refs_1_
  35.8 0.0 collective-permute-done.5.refs_2_
  35.9 0.0 collective-permute-done.6.refs_3_
  35.9 0.0 copy-start.6
  35.9 0.6 copy-done.6
  36.5 2.2 %filter.1 = (f32[2,256,512]{2,1,0:T(8,128)S(1)}, bf16[1024,256]{1,0:T(8,128)(2,1)S(1)}, f32[1,512]{1,0:T(1,128)S(1)}) custom-call(bf16[64,512]{1,0:T(8,128)(2,1)S(1)} %get-tuple-element.28.refs_0_, bf16[64,512]{1,0:T(8,128)(2,1)S(1)} %collective-permute-done.4.refs_1_, bf16[64,512]{1,0:T(8,128)(2,1)S(1)} %collective-permute-done.5.refs_2_, ...), custom_call_target="tpu_custom_call" | custom-call | flops 17179869184 | bytes 268435456 | tf_op jit(solution)/shard_map/filter/pallas_call | solution.py:366
  38.8 6.0 %all-to-all-done.1 = bf16[32,8,512]{2,1,0:T(8,128)(2,1)S(1)} async-done(((bf16[32,8,512]{2,1,0:T(8,128)(2,1)}), bf16[32,8,512]{2,1,0:T(8,128)(2,1)S(1)}, u32[]{:S(2)}, u32[]{:S(2)}) %all-to-all-start.1) | async-done | bytes 262176 | tf_op jit(solution)/shard_map/all_to_all | solution.py:361
  44.8 2.3 %conv.1 = bf16[256,512]{1,0:T(8,128)(2,1)S(1)} custom-call(bf16[256,512]{1,0:T(8,128)(2,1)S(1)} %bitcast.11, f32[2,256,512]{2,1,0:T(8,128)S(1)} %get-tuple-element.32.filter_ref, f32[1,512]{1,0:T(1,128)S(1)} %get-tuple-element.33.gain_ref, bf16[1024,256]{1,0:T(8,128)(2,1)S(1)} %get-tuple-element.34.refs_0_, f32[256,128]{1,0:T(8,128)S(1)} %copy-done.5, ...), custom_call_target="tpu_custom_call" | custom-call | bytes 8388608 | tf_op jit(solution)/shard_map/conv/pallas_call | solution.py:379
  47.1 0.0 copy-start.3
  47.1 12.6 %all_to_all.15 = bf16[32,8,512]{2,1,0:T(8,128)(2,1)S(1)} all-to-all(bf16[32,8,512]{2,1,0:T(8,128)(2,1)S(1)} %bitcast.12), channel_id=1, replica_groups=mesh['grp'=8,'seq'=32] {'seq'}, dimensions={0} | all-to-all | bytes 524288 | tf_op jit(solution)/shard_map/all_to_all | solution.py:389
  59.7 0.0 copy-done.3
  59.7 0.9 %gate.1 = bf16[32,4096]{1,0:T(8,128)(2,1)} custom-call(bf16[256,512]{1,0:T(8,128)(2,1)S(1)} %bitcast.13, bf16[32,4096]{1,0:T(8,128)(2,1)S(1)} %bitcast.15), custom_call_target="tpu_custom_call" | custom-call | bytes 1048576 | tf_op jit(solution)/shard_map/gate/pallas_call | solution.py:393
  (9 shorter events, 0.0 us)
Async XLA Ops:
  0.0 9.2 %copy-start.2 = (f32[32,4096]{1,0:T(8,128)S(1)}, f32[32,4096]{1,0:T(8,128)}, u32[]{:S(2)}) copy-start(f32[32,4096]{1,0:T(8,128)} %taps_ref.1) | copy-start | bytes 1572868
  0.0 27.1 %all-to-all-start = ((bf16[8,2,32,512]{3,2,1,0:T(8,128)(2,1)}), bf16[8,2,32,512]{3,2,1,0:T(8,128)(2,1)S(1)}, u32[]{:S(2)}, u32[]{:S(2)}) async-start(bf16[8,2,32,512]{3,2,1,0:T(8,128)(2,1)} %bitcast.17), calls=%async_computation | async-start | bytes 1048576 | tf_op jit(solution)/shard_map/all_to_all | solution.py:296
  9.4 2.0 %collective-permute-start = (bf16[128,512]{1,0:T(8,128)(2,1)S(1)}, bf16[128,512]{1,0:T(8,128)(2,1)S(1)}, u32[]{:S(2)}, u32[]{:S(2)}) collective-permute-start(bf16[128,512]{1,0:T(8,128)(2,1)S(1)} %get-tuple-element.21), channel_id=1, source_target_pairs={{0,1},{1,0},{2,3},{3,2},{4,5},{5,4},{6,7},{7,6},{8,9},{9,8},{10,11... | collective-permute-start | bytes 393224 | tf_op jit(solution)/shard_map/ppermute | solution.py:311
  11.6 7.1 %collective-permute-start.1 = (bf16[64,512]{1,0:T(8,128)(2,1)S(1)}, bf16[64,512]{1,0:T(8,128)(2,1)S(1)}, u32[]{:S(2)}, u32[]{:S(2)}) collective-permute-start(bf16[64,512]{1,0:T(8,128)(2,1)S(1)} %get-tuple-element.25), channel_id=1, source_target_pairs={{0,2},{1,3},{2,4},{3,5},{4,6},{5,7},{6,0},{7,1},{8,10},{9,11},{10,... | collective-permute-start | bytes 196616 | tf_op jit(solution)/shard_map/ppermute | solution.py:319
  13.0 5.9 %collective-permute-start.2 = (bf16[64,512]{1,0:T(8,128)(2,1)S(1)}, bf16[64,512]{1,0:T(8,128)(2,1)S(1)}, u32[]{:S(2)}, u32[]{:S(2)}) collective-permute-start(bf16[64,512]{1,0:T(8,128)(2,1)S(1)} %get-tuple-element.26), channel_id=1, source_target_pairs={{0,4},{1,5},{2,6},{3,7},{4,0},{5,1},{6,2},{7,3},{8,12},{9,13},{10,... | collective-permute-start | bytes 196616 | tf_op jit(solution)/shard_map/ppermute | solution.py:319
  15.7 3.4 %collective-permute-start.3 = (bf16[64,512]{1,0:T(8,128)(2,1)S(1)}, bf16[64,512]{1,0:T(8,128)(2,1)S(1)}, u32[]{:S(2)}, u32[]{:S(2)}) collective-permute-start(bf16[64,512]{1,0:T(8,128)(2,1)S(1)} %get-tuple-element.27), channel_id=1, source_target_pairs={{0,6},{1,7},{2,0},{3,1},{4,2},{5,3},{6,4},{7,5},{8,14},{9,15},{10,... | collective-permute-start | bytes 196616 | tf_op jit(solution)/shard_map/ppermute | solution.py:319
  19.3 16.5 %collective-permute-start.4 = (bf16[64,512]{1,0:T(8,128)(2,1)S(1)}, bf16[64,512]{1,0:T(8,128)(2,1)S(1)}, u32[]{:S(2)}, u32[]{:S(2)}) collective-permute-start(bf16[64,512]{1,0:T(8,128)(2,1)S(1)} %get-tuple-element.29), channel_id=1, source_target_pairs={{0,8},{1,9},{2,10},{3,11},{4,12},{5,13},{6,14},{7,15},{8,16},{9,17... | collective-permute-start | bytes 196616 | tf_op jit(solution)/shard_map/ppermute | solution.py:350
  20.6 15.3 %collective-permute-start.5 = (bf16[64,512]{1,0:T(8,128)(2,1)S(1)}, bf16[64,512]{1,0:T(8,128)(2,1)S(1)}, u32[]{:S(2)}, u32[]{:S(2)}) collective-permute-start(bf16[64,512]{1,0:T(8,128)(2,1)S(1)} %get-tuple-element.30), channel_id=1, source_target_pairs={{0,16},{1,17},{2,18},{3,19},{4,20},{5,21},{6,22},{7,23},{8,24},{9,... | collective-permute-start | bytes 196616 | tf_op jit(solution)/shard_map/ppermute | solution.py:350
  23.0 12.8 %collective-permute-start.6 = (bf16[64,512]{1,0:T(8,128)(2,1)S(1)}, bf16[64,512]{1,0:T(8,128)(2,1)S(1)}, u32[]{:S(2)}, u32[]{:S(2)}) collective-permute-start(bf16[64,512]{1,0:T(8,128)(2,1)S(1)} %get-tuple-element.31), channel_id=1, source_target_pairs={{0,24},{1,25},{2,26},{3,27},{4,28},{5,29},{6,30},{7,31},{8,0},{9,1... | collective-permute-start | bytes 196616 | tf_op jit(solution)/shard_map/ppermute | solution.py:350
  27.1 8.8 %copy-start.1 = (bf16[2,256,512]{2,1,0:T(8,128)(2,1)S(1)}, bf16[2,256,512]{2,1,0:T(8,128)(2,1)}, u32[]{:S(2)}) copy-start(bf16[2,256,512]{2,1,0:T(8,128)(2,1)} %constant.15.clone.refs_8_.refs_3_) | copy-start | bytes 1572868
  27.1 8.8 %copy-start.4 = (f32[256,128]{1,0:T(8,128)S(1)}, f32[256,128]{1,0:T(8,128)}, u32[]{:S(2)}) copy-start(f32[256,128]{1,0:T(8,128)} %constant.14.clone.refs_7_.refs_2_) | copy-start | bytes 393220
  27.1 8.8 %copy-start.5 = (f32[256,128]{1,0:T(8,128)S(1)}, f32[256,128]{1,0:T(8,128)}, u32[]{:S(2)}) copy-start(f32[256,128]{1,0:T(8,128)} %constant.13.clone.refs_6_.refs_1_) | copy-start | bytes 393220
  28.1 7.8 %copy-start = (bf16[2,256,512]{2,1,0:T(8,128)(2,1)S(1)}, bf16[2,256,512]{2,1,0:T(8,128)(2,1)}, u32[]{:S(2)}) copy-start(bf16[2,256,512]{2,1,0:T(8,128)(2,1)} %constant.16.clone.refs_9_.refs_4_) | copy-start | bytes 1572868
  28.1 16.7 %all-to-all-start.1 = ((bf16[32,8,512]{2,1,0:T(8,128)(2,1)}), bf16[32,8,512]{2,1,0:T(8,128)(2,1)S(1)}, u32[]{:S(2)}, u32[]{:S(2)}) async-start(bf16[32,8,512]{2,1,0:T(8,128)(2,1)} %bitcast.4), calls=%async_computation.1 | async-start | bytes 524288 | tf_op jit(solution)/shard_map/all_to_all | solution.py:361
  35.9 0.7 %copy-start.6 = (f32[32]{0:T(128)S(1)}, f32[32]{0:T(128)}, u32[]{:S(2)}) copy-start(f32[32]{0:T(128)} %param.19) | copy-start | bytes 388
  47.1 12.6 %copy-start.3 = (bf16[1,32,4096]{2,1,0:T(8,128)(2,1)S(1)}, bf16[1,32,4096]{2,1,0:T(8,128)(2,1)}, u32[]{:S(2)}) copy-start(bf16[1,32,4096]{2,1,0:T(8,128)(2,1)} %param.15) | copy-start | bytes 786436

commit v4 on v3

--- a/solution.py
+++ b/solution.py
@@ -101,24 +101,13 @@
     return dot(place_rows(key_row), rows).astype(BF16)
 
 
-def taps_core_kernel(taps_ref, keep_ref, send_ref):
-    _, _, core = place()
+def taps_y_kernel(taps_ref, *outs):
+    _, y, _ = place()
     rows = jnp.concatenate([taps_ref[:, a * N2 : (a + 1) * N2] for a in range(8)], axis=0)
     col = lax.broadcasted_iota(jnp.int32, (1, N1), 1)
-    channel, block = col & 31, col >> 5
-    other = (channel & 1) ^ core
-    key = other * 128 + ((channel >> 1) & 3) * 32 + (channel >> 3) * 8 + block
+    step = (((col >> 1) & 3) - y) & 3
+    key = step * 64 + ((col >> 3) & 3) * 16 + (col & 1) * 8 + (col >> 5)
     full = reorder(key, rows.astype(BF16))
-    keep_ref[...] = full[:128]
-    send_ref[...] = full[128:]
-
-
-def taps_y_kernel(keep_ref, came_ref, *outs):
-    _, y, core = place()
-    col = lax.broadcasted_iota(jnp.int32, (1, N1), 1)
-    step = (((col >> 5) & 3) - y) & 3
-    key = step * 64 + ((col >> 3) & 3) * 16 + ((col >> 7) ^ core) * 8 + (col & 7)
-    full = reorder(key, jnp.concatenate([keep_ref[...], came_ref[...]], axis=0))
     for d in range(4):
         outs[d][...] = full[d * 64 : (d + 1) * 64]
 
@@ -128,10 +117,21 @@
     x, y, _ = place()
     col = lax.broadcasted_iota(jnp.int32, (1, N1), 1)
     step = (((col >> 4) & 3) - x) & 3
-    key = step * 64 + ((y - (col >> 6)) & 3) * 16 + (col & 15)
+    key = step * 64 + ((col >> 3) & 1) * 32 + ((y - (col >> 6)) & 3) * 8 + (col & 7)
     full = reorder(key, jnp.concatenate([ref[...] for ref in ins], axis=0))
     for d in range(4):
         outs[d][...] = full[d * 64 : (d + 1) * 64]
+
+
+def taps_core_kernel(*refs):
+    ins, (keep_ref, send_ref) = refs[:4], refs[4:]
+    x, _, core = place()
+    col = lax.broadcasted_iota(jnp.int32, (1, N1), 1)
+    other = ((col >> 5) & 1) ^ core
+    key = other * 128 + ((x - (col >> 6)) & 3) * 32 + (col & 31)
+    full = reorder(key, jnp.concatenate([ref[...] for ref in ins], axis=0))
+    keep_ref[...] = full[:128]
+    send_ref[...] = full[128:]
 
 
 def stage_kernel(
@@ -204,19 +204,20 @@
 
 
 def filter_kernel(*refs):
-    taps, refs = refs[:4], refs[4:]
-    gain_ref, first_hbm, cos_ref, sin_ref, high_ref, low_ref, *refs = refs
-    out_ref, first_ref, mine_ref, rows_ref, sems = refs
-    fetch([first_hbm], [first_ref], sems)
-    x, _, _ = place()
-    for d in range(4):
-        start = pl.multiple_of(((x - d) & 3) * 64, 64)
-        rows_ref[pl.ds(start, 64), :] = taps[d][...]
+    keep_ref, came_ref, gain_ref, first_hbm, cos_ref, sin_ref, high_ref, low_ref, *refs = refs
+    out_ref, first_ref, mine_ref, sems = refs
+    copy = pltpu.make_async_copy(first_hbm, first_ref, sems)
+    copy.start()
+    _, _, core = place()
+    col = lax.broadcasted_iota(jnp.int32, (1, N1), 1)
+    key = ((col >> 3) & 15) * 16 + ((col >> 7) ^ core) * 8 + (col & 7)
+    rows = reorder(key, jnp.concatenate([keep_ref[...], came_ref[...]], axis=0))
     lane = lax.broadcasted_iota(jnp.int32, (1, 32), 1)
     mine = jnp.where(lane == lax.axis_index("seq"), gain_ref[...], 0.0)
     mine_ref[...] = jnp.broadcast_to(jnp.sum(mine, axis=1, keepdims=True), (1, N2))
     cosine, sine = twiddles(cos_ref, sin_ref)
-    spectra = forward(rows_ref[...], first_ref, cosine, sine, high_ref, low_ref)
+    copy.wait()
+    spectra = forward(rows, first_ref, cosine, sine, high_ref, low_ref)
     for p, spec in enumerate(spectra):
         out_ref[p] = spec
 
@@ -301,21 +302,13 @@
     call = functools.partial(
         pl.pallas_call, compiler_params=params(), cost_estimate=cost(0, 1 << 20)
     )
-    keep, other = call(
-        taps_core_kernel,
-        out_shape=(rows_of(128),) * 2,
-        in_specs=[VMEM],
-        out_specs=(VMEM,) * 2,
-        name="taps_core",
-    )(filter_taps)
-    came = lax.ppermute(other, "seq", hops(0, 0, 1))
     along_y = call(
         taps_y_kernel,
         out_shape=(rows_of(64),) * 4,
-        in_specs=[VMEM] * 2,
+        in_specs=[VMEM],
         out_specs=(VMEM,) * 4,
         name="taps_y",
-    )(keep, came)
+    )(filter_taps)
     moved_y = [lax.ppermute(along_y[d], "seq", hops(0, d, 0)) for d in range(1, 4)]
 
     fresh, row_key = call(
@@ -349,6 +342,16 @@
     )(along_y[0], *moved_y, row_key)
     moved_x = [lax.ppermute(along_x[d], "seq", hops(d, 0, 0)) for d in range(1, 4)]
 
+    keep, other = call(
+        taps_core_kernel,
+        out_shape=(rows_of(128),) * 2,
+        in_specs=[VMEM] * 4,
+        out_specs=(VMEM,) * 2,
+        cost_estimate=cost(1 << 34, 1 << 28),
+        name="taps_core",
+    )(along_x[0], *moved_x)
+    came = lax.ppermute(other, "seq", hops(0, 0, 1))
+
     send = call(
         select_kernel,
         out_shape=rows_of(N1),
@@ -370,12 +373,12 @@
             jax.ShapeDtypeStruct(first.shape, BF16),
             jax.ShapeDtypeStruct((1, N2), F32),
         ),
-        in_specs=[VMEM] * 5 + [HBM] + [VMEM] * 4,
+        in_specs=[VMEM] * 3 + [HBM] + [VMEM] * 4,
         out_specs=(VMEM,) * 3,
-        scratch_shapes=[pltpu.VMEM((N1, N2), BF16), pltpu.SemaphoreType.DMA((1,))],
-        cost_estimate=cost(1 << 34, 1 << 28),
+        scratch_shapes=[pltpu.SemaphoreType.DMA],
+        cost_estimate=cost(1 << 28, 1 << 28),
         name="filter",
-    )(along_x[0], *moved_x, skip_gain.reshape(1, 32), in_hbm(first), *middle)
+    )(keep, came, skip_gain.reshape(1, 32), in_hbm(first), *middle)
     convolved = call(
         conv_kernel,
         out_shape=rows_of(N1),

time: 61 us -> 60.9 us (level)
  starting transfers between devices: 27.9 us -> 27 us
    all_to_all x1, waiting for transfers between devices: 2.93 us -> 4.91 us  [shards(): lax.all_to_all(page_pool.reshape(8, 2, 32, N2), 'grp', split_axis=0, conc...]
    all_to_all x1, waiting for transfers between devices: 6.05 us -> 4.29 us  [shards(): lax.all_to_all(send.reshape(32, 8, N2), 'seq', split_axis=0, concat_axis=...]
    ppermute x1, starting transfers between devices: 1.04 us -> 0.32 us  [shards(): came = lax.ppermute(other, 'seq', hops(0, 0, 1))]
  transfers between devices with their start and end apart: 9 -> 9, of which waited for: 5 -> 4; matrix products, arithmetic and copies ran while one was open for 0% -> 0% of each run, Pallas kernels for 9% -> 9%
where the time goes in v4:
time: 60.9 us; the launch traced here: 60.6 us
  starting transfers between devices  27 us (44%)
  blocking collectives  12.6 us (21%)
  waiting for transfers between devices  10.9 us (18%)
  Pallas kernels  8.57 us (14%)
  between operations  0.81 us (1%)
  local copies, waits for them, and re-layouts  0.67 us (1%)
    all_to_all x1, blocking collectives, shards(): lax.all_to_all(convolved.reshape(32, 8, N2), 'seq', split_axis=0, concat_...  12.6 us
    all_to_all x1, starting transfers between devices, shards(): lax.all_to_all(page_pool.reshape(8, 2, 32, N2), 'grp', split_axis=0, conc...  9.15 us
    all_to_all x1, starting transfers between devices, shards(): lax.all_to_all(send.reshape(32, 8, N2), 'seq', split_axis=0, concat_axis=...  7.58 us
    ppermute x3, starting transfers between devices, shards(): lax.ppermute(along_y[d], 'seq', hops(0, d, 0))  5.06 us
    all_to_all x1, waiting for transfers between devices, shards(): lax.all_to_all(page_pool.reshape(8, 2, 32, N2), 'grp', split_axis=0, conc...  4.91 us
    ppermute x3, starting transfers between devices, shards(): lax.ppermute(along_x[d], 'seq', hops(d, 0, 0))  4.9 us
    all_to_all x1, waiting for transfers between devices, shards(): lax.all_to_all(send.reshape(32, 8, N2), 'seq', split_axis=0, concat_axis=...  4.29 us
    pallas_call x1, Pallas kernels, shards(): call(conv_kernel, out_shape=rows_of(N1), in_specs=[VMEM] * 8 + [HBM], out...  2.31 us
  transfers between devices with their start and end apart: 9, of which 4 were waited for; matrix products, arithmetic and copies ran while one was open for 0% of the time, Pallas kernels for 9%

profile of v4, /device:TPU:1, one launch (start us, length us, event | category | flops | bytes accessed | tf_op | source)
XLA Modules:
  0.0 60.6 jit_solution(5844918347881421896)
XLA Ops:
  0.0 9.1 %all-to-all-start = ((bf16[8,2,32,512]{3,2,1,0:T(8,128)(2,1)}), bf16[8,2,32,512]{3,2,1,0:T(8,128)(2,1)S(1)}, u32[]{:S(2)}, u32[]{:S(2)}) async-start(bf16[8,2,32,512]{3,2,1,0:T(8,128)(2,1)} %bitcast.17), calls=%async_computation | async-start | bytes 1048576 | tf_op jit(solution)/shard_map/all_to_all | solution.py:297
  9.2 0.2 taps_y.1
  9.4 1.4 %collective-permute-start = (bf16[64,512]{1,0:T(8,128)(2,1)S(1)}, bf16[64,512]{1,0:T(8,128)(2,1)S(1)}, u32[]{:S(2)}, u32[]{:S(2)}) collective-permute-start(bf16[64,512]{1,0:T(8,128)(2,1)S(1)} %get-tuple-element.23), channel_id=1, source_target_pairs={{0,2},{1,3},{2,4},{3,5},{4,6},{5,7},{6,0},{7,1},{8,10},{9,11},{10,... | collective-permute-start | bytes 196616 | tf_op jit(solution)/shard_map/ppermute | solution.py:312
  10.8 2.6 %collective-permute-start.1 = (bf16[64,512]{1,0:T(8,128)(2,1)S(1)}, bf16[64,512]{1,0:T(8,128)(2,1)S(1)}, u32[]{:S(2)}, u32[]{:S(2)}) collective-permute-start(bf16[64,512]{1,0:T(8,128)(2,1)S(1)} %get-tuple-element.24), channel_id=1, source_target_pairs={{0,4},{1,5},{2,6},{3,7},{4,0},{5,1},{6,2},{7,3},{8,12},{9,13},{10,... | collective-permute-start | bytes 196616 | tf_op jit(solution)/shard_map/ppermute | solution.py:312
  13.4 1.1 %collective-permute-start.2 = (bf16[64,512]{1,0:T(8,128)(2,1)S(1)}, bf16[64,512]{1,0:T(8,128)(2,1)S(1)}, u32[]{:S(2)}, u32[]{:S(2)}) collective-permute-start(bf16[64,512]{1,0:T(8,128)(2,1)S(1)} %get-tuple-element.25), channel_id=1, source_target_pairs={{0,6},{1,7},{2,0},{3,1},{4,2},{5,3},{6,4},{7,5},{8,14},{9,15},{10,... | collective-permute-start | bytes 196616 | tf_op jit(solution)/shard_map/ppermute | solution.py:312
  15.1 1.4 %stage.1 = (bf16[256,512]{1,0:T(8,128)(2,1)S(1)}, s32[1,512]{1,0:T(1,128)S(1)}) custom-call(s32[1,8]{1,0:T(1,128)} %owner_hbm.1, s32[1,8]{1,0:T(1,128)} %slot_hbm.1, s32[1]{0:T(128)S(6)} %copy.16.suffix_ref, bf16[32,4096]{1,0:T(8,128)(2,1)} %bitcast.18, bf16[32,4096]{1,0:T(8,128)(2,1)} %bitcast.19, bf16[64,512]{1,0:T(8,128)(2,1)S(1)} %get-tuple-element.20.tie_ref.refs_0_), custom_call_target="tpu_custom_call" | custom-call | bytes 1048576 | tf_op jit(solution)/shard_map/stage/pallas_call | solution.py:314
  16.5 0.0 collective-permute-done.refs_1_
  16.5 0.0 collective-permute-done.1.refs_2_
  16.5 0.6 collective-permute-done.2.refs_3_
  17.1 0.2 taps_x.1
  17.3 1.3 %collective-permute-start.3 = (bf16[64,512]{1,0:T(8,128)(2,1)S(1)}, bf16[64,512]{1,0:T(8,128)(2,1)S(1)}, u32[]{:S(2)}, u32[]{:S(2)}) collective-permute-start(bf16[64,512]{1,0:T(8,128)(2,1)S(1)} %get-tuple-element.27), channel_id=1, source_target_pairs={{0,8},{1,9},{2,10},{3,11},{4,12},{5,13},{6,14},{7,15},{8,16},{9,17... | collective-permute-start | bytes 196616 | tf_op jit(solution)/shard_map/ppermute | solution.py:343
  18.6 2.5 %collective-permute-start.4 = (bf16[64,512]{1,0:T(8,128)(2,1)S(1)}, bf16[64,512]{1,0:T(8,128)(2,1)S(1)}, u32[]{:S(2)}, u32[]{:S(2)}) collective-permute-start(bf16[64,512]{1,0:T(8,128)(2,1)S(1)} %get-tuple-element.28), channel_id=1, source_target_pairs={{0,16},{1,17},{2,18},{3,19},{4,20},{5,21},{6,22},{7,23},{8,24},{9,... | collective-permute-start | bytes 196616 | tf_op jit(solution)/shard_map/ppermute | solution.py:343
  21.0 1.2 %collective-permute-start.5 = (bf16[64,512]{1,0:T(8,128)(2,1)S(1)}, bf16[64,512]{1,0:T(8,128)(2,1)S(1)}, u32[]{:S(2)}, u32[]{:S(2)}) collective-permute-start(bf16[64,512]{1,0:T(8,128)(2,1)S(1)} %get-tuple-element.29), channel_id=1, source_target_pairs={{0,24},{1,25},{2,26},{3,27},{4,28},{5,29},{6,30},{7,31},{8,0},{9,1... | collective-permute-start | bytes 196616 | tf_op jit(solution)/shard_map/ppermute | solution.py:343
  22.2 4.9 %all-to-all-done = bf16[8,2,32,512]{3,2,1,0:T(8,128)(2,1)S(1)} async-done(((bf16[8,2,32,512]{3,2,1,0:T(8,128)(2,1)}), bf16[8,2,32,512]{3,2,1,0:T(8,128)(2,1)S(1)}, u32[]{:S(2)}, u32[]{:S(2)}) %all-to-all-start) | async-done | bytes 524320 | tf_op jit(solution)/shard_map/all_to_all | solution.py:297
  27.1 1.0 %select.1 = bf16[256,512]{1,0:T(8,128)(2,1)} custom-call(s32[1,512]{1,0:T(1,128)S(1)} %get-tuple-element.21.row_key_ref.refs_4_, bf16[256,512]{1,0:T(8,128)(2,1)S(1)} %get-tuple-element.22.fresh_ref, bf16[512,512]{1,0:T(8,128)(2,1)S(1)} %bitcast.14), custom_call_target="tpu_custom_call" | custom-call | flops 17179869184 | bytes 268435456 | tf_op jit(solution)/shard_map/select/pallas_call | solution.py:355
  28.1 7.6 %all-to-all-start.1 = ((bf16[32,8,512]{2,1,0:T(8,128)(2,1)}), bf16[32,8,512]{2,1,0:T(8,128)(2,1)S(1)}, u32[]{:S(2)}, u32[]{:S(2)}) async-start(bf16[32,8,512]{2,1,0:T(8,128)(2,1)} %bitcast.4), calls=%async_computation.1 | async-start | bytes 524288 | tf_op jit(solution)/shard_map/all_to_all | solution.py:364
  35.7 0.0 collective-permute-done.3.refs_1_
  35.7 0.0 collective-permute-done.4.refs_2_
  35.7 0.0 copy-start
  35.7 0.0 copy-start.1
  35.8 0.0 copy-start.2
  35.8 0.0 copy-start.3
  35.8 0.2 taps_core.1
  36.0 0.3 collective-permute-start.6
  36.3 1.1 %collective-permute-done.6.refs_1_ = bf16[128,512]{1,0:T(8,128)(2,1)S(1)} collective-permute-done((bf16[128,512]{1,0:T(8,128)(2,1)S(1)}, bf16[128,512]{1,0:T(8,128)(2,1)S(1)}, u32[]{:S(2)}, u32[]{:S(2)}) %collective-permute-start.6) | collective-permute-done | bytes 131104 | tf_op jit(solution)/shard_map/ppermute | solution.py:353
  37.5 0.6 %copy-done.6 = f32[32]{0:T(128)S(1)} copy-done((f32[32]{0:T(128)S(1)}, f32[32]{0:T(128)}, u32[]{:S(2)}) %copy-start.6) | copy-done | bytes 152
  38.1 2.3 %filter.1 = (f32[2,256,512]{2,1,0:T(8,128)S(1)}, bf16[1024,256]{1,0:T(8,128)(2,1)S(1)}, f32[1,512]{1,0:T(1,128)S(1)}) custom-call(bf16[128,512]{1,0:T(8,128)(2,1)S(1)} %get-tuple-element.30.refs_0_, bf16[128,512]{1,0:T(8,128)(2,1)S(1)} %collective-permute-done.6.refs_1_, f32[1,32]{1,0:T(1,128)S(1)} %bitcast.16, bf16[1024,256]{1,0:T(8,128)(2,1)} %constant.12.clone.refs_3_, ...), custom_call_target="tpu_custom_call" | custom-call | flops 268435456 | bytes 268435456 | tf_op jit(solution)/shard_map/filter/pallas_call | solution.py:369
  40.4 4.3 %all-to-all-done.1 = bf16[32,8,512]{2,1,0:T(8,128)(2,1)S(1)} async-done(((bf16[32,8,512]{2,1,0:T(8,128)(2,1)}), bf16[32,8,512]{2,1,0:T(8,128)(2,1)S(1)}, u32[]{:S(2)}, u32[]{:S(2)}) %all-to-all-start.1) | async-done | bytes 262176 | tf_op jit(solution)/shard_map/all_to_all | solution.py:364
  44.7 2.3 %conv.1 = bf16[256,512]{1,0:T(8,128)(2,1)S(1)} custom-call(bf16[256,512]{1,0:T(8,128)(2,1)S(1)} %bitcast.11, f32[2,256,512]{2,1,0:T(8,128)S(1)} %get-tuple-element.32.filter_ref, f32[1,512]{1,0:T(1,128)S(1)} %get-tuple-element.33.gain_ref, bf16[1024,256]{1,0:T(8,128)(2,1)S(1)} %get-tuple-element.34.refs_0_, f32[256,128]{1,0:T(8,128)S(1)} %copy-done.3, ...), custom_call_target="tpu_custom_call" | custom-call | bytes 8388608 | tf_op jit(solution)/shard_map/conv/pallas_call | solution.py:382
  47.0 0.0 copy-start.5
  47.0 12.6 %all_to_all.15 = bf16[32,8,512]{2,1,0:T(8,128)(2,1)S(1)} all-to-all(bf16[32,8,512]{2,1,0:T(8,128)(2,1)S(1)} %bitcast.12), channel_id=1, replica_groups=mesh['grp'=8,'seq'=32] {'seq'}, dimensions={0} | all-to-all | bytes 524288 | tf_op jit(solution)/shard_map/all_to_all | solution.py:392
  59.6 0.9 %gate.1 = bf16[32,4096]{1,0:T(8,128)(2,1)} custom-call(bf16[256,512]{1,0:T(8,128)(2,1)S(1)} %bitcast.13, bf16[32,4096]{1,0:T(8,128)(2,1)S(1)} %bitcast.15), custom_call_target="tpu_custom_call" | custom-call | bytes 1048576 | tf_op jit(solution)/shard_map/gate/pallas_call | solution.py:396
  (9 shorter events, 0.0 us)
Async XLA Ops:
  0.0 9.2 %copy-start.4 = (f32[32,4096]{1,0:T(8,128)S(1)}, f32[32,4096]{1,0:T(8,128)}, u32[]{:S(2)}) copy-start(f32[32,4096]{1,0:T(8,128)} %taps_ref.1) | copy-start | bytes 1572868
  0.0 27.1 %all-to-all-start = ((bf16[8,2,32,512]{3,2,1,0:T(8,128)(2,1)}), bf16[8,2,32,512]{3,2,1,0:T(8,128)(2,1)S(1)}, u32[]{:S(2)}, u32[]{:S(2)}) async-start(bf16[8,2,32,512]{3,2,1,0:T(8,128)(2,1)} %bitcast.17), calls=%async_computation | async-start | bytes 1048576 | tf_op jit(solution)/shard_map/all_to_all | solution.py:297
  9.4 7.1 %collective-permute-start = (bf16[64,512]{1,0:T(8,128)(2,1)S(1)}, bf16[64,512]{1,0:T(8,128)(2,1)S(1)}, u32[]{:S(2)}, u32[]{:S(2)}) collective-permute-start(bf16[64,512]{1,0:T(8,128)(2,1)S(1)} %get-tuple-element.23), channel_id=1, source_target_pairs={{0,2},{1,3},{2,4},{3,5},{4,6},{5,7},{6,0},{7,1},{8,10},{9,11},{10,... | collective-permute-start | bytes 196616 | tf_op jit(solution)/shard_map/ppermute | solution.py:312
  10.8 5.7 %collective-permute-start.1 = (bf16[64,512]{1,0:T(8,128)(2,1)S(1)}, bf16[64,512]{1,0:T(8,128)(2,1)S(1)}, u32[]{:S(2)}, u32[]{:S(2)}) collective-permute-start(bf16[64,512]{1,0:T(8,128)(2,1)S(1)} %get-tuple-element.24), channel_id=1, source_target_pairs={{0,4},{1,5},{2,6},{3,7},{4,0},{5,1},{6,2},{7,3},{8,12},{9,13},{10,... | collective-permute-start | bytes 196616 | tf_op jit(solution)/shard_map/ppermute | solution.py:312
  13.4 3.7 %collective-permute-start.2 = (bf16[64,512]{1,0:T(8,128)(2,1)S(1)}, bf16[64,512]{1,0:T(8,128)(2,1)S(1)}, u32[]{:S(2)}, u32[]{:S(2)}) collective-permute-start(bf16[64,512]{1,0:T(8,128)(2,1)S(1)} %get-tuple-element.25), channel_id=1, source_target_pairs={{0,6},{1,7},{2,0},{3,1},{4,2},{5,3},{6,4},{7,5},{8,14},{9,15},{10,... | collective-permute-start | bytes 196616 | tf_op jit(solution)/shard_map/ppermute | solution.py:312
  17.3 18.4 %collective-permute-start.3 = (bf16[64,512]{1,0:T(8,128)(2,1)S(1)}, bf16[64,512]{1,0:T(8,128)(2,1)S(1)}, u32[]{:S(2)}, u32[]{:S(2)}) collective-permute-start(bf16[64,512]{1,0:T(8,128)(2,1)S(1)} %get-tuple-element.27), channel_id=1, source_target_pairs={{0,8},{1,9},{2,10},{3,11},{4,12},{5,13},{6,14},{7,15},{8,16},{9,17... | collective-permute-start | bytes 196616 | tf_op jit(solution)/shard_map/ppermute | solution.py:343
  18.6 17.1 %collective-permute-start.4 = (bf16[64,512]{1,0:T(8,128)(2,1)S(1)}, bf16[64,512]{1,0:T(8,128)(2,1)S(1)}, u32[]{:S(2)}, u32[]{:S(2)}) collective-permute-start(bf16[64,512]{1,0:T(8,128)(2,1)S(1)} %get-tuple-element.28), channel_id=1, source_target_pairs={{0,16},{1,17},{2,18},{3,19},{4,20},{5,21},{6,22},{7,23},{8,24},{9,... | collective-permute-start | bytes 196616 | tf_op jit(solution)/shard_map/ppermute | solution.py:343
  21.0 14.7 %collective-permute-start.5 = (bf16[64,512]{1,0:T(8,128)(2,1)S(1)}, bf16[64,512]{1,0:T(8,128)(2,1)S(1)}, u32[]{:S(2)}, u32[]{:S(2)}) collective-permute-start(bf16[64,512]{1,0:T(8,128)(2,1)S(1)} %get-tuple-element.29), channel_id=1, source_target_pairs={{0,24},{1,25},{2,26},{3,27},{4,28},{5,29},{6,30},{7,31},{8,0},{9,1... | collective-permute-start | bytes 196616 | tf_op jit(solution)/shard_map/ppermute | solution.py:343
  28.1 16.6 %all-to-all-start.1 = ((bf16[32,8,512]{2,1,0:T(8,128)(2,1)}), bf16[32,8,512]{2,1,0:T(8,128)(2,1)S(1)}, u32[]{:S(2)}, u32[]{:S(2)}) async-start(bf16[32,8,512]{2,1,0:T(8,128)(2,1)} %bitcast.4), calls=%async_computation.1 | async-start | bytes 524288 | tf_op jit(solution)/shard_map/all_to_all | solution.py:364
  35.7 1.7 %copy-start = (bf16[2,256,512]{2,1,0:T(8,128)(2,1)S(1)}, bf16[2,256,512]{2,1,0:T(8,128)(2,1)}, u32[]{:S(2)}) copy-start(bf16[2,256,512]{2,1,0:T(8,128)(2,1)} %constant.16.clone.refs_7_.refs_4_) | copy-start | bytes 1572868
  35.7 1.7 %copy-start.1 = (bf16[2,256,512]{2,1,0:T(8,128)(2,1)S(1)}, bf16[2,256,512]{2,1,0:T(8,128)(2,1)}, u32[]{:S(2)}) copy-start(bf16[2,256,512]{2,1,0:T(8,128)(2,1)} %constant.15.clone.refs_6_.refs_3_) | copy-start | bytes 1572868
  35.8 1.7 %copy-start.2 = (f32[256,128]{1,0:T(8,128)S(1)}, f32[256,128]{1,0:T(8,128)}, u32[]{:S(2)}) copy-start(f32[256,128]{1,0:T(8,128)} %constant.14.clone.refs_5_.refs_2_) | copy-start | bytes 393220
  35.8 1.7 %copy-start.3 = (f32[256,128]{1,0:T(8,128)S(1)}, f32[256,128]{1,0:T(8,128)}, u32[]{:S(2)}) copy-start(f32[256,128]{1,0:T(8,128)} %constant.13.clone.refs_4_.refs_1_) | copy-start | bytes 393220
  36.0 1.4 %collective-permute-start.6 = (bf16[128,512]{1,0:T(8,128)(2,1)S(1)}, bf16[128,512]{1,0:T(8,128)(2,1)S(1)}, u32[]{:S(2)}, u32[]{:S(2)}) collective-permute-start(bf16[128,512]{1,0:T(8,128)(2,1)S(1)} %get-tuple-element.31), channel_id=1, source_target_pairs={{0,1},{1,0},{2,3},{3,2},{4,5},{5,4},{6,7},{7,6},{8,9},{9,8},{10,11... | collective-permute-start | bytes 393224 | tf_op jit(solution)/shard_map/ppermute | solution.py:353
  37.5 0.7 %copy-start.6 = (f32[32]{0:T(128)S(1)}, f32[32]{0:T(128)}, u32[]{:S(2)}) copy-start(f32[32]{0:T(128)} %param.19) | copy-start | bytes 388
  47.0 12.6 %copy-start.5 = (bf16[1,32,4096]{2,1,0:T(8,128)(2,1)S(1)}, bf16[1,32,4096]{2,1,0:T(8,128)(2,1)}, u32[]{:S(2)}) copy-start(bf16[1,32,4096]{2,1,0:T(8,128)(2,1)} %param.15) | copy-start | bytes 786436

commit v5 on v4

--- a/solution.py
+++ b/solution.py
@@ -13,6 +13,7 @@
 N2 = 512
 HALF = N2 // 2
 TOTAL = N1 * N2
+RANKS = (4, 0, 5, 1, 6, 2, 7, 3)
 BF16 = jnp.bfloat16
 F32 = jnp.float32
 
@@ -101,6 +102,23 @@
     return dot(place_rows(key_row), rows).astype(BF16)
 
 
+def slabs_kernel(pool_ref, out_ref, held_ref, in_sems, out_sems):
+    reads = [
+        pltpu.make_async_copy(pool_ref.at[z], held_ref.at[r], in_sems.at[r])
+        for r, z in enumerate(RANKS)
+    ]
+    writes = [
+        pltpu.make_async_copy(held_ref.at[r], out_ref.at[r], out_sems.at[r]) for r in range(8)
+    ]
+    for read in reads:
+        read.start()
+    for read, write in zip(reads, writes):
+        read.wait()
+        write.start()
+    for write in writes:
+        write.wait()
+
+
 def taps_y_kernel(taps_ref, *outs):
     _, y, _ = place()
     rows = jnp.concatenate([taps_ref[:, a * N2 : (a + 1) * N2] for a in range(8)], axis=0)
@@ -159,7 +177,8 @@
     count = 256 - lax.axis_index("seq") * 8 - suffix_ref[0]
     column = lax.broadcasted_iota(jnp.int32, (1, 512), 1)
     row_key = jnp.full((1, 512), -1, jnp.int32)
-    page = owner * 2 + slot - lax.axis_index("grp") * 2
+    rank = sum(jnp.where(owner == z, r, 0) for r, z in enumerate(RANKS))
+    page = rank * 2 + slot - lax.axis_index("grp") * 2
     fresh = []
     for a in range(8):
         hit = ((column >> 5) == page[:, a : a + 1]) & (count > a)
@@ -294,14 +313,26 @@
     page_slot,
     suffix_blocks,
 ):
-    pages = lax.all_to_all(
-        page_pool.reshape(8, 2, 32, N2), "grp", split_axis=0, concat_axis=0, tiled=True
-    ).reshape(512, N2)
-
     rows_of = lambda rows: jax.ShapeDtypeStruct((rows, N2), BF16)
     call = functools.partial(
         pl.pallas_call, compiler_params=params(), cost_estimate=cost(0, 1 << 20)
     )
+    slabs = call(
+        slabs_kernel,
+        out_shape=pltpu.HBM((8, 2, 32, N2), BF16),
+        in_specs=[HBM],
+        out_specs=HBM,
+        scratch_shapes=[
+            pltpu.VMEM((8, 2, 32, N2), BF16),
+            pltpu.SemaphoreType.DMA((8,)),
+            pltpu.SemaphoreType.DMA((8,)),
+        ],
+        name="slabs",
+    )(in_hbm(page_pool.reshape(8, 2, 32, N2)))
+    pages = lax.all_to_all(
+        slabs, "grp", split_axis=0, concat_axis=0, axis_index_groups=[RANKS], tiled=True
+    ).reshape(512, N2)
+
     along_y = call(
         taps_y_kernel,
         out_shape=(rows_of(64),) * 4,

time: 60.9 us -> 59.4 us (0.975)
  waiting for transfers between devices: 10.9 us -> 5.98 us
  Pallas kernels: 8.57 us -> 10.4 us
  starting transfers between devices: 27 us -> 28.5 us
    all_to_all x1, waiting for transfers between devices: 4.91 us -> 0.01 us  [shards(): lax.all_to_all(slabs, 'grp', split_axis=0, concat_axis=0, axis_index_grou...]
    all_to_all x1, starting transfers between devices: 9.15 us -> 11.3 us  [shards(): lax.all_to_all(slabs, 'grp', split_axis=0, concat_axis=0, axis_index_grou...]
    pallas_call x0 -> x1, Pallas kernels: none -> 1.83 us  [shards(): call(slabs_kernel, out_shape=pltpu.HBM((8, 2, 32, N2), BF16), in_specs=[H...]
    all_to_all x1, starting transfers between devices: 7.58 us -> 6.96 us  [shards(): lax.all_to_all(send.reshape(32, 8, N2), 'seq', split_axis=0, concat_axis=...]
  transfers between devices with their start and end apart: 9 -> 9, of which waited for: 4 -> 3; matrix products, arithmetic and copies ran while one was open for 0% -> 0% of each run, Pallas kernels for 9% -> 9%
where the time goes in v5:
time: 59.4 us; the launch traced here: 59 us
  starting transfers between devices  28.5 us (48%)
  blocking collectives  12.6 us (21%)
  Pallas kernels  10.4 us (18%)
  waiting for transfers between devices  5.98 us (10%)
  between operations  0.82 us (1%)
  local copies, waits for them, and re-layouts  0.67 us (1%)
    all_to_all x1, blocking collectives, shards(): lax.all_to_all(convolved.reshape(32, 8, N2), 'seq', split_axis=0, concat_...  12.6 us
    all_to_all x1, starting transfers between devices, shards(): lax.all_to_all(slabs, 'grp', split_axis=0, concat_axis=0, axis_index_grou...  11.3 us
    all_to_all x1, starting transfers between devices, shards(): lax.all_to_all(send.reshape(32, 8, N2), 'seq', split_axis=0, concat_axis=...  6.96 us
    ppermute x3, starting transfers between devices, shards(): lax.ppermute(along_y[d], 'seq', hops(0, d, 0))  5.06 us
    ppermute x3, starting transfers between devices, shards(): lax.ppermute(along_x[d], 'seq', hops(d, 0, 0))  4.89 us
    all_to_all x1, waiting for transfers between devices, shards(): lax.all_to_all(send.reshape(32, 8, N2), 'seq', split_axis=0, concat_axis=...  4.29 us
    pallas_call x1, Pallas kernels, shards(): call(conv_kernel, out_shape=rows_of(N1), in_specs=[VMEM] * 8 + [HBM], out...  2.31 us
    pallas_call x1, Pallas kernels, shards(): call(filter_kernel, out_shape=(jax.ShapeDtypeStruct((2, N1, N2), F32), ja...  2.28 us
  transfers between devices with their start and end apart: 9, of which 3 were waited for; matrix products, arithmetic and copies ran while one was open for 0% of the time, Pallas kernels for 9%

profile of v5, /device:TPU:1, one launch (start us, length us, event | category | flops | bytes accessed | tf_op | source)
XLA Modules:
  0.0 59.0 jit_solution(2770385966841887075)
XLA Ops:
  0.0 1.8 %slabs.1 = bf16[8,2,32,512]{3,2,1,0:T(8,128)(2,1)} custom-call(bf16[8,2,32,512]{3,2,1,0:T(8,128)(2,1)} %bitcast.17), custom_call_target="tpu_custom_call" | custom-call | bytes 1048576 | tf_op jit(solution)/shard_map/slabs/pallas_call | solution.py:320
  1.8 0.0 copy-start.4
  1.9 11.3 %all-to-all-start = ((bf16[8,2,32,512]{3,2,1,0:T(8,128)(2,1)}), bf16[8,2,32,512]{3,2,1,0:T(8,128)(2,1)S(1)}, u32[]{:S(2)}, u32[]{:S(2)}) async-start(bf16[8,2,32,512]{3,2,1,0:T(8,128)(2,1)} %slabs.1), calls=%async_computation | async-start | bytes 1048576 | tf_op jit(solution)/shard_map/all_to_all | solution.py:332
  13.1 0.2 taps_y.1
  13.4 1.4 %collective-permute-start = (bf16[64,512]{1,0:T(8,128)(2,1)S(1)}, bf16[64,512]{1,0:T(8,128)(2,1)S(1)}, u32[]{:S(2)}, u32[]{:S(2)}) collective-permute-start(bf16[64,512]{1,0:T(8,128)(2,1)S(1)} %get-tuple-element.23), channel_id=1, source_target_pairs={{0,2},{1,3},{2,4},{3,5},{4,6},{5,7},{6,0},{7,1},{8,10},{9,11},{10,... | collective-permute-start | bytes 196616 | tf_op jit(solution)/shard_map/ppermute | solution.py:343
  14.7 2.6 %collective-permute-start.1 = (bf16[64,512]{1,0:T(8,128)(2,1)S(1)}, bf16[64,512]{1,0:T(8,128)(2,1)S(1)}, u32[]{:S(2)}, u32[]{:S(2)}) collective-permute-start(bf16[64,512]{1,0:T(8,128)(2,1)S(1)} %get-tuple-element.24), channel_id=1, source_target_pairs={{0,4},{1,5},{2,6},{3,7},{4,0},{5,1},{6,2},{7,3},{8,12},{9,13},{10,... | collective-permute-start | bytes 196616 | tf_op jit(solution)/shard_map/ppermute | solution.py:343
  17.4 1.1 %collective-permute-start.2 = (bf16[64,512]{1,0:T(8,128)(2,1)S(1)}, bf16[64,512]{1,0:T(8,128)(2,1)S(1)}, u32[]{:S(2)}, u32[]{:S(2)}) collective-permute-start(bf16[64,512]{1,0:T(8,128)(2,1)S(1)} %get-tuple-element.25), channel_id=1, source_target_pairs={{0,6},{1,7},{2,0},{3,1},{4,2},{5,3},{6,4},{7,5},{8,14},{9,15},{10,... | collective-permute-start | bytes 196616 | tf_op jit(solution)/shard_map/ppermute | solution.py:343
  19.1 1.4 %stage.1 = (bf16[256,512]{1,0:T(8,128)(2,1)S(1)}, s32[1,512]{1,0:T(1,128)S(1)}) custom-call(s32[1,8]{1,0:T(1,128)} %owner_hbm.1, s32[1,8]{1,0:T(1,128)} %slot_hbm.1, s32[1]{0:T(128)S(6)} %copy.16.suffix_ref, bf16[32,4096]{1,0:T(8,128)(2,1)} %bitcast.18, bf16[32,4096]{1,0:T(8,128)(2,1)} %bitcast.19, bf16[64,512]{1,0:T(8,128)(2,1)S(1)} %get-tuple-element.20.tie_ref.refs_0_), custom_call_target="tpu_custom_call" | custom-call | bytes 1048576 | tf_op jit(solution)/shard_map/stage/pallas_call | solution.py:345
  20.5 0.0 collective-permute-done.refs_1_
  20.5 0.6 collective-permute-done.2.refs_3_
  21.0 0.2 taps_x.1
  21.3 1.3 %collective-permute-start.3 = (bf16[64,512]{1,0:T(8,128)(2,1)S(1)}, bf16[64,512]{1,0:T(8,128)(2,1)S(1)}, u32[]{:S(2)}, u32[]{:S(2)}) collective-permute-start(bf16[64,512]{1,0:T(8,128)(2,1)S(1)} %get-tuple-element.27), channel_id=1, source_target_pairs={{0,8},{1,9},{2,10},{3,11},{4,12},{5,13},{6,14},{7,15},{8,16},{9,17... | collective-permute-start | bytes 196616 | tf_op jit(solution)/shard_map/ppermute | solution.py:374
  22.6 2.5 %collective-permute-start.4 = (bf16[64,512]{1,0:T(8,128)(2,1)S(1)}, bf16[64,512]{1,0:T(8,128)(2,1)S(1)}, u32[]{:S(2)}, u32[]{:S(2)}) collective-permute-start(bf16[64,512]{1,0:T(8,128)(2,1)S(1)} %get-tuple-element.28), channel_id=1, source_target_pairs={{0,16},{1,17},{2,18},{3,19},{4,20},{5,21},{6,22},{7,23},{8,24},{9,... | collective-permute-start | bytes 196616 | tf_op jit(solution)/shard_map/ppermute | solution.py:374
  25.0 1.1 %collective-permute-start.5 = (bf16[64,512]{1,0:T(8,128)(2,1)S(1)}, bf16[64,512]{1,0:T(8,128)(2,1)S(1)}, u32[]{:S(2)}, u32[]{:S(2)}) collective-permute-start(bf16[64,512]{1,0:T(8,128)(2,1)S(1)} %get-tuple-element.29), channel_id=1, source_target_pairs={{0,24},{1,25},{2,26},{3,27},{4,28},{5,29},{6,30},{7,31},{8,0},{9,1... | collective-permute-start | bytes 196616 | tf_op jit(solution)/shard_map/ppermute | solution.py:374
  26.2 0.0 all-to-all-done
  26.2 1.0 %select.1 = bf16[256,512]{1,0:T(8,128)(2,1)} custom-call(s32[1,512]{1,0:T(1,128)S(1)} %get-tuple-element.21.row_key_ref.refs_4_, bf16[256,512]{1,0:T(8,128)(2,1)S(1)} %get-tuple-element.22.fresh_ref, bf16[512,512]{1,0:T(8,128)(2,1)S(1)} %bitcast.14), custom_call_target="tpu_custom_call" | custom-call | flops 17179869184 | bytes 268435456 | tf_op jit(solution)/shard_map/select/pallas_call | solution.py:386
  27.2 7.0 %all-to-all-start.1 = ((bf16[32,8,512]{2,1,0:T(8,128)(2,1)}), bf16[32,8,512]{2,1,0:T(8,128)(2,1)S(1)}, u32[]{:S(2)}, u32[]{:S(2)}) async-start(bf16[32,8,512]{2,1,0:T(8,128)(2,1)} %bitcast.4), calls=%async_computation.1 | async-start | bytes 524288 | tf_op jit(solution)/shard_map/all_to_all | solution.py:395
  34.1 0.0 collective-permute-done.3.refs_1_
  34.2 0.0 copy-start
  34.2 0.0 copy-start.1
  34.2 0.0 copy-start.2
  34.2 0.0 copy-start.3
  34.2 0.2 taps_core.1
  34.5 0.3 collective-permute-start.6
  34.8 1.1 %collective-permute-done.6.refs_1_ = bf16[128,512]{1,0:T(8,128)(2,1)S(1)} collective-permute-done((bf16[128,512]{1,0:T(8,128)(2,1)S(1)}, bf16[128,512]{1,0:T(8,128)(2,1)S(1)}, u32[]{:S(2)}, u32[]{:S(2)}) %collective-permute-start.6) | collective-permute-done | bytes 131104 | tf_op jit(solution)/shard_map/ppermute | solution.py:384
  35.9 0.6 %copy-done.6 = f32[32]{0:T(128)S(1)} copy-done((f32[32]{0:T(128)S(1)}, f32[32]{0:T(128)}, u32[]{:S(2)}) %copy-start.6) | copy-done | bytes 152
  36.6 2.3 %filter.1 = (f32[2,256,512]{2,1,0:T(8,128)S(1)}, bf16[1024,256]{1,0:T(8,128)(2,1)S(1)}, f32[1,512]{1,0:T(1,128)S(1)}) custom-call(bf16[128,512]{1,0:T(8,128)(2,1)S(1)} %get-tuple-element.30.refs_0_, bf16[128,512]{1,0:T(8,128)(2,1)S(1)} %collective-permute-done.6.refs_1_, f32[1,32]{1,0:T(1,128)S(1)} %bitcast.16, bf16[1024,256]{1,0:T(8,128)(2,1)} %constant.12.clone.refs_3_, ...), custom_call_target="tpu_custom_call" | custom-call | flops 268435456 | bytes 268435456 | tf_op jit(solution)/shard_map/filter/pallas_call | solution.py:400
  38.8 4.3 %all-to-all-done.1 = bf16[32,8,512]{2,1,0:T(8,128)(2,1)S(1)} async-done(((bf16[32,8,512]{2,1,0:T(8,128)(2,1)}), bf16[32,8,512]{2,1,0:T(8,128)(2,1)S(1)}, u32[]{:S(2)}, u32[]{:S(2)}) %all-to-all-start.1) | async-done | bytes 262176 | tf_op jit(solution)/shard_map/all_to_all | solution.py:395
  43.1 2.3 %conv.1 = bf16[256,512]{1,0:T(8,128)(2,1)S(1)} custom-call(bf16[256,512]{1,0:T(8,128)(2,1)S(1)} %bitcast.11, f32[2,256,512]{2,1,0:T(8,128)S(1)} %get-tuple-element.32.filter_ref, f32[1,512]{1,0:T(1,128)S(1)} %get-tuple-element.33.gain_ref, bf16[1024,256]{1,0:T(8,128)(2,1)S(1)} %get-tuple-element.34.refs_0_, f32[256,128]{1,0:T(8,128)S(1)} %copy-done.3, ...), custom_call_target="tpu_custom_call" | custom-call | bytes 8388608 | tf_op jit(solution)/shard_map/conv/pallas_call | solution.py:413
  45.5 0.0 copy-start.5
  45.5 12.6 %all_to_all.15 = bf16[32,8,512]{2,1,0:T(8,128)(2,1)S(1)} all-to-all(bf16[32,8,512]{2,1,0:T(8,128)(2,1)S(1)} %bitcast.12), channel_id=1, replica_groups=mesh['grp'=8,'seq'=32] {'seq'}, dimensions={0} | all-to-all | bytes 524288 | tf_op jit(solution)/shard_map/all_to_all | solution.py:423
  58.1 0.9 %gate.1 = bf16[32,4096]{1,0:T(8,128)(2,1)} custom-call(bf16[256,512]{1,0:T(8,128)(2,1)S(1)} %bitcast.13, bf16[32,4096]{1,0:T(8,128)(2,1)S(1)} %bitcast.15), custom_call_target="tpu_custom_call" | custom-call | bytes 1048576 | tf_op jit(solution)/shard_map/gate/pallas_call | solution.py:427
  (10 shorter events, 0.0 us)
Async XLA Ops:
  1.8 11.3 %copy-start.4 = (f32[32,4096]{1,0:T(8,128)S(1)}, f32[32,4096]{1,0:T(8,128)}, u32[]{:S(2)}) copy-start(f32[32,4096]{1,0:T(8,128)} %taps_ref.1) | copy-start | bytes 1572868
  1.9 24.3 %all-to-all-start = ((bf16[8,2,32,512]{3,2,1,0:T(8,128)(2,1)}), bf16[8,2,32,512]{3,2,1,0:T(8,128)(2,1)S(1)}, u32[]{:S(2)}, u32[]{:S(2)}) async-start(bf16[8,2,32,512]{3,2,1,0:T(8,128)(2,1)} %slabs.1), calls=%async_computation | async-start | bytes 1048576 | tf_op jit(solution)/shard_map/all_to_all | solution.py:332
  13.4 7.1 %collective-permute-start = (bf16[64,512]{1,0:T(8,128)(2,1)S(1)}, bf16[64,512]{1,0:T(8,128)(2,1)S(1)}, u32[]{:S(2)}, u32[]{:S(2)}) collective-permute-start(bf16[64,512]{1,0:T(8,128)(2,1)S(1)} %get-tuple-element.23), channel_id=1, source_target_pairs={{0,2},{1,3},{2,4},{3,5},{4,6},{5,7},{6,0},{7,1},{8,10},{9,11},{10,... | collective-permute-start | bytes 196616 | tf_op jit(solution)/shard_map/ppermute | solution.py:343
  14.7 5.7 %collective-permute-start.1 = (bf16[64,512]{1,0:T(8,128)(2,1)S(1)}, bf16[64,512]{1,0:T(8,128)(2,1)S(1)}, u32[]{:S(2)}, u32[]{:S(2)}) collective-permute-start(bf16[64,512]{1,0:T(8,128)(2,1)S(1)} %get-tuple-element.24), channel_id=1, source_target_pairs={{0,4},{1,5},{2,6},{3,7},{4,0},{5,1},{6,2},{7,3},{8,12},{9,13},{10,... | collective-permute-start | bytes 196616 | tf_op jit(solution)/shard_map/ppermute | solution.py:343
  17.4 3.7 %collective-permute-start.2 = (bf16[64,512]{1,0:T(8,128)(2,1)S(1)}, bf16[64,512]{1,0:T(8,128)(2,1)S(1)}, u32[]{:S(2)}, u32[]{:S(2)}) collective-permute-start(bf16[64,512]{1,0:T(8,128)(2,1)S(1)} %get-tuple-element.25), channel_id=1, source_target_pairs={{0,6},{1,7},{2,0},{3,1},{4,2},{5,3},{6,4},{7,5},{8,14},{9,15},{10,... | collective-permute-start | bytes 196616 | tf_op jit(solution)/shard_map/ppermute | solution.py:343
  21.3 12.9 %collective-permute-start.3 = (bf16[64,512]{1,0:T(8,128)(2,1)S(1)}, bf16[64,512]{1,0:T(8,128)(2,1)S(1)}, u32[]{:S(2)}, u32[]{:S(2)}) collective-permute-start(bf16[64,512]{1,0:T(8,128)(2,1)S(1)} %get-tuple-element.27), channel_id=1, source_target_pairs={{0,8},{1,9},{2,10},{3,11},{4,12},{5,13},{6,14},{7,15},{8,16},{9,17... | collective-permute-start | bytes 196616 | tf_op jit(solution)/shard_map/ppermute | solution.py:374
  22.6 11.6 %collective-permute-start.4 = (bf16[64,512]{1,0:T(8,128)(2,1)S(1)}, bf16[64,512]{1,0:T(8,128)(2,1)S(1)}, u32[]{:S(2)}, u32[]{:S(2)}) collective-permute-start(bf16[64,512]{1,0:T(8,128)(2,1)S(1)} %get-tuple-element.28), channel_id=1, source_target_pairs={{0,16},{1,17},{2,18},{3,19},{4,20},{5,21},{6,22},{7,23},{8,24},{9,... | collective-permute-start | bytes 196616 | tf_op jit(solution)/shard_map/ppermute | solution.py:374
  25.0 9.2 %collective-permute-start.5 = (bf16[64,512]{1,0:T(8,128)(2,1)S(1)}, bf16[64,512]{1,0:T(8,128)(2,1)S(1)}, u32[]{:S(2)}, u32[]{:S(2)}) collective-permute-start(bf16[64,512]{1,0:T(8,128)(2,1)S(1)} %get-tuple-element.29), channel_id=1, source_target_pairs={{0,24},{1,25},{2,26},{3,27},{4,28},{5,29},{6,30},{7,31},{8,0},{9,1... | collective-permute-start | bytes 196616 | tf_op jit(solution)/shard_map/ppermute | solution.py:374
  27.2 16.0 %all-to-all-start.1 = ((bf16[32,8,512]{2,1,0:T(8,128)(2,1)}), bf16[32,8,512]{2,1,0:T(8,128)(2,1)S(1)}, u32[]{:S(2)}, u32[]{:S(2)}) async-start(bf16[32,8,512]{2,1,0:T(8,128)(2,1)} %bitcast.4), calls=%async_computation.1 | async-start | bytes 524288 | tf_op jit(solution)/shard_map/all_to_all | solution.py:395
  34.2 1.7 %copy-start = (bf16[2,256,512]{2,1,0:T(8,128)(2,1)S(1)}, bf16[2,256,512]{2,1,0:T(8,128)(2,1)}, u32[]{:S(2)}) copy-start(bf16[2,256,512]{2,1,0:T(8,128)(2,1)} %constant.16.clone.refs_7_.refs_4_) | copy-start | bytes 1572868
  34.2 1.7 %copy-start.1 = (bf16[2,256,512]{2,1,0:T(8,128)(2,1)S(1)}, bf16[2,256,512]{2,1,0:T(8,128)(2,1)}, u32[]{:S(2)}) copy-start(bf16[2,256,512]{2,1,0:T(8,128)(2,1)} %constant.15.clone.refs_6_.refs_3_) | copy-start | bytes 1572868
  34.2 1.7 %copy-start.2 = (f32[256,128]{1,0:T(8,128)S(1)}, f32[256,128]{1,0:T(8,128)}, u32[]{:S(2)}) copy-start(f32[256,128]{1,0:T(8,128)} %constant.14.clone.refs_5_.refs_2_) | copy-start | bytes 393220
  34.2 1.7 %copy-start.3 = (f32[256,128]{1,0:T(8,128)S(1)}, f32[256,128]{1,0:T(8,128)}, u32[]{:S(2)}) copy-start(f32[256,128]{1,0:T(8,128)} %constant.13.clone.refs_4_.refs_1_) | copy-start | bytes 393220
  34.5 1.4 %collective-permute-start.6 = (bf16[128,512]{1,0:T(8,128)(2,1)S(1)}, bf16[128,512]{1,0:T(8,128)(2,1)S(1)}, u32[]{:S(2)}, u32[]{:S(2)}) collective-permute-start(bf16[128,512]{1,0:T(8,128)(2,1)S(1)} %get-tuple-element.31), channel_id=1, source_target_pairs={{0,1},{1,0},{2,3},{3,2},{4,5},{5,4},{6,7},{7,6},{8,9},{9,8},{10,11... | collective-permute-start | bytes 393224 | tf_op jit(solution)/shard_map/ppermute | solution.py:384
  35.9 0.7 %copy-start.6 = (f32[32]{0:T(128)S(1)}, f32[32]{0:T(128)}, u32[]{:S(2)}) copy-start(f32[32]{0:T(128)} %param.19) | copy-start | bytes 388
  45.5 12.6 %copy-start.5 = (bf16[1,32,4096]{2,1,0:T(8,128)(2,1)S(1)}, bf16[1,32,4096]{2,1,0:T(8,128)(2,1)}, u32[]{:S(2)}) copy-start(bf16[1,32,4096]{2,1,0:T(8,128)(2,1)} %param.15) | copy-start | bytes 786436

commit v6 on v5

--- a/solution.py
+++ b/solution.py
@@ -41,8 +41,7 @@
         second_high.append(high)
         second_low.append(low)
     back = rows.conj().T / TOTAL
-    high, low = split_table(np.concatenate([back.real, -back.imag], axis=1))
-    last = np.concatenate([high, low], axis=0)
+    last, _ = split_table(np.concatenate([back.real, -back.imag], axis=1))
     return (
         first,
         twiddle.real.astype(np.float32),
@@ -102,7 +101,8 @@
     return dot(place_rows(key_row), rows).astype(BF16)
 
 
-def slabs_kernel(pool_ref, out_ref, held_ref, in_sems, out_sems):
+def slabs_kernel(pool_ref, taps_hbm, out_ref, *refs):
+    outs, (held_ref, taps_ref, in_sems, out_sems, sem) = refs[:4], refs[4:]
     reads = [
         pltpu.make_async_copy(pool_ref.at[z], held_ref.at[r], in_sems.at[r])
         for r, z in enumerate(RANKS)
@@ -110,16 +110,14 @@
     writes = [
         pltpu.make_async_copy(held_ref.at[r], out_ref.at[r], out_sems.at[r]) for r in range(8)
     ]
+    taps_read = pltpu.make_async_copy(taps_hbm, taps_ref, sem)
     for read in reads:
         read.start()
+    taps_read.start()
     for read, write in zip(reads, writes):
         read.wait()
         write.start()
-    for write in writes:
-        write.wait()
-
-
-def taps_y_kernel(taps_ref, *outs):
+    taps_read.wait()
     _, y, _ = place()
     rows = jnp.concatenate([taps_ref[:, a * N2 : (a + 1) * N2] for a in range(8)], axis=0)
     col = lax.broadcasted_iota(jnp.int32, (1, N1), 1)
@@ -128,6 +126,8 @@
     full = reorder(key, rows.astype(BF16))
     for d in range(4):
         outs[d][...] = full[d * 64 : (d + 1) * 64]
+    for write in writes:
+        write.wait()
 
 
 def taps_x_kernel(*refs):
@@ -252,8 +252,7 @@
         xr, xi = spec[:, :HALF], spec[:, HALF:]
         hr, hi = filter_ref[p, :, :HALF], filter_ref[p, :, HALF:]
         prod = jnp.concatenate([xr * hr - xi * hi, xr * hi + xi * hr], axis=1).astype(BF16)
-        high, low = whole_table(high_ref[p]), whole_table(low_ref[p])
-        turned.append(dot_t(prod, high) + dot_t(prod, low))
+        turned.append(dot_t(prod, whole_table(high_ref[p])))
     plus = turned[0] + turned[1]
     minus = turned[0] - turned[1]
     dr = jnp.concatenate([plus[:, :HALF], minus[:, :HALF]], axis=1)
@@ -261,9 +260,9 @@
     er = (dr * cosine + di * sine).astype(BF16)
     ei = (di * cosine - dr * sine).astype(BF16)
     copy.wait()
-    part = dot(last_ref[...], jnp.concatenate([er, ei], axis=0))
+    convolved = dot(last_ref[...], jnp.concatenate([er, ei], axis=0))
     direct = gain_ref[...] * x_ref[...].astype(F32)
-    out_ref[...] = (part[:N1] + part[N1:] + direct).astype(BF16)
+    out_ref[...] = (convolved + direct).astype(BF16)
 
 
 def gate_kernel(total_ref, query_ref, out_ref):
@@ -317,29 +316,24 @@
     call = functools.partial(
         pl.pallas_call, compiler_params=params(), cost_estimate=cost(0, 1 << 20)
     )
-    slabs = call(
+    slabs, *along_y = call(
         slabs_kernel,
-        out_shape=pltpu.HBM((8, 2, 32, N2), BF16),
-        in_specs=[HBM],
-        out_specs=HBM,
+        out_shape=(pltpu.HBM((8, 2, 32, N2), BF16),) + (rows_of(64),) * 4,
+        in_specs=[HBM, HBM],
+        out_specs=(HBM,) + (VMEM,) * 4,
         scratch_shapes=[
             pltpu.VMEM((8, 2, 32, N2), BF16),
+            pltpu.VMEM((32, 8 * N2), F32),
             pltpu.SemaphoreType.DMA((8,)),
             pltpu.SemaphoreType.DMA((8,)),
+            pltpu.SemaphoreType.DMA,
         ],
         name="slabs",
-    )(in_hbm(page_pool.reshape(8, 2, 32, N2)))
+    )(in_hbm(page_pool.reshape(8, 2, 32, N2)), in_hbm(filter_taps))
     pages = lax.all_to_all(
         slabs, "grp", split_axis=0, concat_axis=0, axis_index_groups=[RANKS], tiled=True
     ).reshape(512, N2)
 
-    along_y = call(
-        taps_y_kernel,
-        out_shape=(rows_of(64),) * 4,
-        in_specs=[VMEM],
-        out_specs=(VMEM,) * 4,
-        name="taps_y",
-    )(filter_taps)
     moved_y = [lax.ppermute(along_y[d], "seq", hops(0, d, 0)) for d in range(1, 4)]
 
     fresh, row_key = call(
@@ -415,7 +409,7 @@
         out_shape=rows_of(N1),
         in_specs=[VMEM] * 8 + [HBM],
         out_specs=VMEM,
-        scratch_shapes=[pltpu.VMEM((2 * N1, N2), BF16), pltpu.SemaphoreType.DMA],
+        scratch_shapes=[pltpu.VMEM((N1, N2), BF16), pltpu.SemaphoreType.DMA],
         cost_estimate=cost(0, 1 << 23),
         name="conv",
     )(columns, spectrum, gain, first, *middle, in_hbm(last))

time: 59.4 us -> 58.5 us (0.985)
  Pallas kernels: 10.4 us -> 9.73 us
    pallas_call x2 -> x1, Pallas kernels: 2.06 us -> 1.82 us  [shards(): call(slabs_kernel, out_shape=(pltpu.HBM((8, 2, 32, N2), BF16),) + (rows_o...]
where the time goes in v6:
time: 58.5 us; the launch traced here: 58.1 us
  starting transfers between devices  28.3 us (48%)
  blocking collectives  12.6 us (22%)
  Pallas kernels  9.73 us (17%)
  waiting for transfers between devices  5.99 us (10%)
  between operations  0.81 us (1%)
  local copies, waits for them, and re-layouts  0.67 us (1%)
    all_to_all x1, blocking collectives, shards(): lax.all_to_all(convolved.reshape(32, 8, N2), 'seq', split_axis=0, concat_...  12.6 us
    all_to_all x1, starting transfers between devices, shards(): lax.all_to_all(slabs, 'grp', split_axis=0, concat_axis=0, axis_index_grou...  11.1 us
    all_to_all x1, starting transfers between devices, shards(): lax.all_to_all(send.reshape(32, 8, N2), 'seq', split_axis=0, concat_axis=...  6.96 us
    ppermute x3, starting transfers between devices, shards(): lax.ppermute(along_y[d], 'seq', hops(0, d, 0))  4.99 us
    ppermute x3, starting transfers between devices, shards(): lax.ppermute(along_x[d], 'seq', hops(d, 0, 0))  4.89 us
    all_to_all x1, waiting for transfers between devices, shards(): lax.all_to_all(send.reshape(32, 8, N2), 'seq', split_axis=0, concat_axis=...  4.3 us
    pallas_call x1, Pallas kernels, shards(): call(filter_kernel, out_shape=(jax.ShapeDtypeStruct((2, N1, N2), F32), ja...  2.28 us
    pallas_call x1, Pallas kernels, shards(): call(conv_kernel, out_shape=rows_of(N1), in_specs=[VMEM] * 8 + [HBM], out...  1.87 us
  transfers between devices with their start and end apart: 9, of which 3 were waited for; matrix products, arithmetic and copies ran while one was open for 0% of the time, Pallas kernels for 9%

profile of v6, /device:TPU:1, one launch (start us, length us, event | category | flops | bytes accessed | tf_op | source)
XLA Modules:
  0.0 58.1 jit_solution(7254423311120589876)
XLA Ops:
  0.0 1.8 %slabs.1 = (bf16[8,2,32,512]{3,2,1,0:T(8,128)(2,1)}, bf16[64,512]{1,0:T(8,128)(2,1)S(1)}, bf16[64,512]{1,0:T(8,128)(2,1)S(1)}, bf16[64,512]{1,0:T(8,128)(2,1)S(1)}, bf16[64,512]{1,0:T(8,128)(2,1)S(1)}) custom-call(bf16[8,2,32,512]{3,2,1,0:T(8,128)(2,1)} %bitcast.17, f32[32,4096]{1,0:T(8,128)} %taps_hbm.1), custom_call_target="tpu_custom_call" | custom-call | bytes 1048576 | tf_op jit(solution)/shard_map/slabs/pallas_call | solution.py:319
  1.8 11.1 %all-to-all-start = ((bf16[8,2,32,512]{3,2,1,0:T(8,128)(2,1)}), bf16[8,2,32,512]{3,2,1,0:T(8,128)(2,1)S(1)}, u32[]{:S(2)}, u32[]{:S(2)}) async-start(bf16[8,2,32,512]{3,2,1,0:T(8,128)(2,1)} %get-tuple-element.24), calls=%async_computation | async-start | bytes 1048576 | tf_op jit(solution)/shard_map/all_to_all | solution.py:333
  13.0 1.3 %collective-permute-start = (bf16[64,512]{1,0:T(8,128)(2,1)S(1)}, bf16[64,512]{1,0:T(8,128)(2,1)S(1)}, u32[]{:S(2)}, u32[]{:S(2)}) collective-permute-start(bf16[64,512]{1,0:T(8,128)(2,1)S(1)} %get-tuple-element.25), channel_id=1, source_target_pairs={{0,2},{1,3},{2,4},{3,5},{4,6},{5,7},{6,0},{7,1},{8,10},{9,11},{10,... | collective-permute-start | bytes 196616 | tf_op jit(solution)/shard_map/ppermute | solution.py:337
  14.3 2.6 %collective-permute-start.1 = (bf16[64,512]{1,0:T(8,128)(2,1)S(1)}, bf16[64,512]{1,0:T(8,128)(2,1)S(1)}, u32[]{:S(2)}, u32[]{:S(2)}) collective-permute-start(bf16[64,512]{1,0:T(8,128)(2,1)S(1)} %get-tuple-element.26), channel_id=1, source_target_pairs={{0,4},{1,5},{2,6},{3,7},{4,0},{5,1},{6,2},{7,3},{8,12},{9,13},{10,... | collective-permute-start | bytes 196616 | tf_op jit(solution)/shard_map/ppermute | solution.py:337
  16.9 1.1 %collective-permute-start.2 = (bf16[64,512]{1,0:T(8,128)(2,1)S(1)}, bf16[64,512]{1,0:T(8,128)(2,1)S(1)}, u32[]{:S(2)}, u32[]{:S(2)}) collective-permute-start(bf16[64,512]{1,0:T(8,128)(2,1)S(1)} %get-tuple-element.27), channel_id=1, source_target_pairs={{0,6},{1,7},{2,0},{3,1},{4,2},{5,3},{6,4},{7,5},{8,14},{9,15},{10,... | collective-permute-start | bytes 196616 | tf_op jit(solution)/shard_map/ppermute | solution.py:337
  18.6 1.4 %stage.1 = (bf16[256,512]{1,0:T(8,128)(2,1)S(1)}, s32[1,512]{1,0:T(1,128)S(1)}) custom-call(s32[1,8]{1,0:T(1,128)} %owner_hbm.1, s32[1,8]{1,0:T(1,128)} %slot_hbm.1, s32[1]{0:T(128)S(6)} %copy.16.suffix_ref, bf16[32,4096]{1,0:T(8,128)(2,1)} %bitcast.18, bf16[32,4096]{1,0:T(8,128)(2,1)} %bitcast.19, bf16[64,512]{1,0:T(8,128)(2,1)S(1)} %get-tuple-element.21.tie_ref.refs_0_), custom_call_target="tpu_custom_call" | custom-call | bytes 1048576 | tf_op jit(solution)/shard_map/stage/pallas_call | solution.py:339
  20.0 0.0 collective-permute-done.refs_1_
  20.0 0.0 collective-permute-done.1.refs_2_
  20.0 0.6 collective-permute-done.2.refs_3_
  20.6 0.2 taps_x.1
  20.8 1.3 %collective-permute-start.3 = (bf16[64,512]{1,0:T(8,128)(2,1)S(1)}, bf16[64,512]{1,0:T(8,128)(2,1)S(1)}, u32[]{:S(2)}, u32[]{:S(2)}) collective-permute-start(bf16[64,512]{1,0:T(8,128)(2,1)S(1)} %get-tuple-element.29), channel_id=1, source_target_pairs={{0,8},{1,9},{2,10},{3,11},{4,12},{5,13},{6,14},{7,15},{8,16},{9,17... | collective-permute-start | bytes 196616 | tf_op jit(solution)/shard_map/ppermute | solution.py:368
  22.1 2.5 %collective-permute-start.4 = (bf16[64,512]{1,0:T(8,128)(2,1)S(1)}, bf16[64,512]{1,0:T(8,128)(2,1)S(1)}, u32[]{:S(2)}, u32[]{:S(2)}) collective-permute-start(bf16[64,512]{1,0:T(8,128)(2,1)S(1)} %get-tuple-element.30), channel_id=1, source_target_pairs={{0,16},{1,17},{2,18},{3,19},{4,20},{5,21},{6,22},{7,23},{8,24},{9,... | collective-permute-start | bytes 196616 | tf_op jit(solution)/shard_map/ppermute | solution.py:368
  24.5 1.1 %collective-permute-start.5 = (bf16[64,512]{1,0:T(8,128)(2,1)S(1)}, bf16[64,512]{1,0:T(8,128)(2,1)S(1)}, u32[]{:S(2)}, u32[]{:S(2)}) collective-permute-start(bf16[64,512]{1,0:T(8,128)(2,1)S(1)} %get-tuple-element.31), channel_id=1, source_target_pairs={{0,24},{1,25},{2,26},{3,27},{4,28},{5,29},{6,30},{7,31},{8,0},{9,1... | collective-permute-start | bytes 196616 | tf_op jit(solution)/shard_map/ppermute | solution.py:368
  25.7 0.0 all-to-all-done
  25.7 1.0 %select.1 = bf16[256,512]{1,0:T(8,128)(2,1)} custom-call(s32[1,512]{1,0:T(1,128)S(1)} %get-tuple-element.22.row_key_ref.refs_4_, bf16[256,512]{1,0:T(8,128)(2,1)S(1)} %get-tuple-element.23.fresh_ref, bf16[512,512]{1,0:T(8,128)(2,1)S(1)} %bitcast.14), custom_call_target="tpu_custom_call" | custom-call | flops 17179869184 | bytes 268435456 | tf_op jit(solution)/shard_map/select/pallas_call | solution.py:380
  26.7 7.0 %all-to-all-start.1 = ((bf16[32,8,512]{2,1,0:T(8,128)(2,1)}), bf16[32,8,512]{2,1,0:T(8,128)(2,1)S(1)}, u32[]{:S(2)}, u32[]{:S(2)}) async-start(bf16[32,8,512]{2,1,0:T(8,128)(2,1)} %bitcast.4), calls=%async_computation.1 | async-start | bytes 524288 | tf_op jit(solution)/shard_map/all_to_all | solution.py:389
  33.7 0.0 collective-permute-done.4.refs_2_
  33.7 0.0 collective-permute-done.5.refs_3_
  33.7 0.0 copy-start
  33.7 0.0 copy-start.1
  33.7 0.0 copy-start.2
  33.7 0.0 copy-start.3
  33.8 0.2 taps_core.1
  34.0 0.3 collective-permute-start.6
  34.3 1.1 %collective-permute-done.6.refs_1_ = bf16[128,512]{1,0:T(8,128)(2,1)S(1)} collective-permute-done((bf16[128,512]{1,0:T(8,128)(2,1)S(1)}, bf16[128,512]{1,0:T(8,128)(2,1)S(1)}, u32[]{:S(2)}, u32[]{:S(2)}) %collective-permute-start.6) | collective-permute-done | bytes 131104 | tf_op jit(solution)/shard_map/ppermute | solution.py:378
  35.4 0.6 %copy-done.5 = f32[32]{0:T(128)S(1)} copy-done((f32[32]{0:T(128)S(1)}, f32[32]{0:T(128)}, u32[]{:S(2)}) %copy-start.5) | copy-done | bytes 152
  36.1 2.3 %filter.1 = (f32[2,256,512]{2,1,0:T(8,128)S(1)}, bf16[1024,256]{1,0:T(8,128)(2,1)S(1)}, f32[1,512]{1,0:T(1,128)S(1)}) custom-call(bf16[128,512]{1,0:T(8,128)(2,1)S(1)} %get-tuple-element.32.refs_0_, bf16[128,512]{1,0:T(8,128)(2,1)S(1)} %collective-permute-done.6.refs_1_, f32[1,32]{1,0:T(1,128)S(1)} %bitcast.16, bf16[1024,256]{1,0:T(8,128)(2,1)} %constant.12.clone.refs_3_, ...), custom_call_target="tpu_custom_call" | custom-call | flops 268435456 | bytes 268435456 | tf_op jit(solution)/shard_map/filter/pallas_call | solution.py:394
  38.4 4.3 %all-to-all-done.1 = bf16[32,8,512]{2,1,0:T(8,128)(2,1)S(1)} async-done(((bf16[32,8,512]{2,1,0:T(8,128)(2,1)}), bf16[32,8,512]{2,1,0:T(8,128)(2,1)S(1)}, u32[]{:S(2)}, u32[]{:S(2)}) %all-to-all-start.1) | async-done | bytes 262176 | tf_op jit(solution)/shard_map/all_to_all | solution.py:389
  42.7 1.9 %conv.1 = bf16[256,512]{1,0:T(8,128)(2,1)S(1)} custom-call(bf16[256,512]{1,0:T(8,128)(2,1)S(1)} %bitcast.11, f32[2,256,512]{2,1,0:T(8,128)S(1)} %get-tuple-element.34.filter_ref, f32[1,512]{1,0:T(1,128)S(1)} %get-tuple-element.35.gain_ref, bf16[1024,256]{1,0:T(8,128)(2,1)S(1)} %get-tuple-element.36.refs_0_, f32[256,128]{1,0:T(8,128)S(1)} %copy-done.3, ...), custom_call_target="tpu_custom_call" | custom-call | bytes 8388608 | tf_op jit(solution)/shard_map/conv/pallas_call | solution.py:407
  44.5 0.0 copy-start.4
  44.6 12.6 %all_to_all.15 = bf16[32,8,512]{2,1,0:T(8,128)(2,1)S(1)} all-to-all(bf16[32,8,512]{2,1,0:T(8,128)(2,1)S(1)} %bitcast.12), channel_id=1, replica_groups=mesh['grp'=8,'seq'=32] {'seq'}, dimensions={0} | all-to-all | bytes 524288 | tf_op jit(solution)/shard_map/all_to_all | solution.py:417
  57.1 0.9 %gate.1 = bf16[32,4096]{1,0:T(8,128)(2,1)} custom-call(bf16[256,512]{1,0:T(8,128)(2,1)S(1)} %bitcast.13, bf16[32,4096]{1,0:T(8,128)(2,1)S(1)} %bitcast.15), custom_call_target="tpu_custom_call" | custom-call | bytes 1048576 | tf_op jit(solution)/shard_map/gate/pallas_call | solution.py:421
  (7 shorter events, 0.0 us)
Async XLA Ops:
  1.8 23.9 %all-to-all-start = ((bf16[8,2,32,512]{3,2,1,0:T(8,128)(2,1)}), bf16[8,2,32,512]{3,2,1,0:T(8,128)(2,1)S(1)}, u32[]{:S(2)}, u32[]{:S(2)}) async-start(bf16[8,2,32,512]{3,2,1,0:T(8,128)(2,1)} %get-tuple-element.24), calls=%async_computation | async-start | bytes 1048576 | tf_op jit(solution)/shard_map/all_to_all | solution.py:333
  13.0 7.0 %collective-permute-start = (bf16[64,512]{1,0:T(8,128)(2,1)S(1)}, bf16[64,512]{1,0:T(8,128)(2,1)S(1)}, u32[]{:S(2)}, u32[]{:S(2)}) collective-permute-start(bf16[64,512]{1,0:T(8,128)(2,1)S(1)} %get-tuple-element.25), channel_id=1, source_target_pairs={{0,2},{1,3},{2,4},{3,5},{4,6},{5,7},{6,0},{7,1},{8,10},{9,11},{10,... | collective-permute-start | bytes 196616 | tf_op jit(solution)/shard_map/ppermute | solution.py:337
  14.3 5.7 %collective-permute-start.1 = (bf16[64,512]{1,0:T(8,128)(2,1)S(1)}, bf16[64,512]{1,0:T(8,128)(2,1)S(1)}, u32[]{:S(2)}, u32[]{:S(2)}) collective-permute-start(bf16[64,512]{1,0:T(8,128)(2,1)S(1)} %get-tuple-element.26), channel_id=1, source_target_pairs={{0,4},{1,5},{2,6},{3,7},{4,0},{5,1},{6,2},{7,3},{8,12},{9,13},{10,... | collective-permute-start | bytes 196616 | tf_op jit(solution)/shard_map/ppermute | solution.py:337
  16.9 3.7 %collective-permute-start.2 = (bf16[64,512]{1,0:T(8,128)(2,1)S(1)}, bf16[64,512]{1,0:T(8,128)(2,1)S(1)}, u32[]{:S(2)}, u32[]{:S(2)}) collective-permute-start(bf16[64,512]{1,0:T(8,128)(2,1)S(1)} %get-tuple-element.27), channel_id=1, source_target_pairs={{0,6},{1,7},{2,0},{3,1},{4,2},{5,3},{6,4},{7,5},{8,14},{9,15},{10,... | collective-permute-start | bytes 196616 | tf_op jit(solution)/shard_map/ppermute | solution.py:337
  20.8 12.9 %collective-permute-start.3 = (bf16[64,512]{1,0:T(8,128)(2,1)S(1)}, bf16[64,512]{1,0:T(8,128)(2,1)S(1)}, u32[]{:S(2)}, u32[]{:S(2)}) collective-permute-start(bf16[64,512]{1,0:T(8,128)(2,1)S(1)} %get-tuple-element.29), channel_id=1, source_target_pairs={{0,8},{1,9},{2,10},{3,11},{4,12},{5,13},{6,14},{7,15},{8,16},{9,17... | collective-permute-start | bytes 196616 | tf_op jit(solution)/shard_map/ppermute | solution.py:368
  22.1 11.6 %collective-permute-start.4 = (bf16[64,512]{1,0:T(8,128)(2,1)S(1)}, bf16[64,512]{1,0:T(8,128)(2,1)S(1)}, u32[]{:S(2)}, u32[]{:S(2)}) collective-permute-start(bf16[64,512]{1,0:T(8,128)(2,1)S(1)} %get-tuple-element.30), channel_id=1, source_target_pairs={{0,16},{1,17},{2,18},{3,19},{4,20},{5,21},{6,22},{7,23},{8,24},{9,... | collective-permute-start | bytes 196616 | tf_op jit(solution)/shard_map/ppermute | solution.py:368
  24.5 9.1 %collective-permute-start.5 = (bf16[64,512]{1,0:T(8,128)(2,1)S(1)}, bf16[64,512]{1,0:T(8,128)(2,1)S(1)}, u32[]{:S(2)}, u32[]{:S(2)}) collective-permute-start(bf16[64,512]{1,0:T(8,128)(2,1)S(1)} %get-tuple-element.31), channel_id=1, source_target_pairs={{0,24},{1,25},{2,26},{3,27},{4,28},{5,29},{6,30},{7,31},{8,0},{9,1... | collective-permute-start | bytes 196616 | tf_op jit(solution)/shard_map/ppermute | solution.py:368
  26.7 16.0 %all-to-all-start.1 = ((bf16[32,8,512]{2,1,0:T(8,128)(2,1)}), bf16[32,8,512]{2,1,0:T(8,128)(2,1)S(1)}, u32[]{:S(2)}, u32[]{:S(2)}) async-start(bf16[32,8,512]{2,1,0:T(8,128)(2,1)} %bitcast.4), calls=%async_computation.1 | async-start | bytes 524288 | tf_op jit(solution)/shard_map/all_to_all | solution.py:389
  33.7 1.7 %copy-start = (bf16[2,256,512]{2,1,0:T(8,128)(2,1)S(1)}, bf16[2,256,512]{2,1,0:T(8,128)(2,1)}, u32[]{:S(2)}) copy-start(bf16[2,256,512]{2,1,0:T(8,128)(2,1)} %constant.16.clone.refs_7_.refs_4_) | copy-start | bytes 1572868
  33.7 1.7 %copy-start.1 = (bf16[2,256,512]{2,1,0:T(8,128)(2,1)S(1)}, bf16[2,256,512]{2,1,0:T(8,128)(2,1)}, u32[]{:S(2)}) copy-start(bf16[2,256,512]{2,1,0:T(8,128)(2,1)} %constant.15.clone.refs_6_.refs_3_) | copy-start | bytes 1572868
  33.7 1.7 %copy-start.2 = (f32[256,128]{1,0:T(8,128)S(1)}, f32[256,128]{1,0:T(8,128)}, u32[]{:S(2)}) copy-start(f32[256,128]{1,0:T(8,128)} %constant.14.clone.refs_5_.refs_2_) | copy-start | bytes 393220
  33.7 1.7 %copy-start.3 = (f32[256,128]{1,0:T(8,128)S(1)}, f32[256,128]{1,0:T(8,128)}, u32[]{:S(2)}) copy-start(f32[256,128]{1,0:T(8,128)} %constant.13.clone.refs_4_.refs_1_) | copy-start | bytes 393220
  34.0 1.4 %collective-permute-start.6 = (bf16[128,512]{1,0:T(8,128)(2,1)S(1)}, bf16[128,512]{1,0:T(8,128)(2,1)S(1)}, u32[]{:S(2)}, u32[]{:S(2)}) collective-permute-start(bf16[128,512]{1,0:T(8,128)(2,1)S(1)} %get-tuple-element.33), channel_id=1, source_target_pairs={{0,1},{1,0},{2,3},{3,2},{4,5},{5,4},{6,7},{7,6},{8,9},{9,8},{10,11... | collective-permute-start | bytes 393224 | tf_op jit(solution)/shard_map/ppermute | solution.py:378
  35.4 0.7 %copy-start.5 = (f32[32]{0:T(128)S(1)}, f32[32]{0:T(128)}, u32[]{:S(2)}) copy-start(f32[32]{0:T(128)} %param.19) | copy-start | bytes 388
  44.5 12.6 %copy-start.4 = (bf16[1,32,4096]{2,1,0:T(8,128)(2,1)S(1)}, bf16[1,32,4096]{2,1,0:T(8,128)(2,1)}, u32[]{:S(2)}) copy-start(bf16[1,32,4096]{2,1,0:T(8,128)(2,1)} %param.15) | copy-start | bytes 786436

commit v7 on v6

--- a/solution.py
+++ b/solution.py
@@ -14,41 +14,33 @@
 HALF = N2 // 2
 TOTAL = N1 * N2
 RANKS = (4, 0, 5, 1, 6, 2, 7, 3)
+STEP, UNSTEP = 13, 5
+SEQ_RANKS = tuple(STEP * r % 32 for r in range(32))
 BF16 = jnp.bfloat16
 F32 = jnp.float32
-
-
-def split_table(table):
-    high = table.astype(ml_dtypes.bfloat16)
-    low = (table - high.astype(np.float64)).astype(ml_dtypes.bfloat16)
-    return high, low
 
 
 @functools.cache
 def tables():
     k1 = np.arange(N1)[:, None] + 0.25
-    n1 = np.arange(N1)[None, :]
+    n1 = (np.array(SEQ_RANKS)[:, None] * 8 + np.arange(8)[None, :]).reshape(1, N1)
     rows = np.exp(-2j * np.pi * k1 * n1 / N1)
-    high, low = split_table(np.concatenate([rows.real, rows.imag], axis=0))
-    first = np.concatenate([high, low], axis=0)
+    first = np.concatenate([rows.real, rows.imag], axis=0)
     twiddle = np.exp(-2j * np.pi * k1 * np.arange(128)[None, :] / TOTAL)
     m = np.arange(HALF)[:, None]
     l = np.arange(HALF)[None, :]
-    second_high, second_low = [], []
+    second = []
     for p in range(2):
         f = np.exp(-2j * np.pi * m * (l + 0.5 * p) / HALF)
-        high, low = split_table(np.concatenate([f.real, f.imag], axis=1))
-        second_high.append(high)
-        second_low.append(low)
+        second.append(np.concatenate([f.real, f.imag], axis=1))
     back = rows.conj().T / TOTAL
-    last, _ = split_table(np.concatenate([back.real, -back.imag], axis=1))
+    last = np.concatenate([back.real, -back.imag], axis=1)
     return (
-        first,
+        first.astype(ml_dtypes.bfloat16),
         twiddle.real.astype(np.float32),
         twiddle.imag.astype(np.float32),
-        np.stack(second_high),
-        np.stack(second_low),
-        last,
+        np.stack(second).astype(ml_dtypes.bfloat16),
+        last.astype(ml_dtypes.bfloat16),
     )
 
 
@@ -73,12 +65,12 @@
 
 def send_order():
     col = lax.broadcasted_iota(jnp.int32, (1, N1), 1)
-    return (col & 31) * 8 + (col >> 5)
+    return ((col * UNSTEP) & 31) * 8 + (col >> 5)
 
 
 def block_order():
     col = lax.broadcasted_iota(jnp.int32, (1, N1), 1)
-    return (col & 7) * 32 + (col >> 3)
+    return (col & 7) * 32 + (((col >> 3) * STEP) & 31)
 
 
 def fetch(sources, targets, sems):
@@ -182,7 +174,7 @@
     fresh = []
     for a in range(8):
         hit = ((column >> 5) == page[:, a : a + 1]) & (count > a)
-        row_key = jnp.where(hit, (column & 31) * 8 + a, row_key)
+        row_key = jnp.where(hit, ((column * UNSTEP) & 31) * 8 + a, row_key)
         cols = slice(a * N2, (a + 1) * N2)
         product = key_ref[:, cols].astype(F32) * value_ref[:, cols].astype(F32)
         fresh.append(jnp.where(count > a, 0.0, product))
@@ -207,10 +199,9 @@
     return jnp.concatenate(cosines, axis=1), jnp.concatenate(sines, axis=1)
 
 
-def forward(rows, first_ref, cosine, sine, high_ref, low_ref):
+def forward(rows, first_ref, cosine, sine, second_ref):
     part = dot(first_ref[...], rows)
-    r = part[:N1] + part[2 * N1 : 3 * N1]
-    i = part[N1 : 2 * N1] + part[3 * N1 :]
+    r, i = part[:N1], part[N1:]
     br = r * cosine - i * sine
     bi = r * sine + i * cosine
     spectra = []
@@ -218,41 +209,42 @@
         cr = br[:, :HALF] + sign * br[:, HALF:]
         ci = bi[:, :HALF] + sign * bi[:, HALF:]
         c = jnp.concatenate([cr, ci], axis=1).astype(BF16)
-        spectra.append(dot(c, whole_table(high_ref[p])) + dot(c, whole_table(low_ref[p])))
+        spectra.append(dot(c, whole_table(second_ref[p])))
     return spectra
 
 
 def filter_kernel(*refs):
-    keep_ref, came_ref, gain_ref, first_hbm, cos_ref, sin_ref, high_ref, low_ref, *refs = refs
+    keep_ref, came_ref, gain_ref, first_hbm, cos_ref, sin_ref, second_ref, *refs = refs
     out_ref, first_ref, mine_ref, sems = refs
     copy = pltpu.make_async_copy(first_hbm, first_ref, sems)
     copy.start()
     _, _, core = place()
     col = lax.broadcasted_iota(jnp.int32, (1, N1), 1)
-    key = ((col >> 3) & 15) * 16 + ((col >> 7) ^ core) * 8 + (col & 7)
+    source = ((col >> 3) & 15) * 2 + ((col >> 7) ^ core)
+    key = ((source * UNSTEP) & 31) * 8 + (col & 7)
     rows = reorder(key, jnp.concatenate([keep_ref[...], came_ref[...]], axis=0))
     lane = lax.broadcasted_iota(jnp.int32, (1, 32), 1)
     mine = jnp.where(lane == lax.axis_index("seq"), gain_ref[...], 0.0)
     mine_ref[...] = jnp.broadcast_to(jnp.sum(mine, axis=1, keepdims=True), (1, N2))
     cosine, sine = twiddles(cos_ref, sin_ref)
     copy.wait()
-    spectra = forward(rows, first_ref, cosine, sine, high_ref, low_ref)
+    spectra = forward(rows, first_ref, cosine, sine, second_ref)
     for p, spec in enumerate(spectra):
         out_ref[p] = spec
 
 
 def conv_kernel(x_ref, filter_ref, gain_ref, *refs):
-    first_ref, cos_ref, sin_ref, high_ref, low_ref, last_hbm, out_ref, last_ref, sem = refs
+    first_ref, cos_ref, sin_ref, second_ref, last_hbm, out_ref, last_ref, sem = refs
     copy = pltpu.make_async_copy(last_hbm, last_ref, sem)
     copy.start()
     turned = []
     cosine, sine = twiddles(cos_ref, sin_ref)
-    spectra = forward(x_ref[...], first_ref, cosine, sine, high_ref, low_ref)
+    spectra = forward(x_ref[...], first_ref, cosine, sine, second_ref)
     for p, spec in enumerate(spectra):
         xr, xi = spec[:, :HALF], spec[:, HALF:]
         hr, hi = filter_ref[p, :, :HALF], filter_ref[p, :, HALF:]
         prod = jnp.concatenate([xr * hr - xi * hi, xr * hi + xi * hr], axis=1).astype(BF16)
-        turned.append(dot_t(prod, whole_table(high_ref[p])))
+        turned.append(dot_t(prod, whole_table(second_ref[p])))
     plus = turned[0] + turned[1]
     minus = turned[0] - turned[1]
     dr = jnp.concatenate([plus[:, :HALF], minus[:, :HALF]], axis=1)
@@ -387,7 +379,7 @@
     )(row_key, fresh, pages)
 
     columns = lax.all_to_all(
-        send.reshape(32, 8, N2), "seq", split_axis=0, concat_axis=0, tiled=True
+        send.reshape(32, 8, N2), "seq", split_axis=0, concat_axis=0, axis_index_groups=[SEQ_RANKS], tiled=True
     ).reshape(N1, N2)
 
     first, *middle, last = [jnp.asarray(t) for t in tables()]
@@ -398,7 +390,7 @@
             jax.ShapeDtypeStruct(first.shape, BF16),
             jax.ShapeDtypeStruct((1, N2), F32),
         ),
-        in_specs=[VMEM] * 3 + [HBM] + [VMEM] * 4,
+        in_specs=[VMEM] * 3 + [HBM] + [VMEM] * 3,
         out_specs=(VMEM,) * 3,
         scratch_shapes=[pltpu.SemaphoreType.DMA],
         cost_estimate=cost(1 << 28, 1 << 28),
@@ -407,7 +399,7 @@
     convolved = call(
         conv_kernel,
         out_shape=rows_of(N1),
-        in_specs=[VMEM] * 8 + [HBM],
+        in_specs=[VMEM] * 7 + [HBM],
         out_specs=VMEM,
         scratch_shapes=[pltpu.VMEM((N1, N2), BF16), pltpu.SemaphoreType.DMA],
         cost_estimate=cost(0, 1 << 23),
@@ -415,7 +407,7 @@
     )(columns, spectrum, gain, first, *middle, in_hbm(last))
 
     back = lax.all_to_all(
-        convolved.reshape(32, 8, N2), "seq", split_axis=0, concat_axis=0, tiled=True
+        convolved.reshape(32, 8, N2), "seq", split_axis=0, concat_axis=0, axis_index_groups=[SEQ_RANKS], tiled=True
     ).reshape(N1, N2)
 
     gated = call(

time: 58.5 us -> 57.3 us (0.979)
  Pallas kernels: 9.73 us -> 8.9 us
  transfers between devices with their start and end apart: 9 -> 9, of which waited for: 3 -> 3; matrix products, arithmetic and copies ran while one was open for 0% -> 0% of each run, Pallas kernels for 9% -> 8%
where the time goes in v7:
time: 57.3 us; the launch traced here: 56.9 us
  starting transfers between devices  28.3 us (49%)
  blocking collectives  12.4 us (22%)
  Pallas kernels  8.9 us (16%)
  waiting for transfers between devices  5.83 us (10%)
  between operations  0.79 us (1%)
  local copies, waits for them, and re-layouts  0.67 us (1%)
    all_to_all x1, blocking collectives, shards(): lax.all_to_all(convolved.reshape(32, 8, N2), 'seq', split_axis=0, concat_...  12.4 us
    all_to_all x1, starting transfers between devices, shards(): lax.all_to_all(slabs, 'grp', split_axis=0, concat_axis=0, axis_index_grou...  11.1 us
    all_to_all x1, starting transfers between devices, shards(): lax.all_to_all(send.reshape(32, 8, N2), 'seq', split_axis=0, concat_axis=...  6.96 us
    ppermute x3, starting transfers between devices, shards(): lax.ppermute(along_y[d], 'seq', hops(0, d, 0))  4.99 us
    ppermute x3, starting transfers between devices, shards(): lax.ppermute(along_x[d], 'seq', hops(d, 0, 0))  4.9 us
    all_to_all x1, waiting for transfers between devices, shards(): lax.all_to_all(send.reshape(32, 8, N2), 'seq', split_axis=0, concat_axis=...  4.13 us
    pallas_call x1, Pallas kernels, shards(): call(slabs_kernel, out_shape=(pltpu.HBM((8, 2, 32, N2), BF16),) + (rows_o...  1.83 us
    pallas_call x1, Pallas kernels, shards(): call(filter_kernel, out_shape=(jax.ShapeDtypeStruct((2, N1, N2), F32), ja...  1.8 us
  transfers between devices with their start and end apart: 9, of which 3 were waited for; matrix products, arithmetic and copies ran while one was open for 0% of the time, Pallas kernels for 8%

profile of v7, /device:TPU:1, one launch (start us, length us, event | category | flops | bytes accessed | tf_op | source)
XLA Modules:
  0.0 56.9 jit_solution(6411005613991638395)
XLA Ops:
  0.0 1.8 %slabs.1 = (bf16[8,2,32,512]{3,2,1,0:T(8,128)(2,1)}, bf16[64,512]{1,0:T(8,128)(2,1)S(1)}, bf16[64,512]{1,0:T(8,128)(2,1)S(1)}, bf16[64,512]{1,0:T(8,128)(2,1)S(1)}, bf16[64,512]{1,0:T(8,128)(2,1)S(1)}) custom-call(bf16[8,2,32,512]{3,2,1,0:T(8,128)(2,1)} %bitcast.17, f32[32,4096]{1,0:T(8,128)} %taps_hbm.1), custom_call_target="tpu_custom_call" | custom-call | bytes 1048576 | tf_op jit(solution)/shard_map/slabs/pallas_call | solution.py:311
  1.8 11.1 %all-to-all-start = ((bf16[8,2,32,512]{3,2,1,0:T(8,128)(2,1)}), bf16[8,2,32,512]{3,2,1,0:T(8,128)(2,1)S(1)}, u32[]{:S(2)}, u32[]{:S(2)}) async-start(bf16[8,2,32,512]{3,2,1,0:T(8,128)(2,1)} %get-tuple-element.24), calls=%async_computation | async-start | bytes 1048576 | tf_op jit(solution)/shard_map/all_to_all | solution.py:325
  13.0 1.3 %collective-permute-start = (bf16[64,512]{1,0:T(8,128)(2,1)S(1)}, bf16[64,512]{1,0:T(8,128)(2,1)S(1)}, u32[]{:S(2)}, u32[]{:S(2)}) collective-permute-start(bf16[64,512]{1,0:T(8,128)(2,1)S(1)} %get-tuple-element.25), channel_id=1, source_target_pairs={{0,2},{1,3},{2,4},{3,5},{4,6},{5,7},{6,0},{7,1},{8,10},{9,11},{10,... | collective-permute-start | bytes 196616 | tf_op jit(solution)/shard_map/ppermute | solution.py:329
  14.3 2.6 %collective-permute-start.1 = (bf16[64,512]{1,0:T(8,128)(2,1)S(1)}, bf16[64,512]{1,0:T(8,128)(2,1)S(1)}, u32[]{:S(2)}, u32[]{:S(2)}) collective-permute-start(bf16[64,512]{1,0:T(8,128)(2,1)S(1)} %get-tuple-element.26), channel_id=1, source_target_pairs={{0,4},{1,5},{2,6},{3,7},{4,0},{5,1},{6,2},{7,3},{8,12},{9,13},{10,... | collective-permute-start | bytes 196616 | tf_op jit(solution)/shard_map/ppermute | solution.py:329
  16.9 1.1 %collective-permute-start.2 = (bf16[64,512]{1,0:T(8,128)(2,1)S(1)}, bf16[64,512]{1,0:T(8,128)(2,1)S(1)}, u32[]{:S(2)}, u32[]{:S(2)}) collective-permute-start(bf16[64,512]{1,0:T(8,128)(2,1)S(1)} %get-tuple-element.27), channel_id=1, source_target_pairs={{0,6},{1,7},{2,0},{3,1},{4,2},{5,3},{6,4},{7,5},{8,14},{9,15},{10,... | collective-permute-start | bytes 196616 | tf_op jit(solution)/shard_map/ppermute | solution.py:329
  18.6 1.4 %stage.1 = (bf16[256,512]{1,0:T(8,128)(2,1)S(1)}, s32[1,512]{1,0:T(1,128)S(1)}) custom-call(s32[1,8]{1,0:T(1,128)} %owner_hbm.1, s32[1,8]{1,0:T(1,128)} %slot_hbm.1, s32[1]{0:T(128)S(6)} %copy.15.suffix_ref, bf16[32,4096]{1,0:T(8,128)(2,1)} %bitcast.18, bf16[32,4096]{1,0:T(8,128)(2,1)} %bitcast.19, bf16[64,512]{1,0:T(8,128)(2,1)S(1)} %get-tuple-element.21.tie_ref.refs_0_), custom_call_target="tpu_custom_call" | custom-call | bytes 1048576 | tf_op jit(solution)/shard_map/stage/pallas_call | solution.py:331
  20.0 0.0 collective-permute-done.refs_1_
  20.0 0.0 collective-permute-done.1.refs_2_
  20.0 0.6 collective-permute-done.2.refs_3_
  20.6 0.2 taps_x.1
  20.8 1.3 %collective-permute-start.3 = (bf16[64,512]{1,0:T(8,128)(2,1)S(1)}, bf16[64,512]{1,0:T(8,128)(2,1)S(1)}, u32[]{:S(2)}, u32[]{:S(2)}) collective-permute-start(bf16[64,512]{1,0:T(8,128)(2,1)S(1)} %get-tuple-element.29), channel_id=1, source_target_pairs={{0,8},{1,9},{2,10},{3,11},{4,12},{5,13},{6,14},{7,15},{8,16},{9,17... | collective-permute-start | bytes 196616 | tf_op jit(solution)/shard_map/ppermute | solution.py:360
  22.1 2.4 %collective-permute-start.4 = (bf16[64,512]{1,0:T(8,128)(2,1)S(1)}, bf16[64,512]{1,0:T(8,128)(2,1)S(1)}, u32[]{:S(2)}, u32[]{:S(2)}) collective-permute-start(bf16[64,512]{1,0:T(8,128)(2,1)S(1)} %get-tuple-element.30), channel_id=1, source_target_pairs={{0,16},{1,17},{2,18},{3,19},{4,20},{5,21},{6,22},{7,23},{8,24},{9,... | collective-permute-start | bytes 196616 | tf_op jit(solution)/shard_map/ppermute | solution.py:360
  24.6 1.2 %collective-permute-start.5 = (bf16[64,512]{1,0:T(8,128)(2,1)S(1)}, bf16[64,512]{1,0:T(8,128)(2,1)S(1)}, u32[]{:S(2)}, u32[]{:S(2)}) collective-permute-start(bf16[64,512]{1,0:T(8,128)(2,1)S(1)} %get-tuple-element.31), channel_id=1, source_target_pairs={{0,24},{1,25},{2,26},{3,27},{4,28},{5,29},{6,30},{7,31},{8,0},{9,1... | collective-permute-start | bytes 196616 | tf_op jit(solution)/shard_map/ppermute | solution.py:360
  25.7 0.0 all-to-all-done
  25.7 1.0 %select.1 = bf16[256,512]{1,0:T(8,128)(2,1)} custom-call(s32[1,512]{1,0:T(1,128)S(1)} %get-tuple-element.22.row_key_ref.refs_4_, bf16[256,512]{1,0:T(8,128)(2,1)S(1)} %get-tuple-element.23.fresh_ref, bf16[512,512]{1,0:T(8,128)(2,1)S(1)} %bitcast.14), custom_call_target="tpu_custom_call" | custom-call | flops 17179869184 | bytes 268435456 | tf_op jit(solution)/shard_map/select/pallas_call | solution.py:372
  26.7 7.0 %all-to-all-start.1 = ((bf16[32,8,512]{2,1,0:T(8,128)(2,1)}), bf16[32,8,512]{2,1,0:T(8,128)(2,1)S(1)}, u32[]{:S(2)}, u32[]{:S(2)}) async-start(bf16[32,8,512]{2,1,0:T(8,128)(2,1)} %bitcast.4), calls=%async_computation.1 | async-start | bytes 524288 | tf_op jit(solution)/shard_map/all_to_all | solution.py:381
  33.7 0.0 collective-permute-done.3.refs_1_
  33.7 0.0 collective-permute-done.4.refs_2_
  33.7 0.0 collective-permute-done.5.refs_3_
  33.7 0.0 copy-start
  33.7 0.0 copy-start.1
  33.7 0.0 copy-start.2
  33.8 0.2 taps_core.1
  34.0 0.3 collective-permute-start.6
  34.3 1.1 %collective-permute-done.6.refs_1_ = bf16[128,512]{1,0:T(8,128)(2,1)S(1)} collective-permute-done((bf16[128,512]{1,0:T(8,128)(2,1)S(1)}, bf16[128,512]{1,0:T(8,128)(2,1)S(1)}, u32[]{:S(2)}, u32[]{:S(2)}) %collective-permute-start.6) | collective-permute-done | bytes 131104 | tf_op jit(solution)/shard_map/ppermute | solution.py:370
  35.4 0.6 %copy-done.4 = f32[32]{0:T(128)S(1)} copy-done((f32[32]{0:T(128)S(1)}, f32[32]{0:T(128)}, u32[]{:S(2)}) %copy-start.4) | copy-done | bytes 152
  36.1 1.8 %filter.1 = (f32[2,256,512]{2,1,0:T(8,128)S(1)}, bf16[512,256]{1,0:T(8,128)(2,1)S(1)}, f32[1,512]{1,0:T(1,128)S(1)}) custom-call(bf16[128,512]{1,0:T(8,128)(2,1)S(1)} %get-tuple-element.32.refs_0_, bf16[128,512]{1,0:T(8,128)(2,1)S(1)} %collective-permute-done.6.refs_1_, f32[1,32]{1,0:T(1,128)S(1)} %bitcast.16, bf16[512,256]{1,0:T(8,128)(2,1)} %constant.10.clone.refs_3_, ...), custom_call_target="tpu_custom_call" | custom-call | flops 268435456 | bytes 268435456 | tf_op jit(solution)/shard_map/filter/pallas_call | solution.py:386
  37.9 4.1 %all-to-all-done.1 = bf16[32,8,512]{2,1,0:T(8,128)(2,1)S(1)} async-done(((bf16[32,8,512]{2,1,0:T(8,128)(2,1)}), bf16[32,8,512]{2,1,0:T(8,128)(2,1)S(1)}, u32[]{:S(2)}, u32[]{:S(2)}) %all-to-all-start.1) | async-done | bytes 262176 | tf_op jit(solution)/shard_map/all_to_all | solution.py:381
  42.0 1.5 %conv.1 = bf16[256,512]{1,0:T(8,128)(2,1)S(1)} custom-call(bf16[256,512]{1,0:T(8,128)(2,1)S(1)} %bitcast.11, f32[2,256,512]{2,1,0:T(8,128)S(1)} %get-tuple-element.34.filter_ref, f32[1,512]{1,0:T(1,128)S(1)} %get-tuple-element.35.gain_ref, bf16[512,256]{1,0:T(8,128)(2,1)S(1)} %get-tuple-element.36.refs_0_, f32[256,128]{1,0:T(8,128)S(1)} %copy-done.2, ...), custom_call_target="tpu_custom_call" | custom-call | bytes 8388608 | tf_op jit(solution)/shard_map/conv/pallas_call | solution.py:399
  43.6 0.0 copy-start.3
  43.6 12.4 %all_to_all.15 = bf16[32,8,512]{2,1,0:T(8,128)(2,1)S(1)} all-to-all(bf16[32,8,512]{2,1,0:T(8,128)(2,1)S(1)} %bitcast.12), channel_id=1, replica_groups={{0,13,26,7,20,1,14,27,8,21,2,15,28,9,22,3,16,29,10,23,4,17,30,11,24,5,1..., dimensions={0} | all-to-all | bytes 524288 | tf_op jit(solution)/shard_map/all_to_all | solution.py:409
  56.0 0.9 %gate.1 = bf16[32,4096]{1,0:T(8,128)(2,1)} custom-call(bf16[256,512]{1,0:T(8,128)(2,1)S(1)} %bitcast.13, bf16[32,4096]{1,0:T(8,128)(2,1)S(1)} %bitcast.15), custom_call_target="tpu_custom_call" | custom-call | bytes 1048576 | tf_op jit(solution)/shard_map/gate/pallas_call | solution.py:413
  (5 shorter events, 0.0 us)
Async XLA Ops:
  1.8 23.9 %all-to-all-start = ((bf16[8,2,32,512]{3,2,1,0:T(8,128)(2,1)}), bf16[8,2,32,512]{3,2,1,0:T(8,128)(2,1)S(1)}, u32[]{:S(2)}, u32[]{:S(2)}) async-start(bf16[8,2,32,512]{3,2,1,0:T(8,128)(2,1)} %get-tuple-element.24), calls=%async_computation | async-start | bytes 1048576 | tf_op jit(solution)/shard_map/all_to_all | solution.py:325
  13.0 7.0 %collective-permute-start = (bf16[64,512]{1,0:T(8,128)(2,1)S(1)}, bf16[64,512]{1,0:T(8,128)(2,1)S(1)}, u32[]{:S(2)}, u32[]{:S(2)}) collective-permute-start(bf16[64,512]{1,0:T(8,128)(2,1)S(1)} %get-tuple-element.25), channel_id=1, source_target_pairs={{0,2},{1,3},{2,4},{3,5},{4,6},{5,7},{6,0},{7,1},{8,10},{9,11},{10,... | collective-permute-start | bytes 196616 | tf_op jit(solution)/shard_map/ppermute | solution.py:329
  14.3 5.7 %collective-permute-start.1 = (bf16[64,512]{1,0:T(8,128)(2,1)S(1)}, bf16[64,512]{1,0:T(8,128)(2,1)S(1)}, u32[]{:S(2)}, u32[]{:S(2)}) collective-permute-start(bf16[64,512]{1,0:T(8,128)(2,1)S(1)} %get-tuple-element.26), channel_id=1, source_target_pairs={{0,4},{1,5},{2,6},{3,7},{4,0},{5,1},{6,2},{7,3},{8,12},{9,13},{10,... | collective-permute-start | bytes 196616 | tf_op jit(solution)/shard_map/ppermute | solution.py:329
  16.9 3.7 %collective-permute-start.2 = (bf16[64,512]{1,0:T(8,128)(2,1)S(1)}, bf16[64,512]{1,0:T(8,128)(2,1)S(1)}, u32[]{:S(2)}, u32[]{:S(2)}) collective-permute-start(bf16[64,512]{1,0:T(8,128)(2,1)S(1)} %get-tuple-element.27), channel_id=1, source_target_pairs={{0,6},{1,7},{2,0},{3,1},{4,2},{5,3},{6,4},{7,5},{8,14},{9,15},{10,... | collective-permute-start | bytes 196616 | tf_op jit(solution)/shard_map/ppermute | solution.py:329
  20.8 12.9 %collective-permute-start.3 = (bf16[64,512]{1,0:T(8,128)(2,1)S(1)}, bf16[64,512]{1,0:T(8,128)(2,1)S(1)}, u32[]{:S(2)}, u32[]{:S(2)}) collective-permute-start(bf16[64,512]{1,0:T(8,128)(2,1)S(1)} %get-tuple-element.29), channel_id=1, source_target_pairs={{0,8},{1,9},{2,10},{3,11},{4,12},{5,13},{6,14},{7,15},{8,16},{9,17... | collective-permute-start | bytes 196616 | tf_op jit(solution)/shard_map/ppermute | solution.py:360
  22.1 11.6 %collective-permute-start.4 = (bf16[64,512]{1,0:T(8,128)(2,1)S(1)}, bf16[64,512]{1,0:T(8,128)(2,1)S(1)}, u32[]{:S(2)}, u32[]{:S(2)}) collective-permute-start(bf16[64,512]{1,0:T(8,128)(2,1)S(1)} %get-tuple-element.30), channel_id=1, source_target_pairs={{0,16},{1,17},{2,18},{3,19},{4,20},{5,21},{6,22},{7,23},{8,24},{9,... | collective-permute-start | bytes 196616 | tf_op jit(solution)/shard_map/ppermute | solution.py:360
  24.6 9.2 %collective-permute-start.5 = (bf16[64,512]{1,0:T(8,128)(2,1)S(1)}, bf16[64,512]{1,0:T(8,128)(2,1)S(1)}, u32[]{:S(2)}, u32[]{:S(2)}) collective-permute-start(bf16[64,512]{1,0:T(8,128)(2,1)S(1)} %get-tuple-element.31), channel_id=1, source_target_pairs={{0,24},{1,25},{2,26},{3,27},{4,28},{5,29},{6,30},{7,31},{8,0},{9,1... | collective-permute-start | bytes 196616 | tf_op jit(solution)/shard_map/ppermute | solution.py:360
  26.7 15.3 %all-to-all-start.1 = ((bf16[32,8,512]{2,1,0:T(8,128)(2,1)}), bf16[32,8,512]{2,1,0:T(8,128)(2,1)S(1)}, u32[]{:S(2)}, u32[]{:S(2)}) async-start(bf16[32,8,512]{2,1,0:T(8,128)(2,1)} %bitcast.4), calls=%async_computation.1 | async-start | bytes 524288 | tf_op jit(solution)/shard_map/all_to_all | solution.py:381
  33.7 1.7 %copy-start = (bf16[2,256,512]{2,1,0:T(8,128)(2,1)S(1)}, bf16[2,256,512]{2,1,0:T(8,128)(2,1)}, u32[]{:S(2)}) copy-start(bf16[2,256,512]{2,1,0:T(8,128)(2,1)} %constant.13.clone.refs_6_.refs_3_) | copy-start | bytes 1572868
  33.7 1.7 %copy-start.1 = (f32[256,128]{1,0:T(8,128)S(1)}, f32[256,128]{1,0:T(8,128)}, u32[]{:S(2)}) copy-start(f32[256,128]{1,0:T(8,128)} %constant.12.clone.refs_5_.refs_2_) | copy-start | bytes 393220
  33.7 1.7 %copy-start.2 = (f32[256,128]{1,0:T(8,128)S(1)}, f32[256,128]{1,0:T(8,128)}, u32[]{:S(2)}) copy-start(f32[256,128]{1,0:T(8,128)} %constant.11.clone.refs_4_.refs_1_) | copy-start | bytes 393220
  34.0 1.4 %collective-permute-start.6 = (bf16[128,512]{1,0:T(8,128)(2,1)S(1)}, bf16[128,512]{1,0:T(8,128)(2,1)S(1)}, u32[]{:S(2)}, u32[]{:S(2)}) collective-permute-start(bf16[128,512]{1,0:T(8,128)(2,1)S(1)} %get-tuple-element.33), channel_id=1, source_target_pairs={{0,1},{1,0},{2,3},{3,2},{4,5},{5,4},{6,7},{7,6},{8,9},{9,8},{10,11... | collective-permute-start | bytes 393224 | tf_op jit(solution)/shard_map/ppermute | solution.py:370
  35.4 0.7 %copy-start.4 = (f32[32]{0:T(128)S(1)}, f32[32]{0:T(128)}, u32[]{:S(2)}) copy-start(f32[32]{0:T(128)} %param.18) | copy-start | bytes 388
  43.6 12.5 %copy-start.3 = (bf16[1,32,4096]{2,1,0:T(8,128)(2,1)S(1)}, bf16[1,32,4096]{2,1,0:T(8,128)(2,1)}, u32[]{:S(2)}) copy-start(bf16[1,32,4096]{2,1,0:T(8,128)(2,1)} %param.14) | copy-start | bytes 786436

commit v8 on v7

--- a/solution.py
+++ b/solution.py
@@ -13,8 +13,8 @@
 N2 = 512
 HALF = N2 // 2
 TOTAL = N1 * N2
-RANKS = (4, 0, 5, 1, 6, 2, 7, 3)
-STEP, UNSTEP = 13, 5
+RANKS = (4, 0, 7, 1, 6, 2, 5, 3)
+STEP, UNSTEP = 11, 3
 SEQ_RANKS = tuple(STEP * r % 32 for r in range(32))
 BF16 = jnp.bfloat16
 F32 = jnp.float32

time: 57.3 us -> 57.7 us (level)
  no operation moved by 1% of the time
where the time goes in v8:
time: 57.7 us; the launch traced here: 57.3 us
  starting transfers between devices  28.3 us (49%)
  blocking collectives  12.5 us (22%)
  Pallas kernels  8.9 us (15%)
  waiting for transfers between devices  6.14 us (11%)
  between operations  0.79 us (1%)
  local copies, waits for them, and re-layouts  0.67 us (1%)
    all_to_all x1, blocking collectives, shards(): lax.all_to_all(convolved.reshape(32, 8, N2), 'seq', split_axis=0, concat_...  12.5 us
    all_to_all x1, starting transfers between devices, shards(): lax.all_to_all(slabs, 'grp', split_axis=0, concat_axis=0, axis_index_grou...  11.1 us
    all_to_all x1, starting transfers between devices, shards(): lax.all_to_all(send.reshape(32, 8, N2), 'seq', split_axis=0, concat_axis=...  6.96 us
    ppermute x3, starting transfers between devices, shards(): lax.ppermute(along_y[d], 'seq', hops(0, d, 0))  4.99 us
    ppermute x3, starting transfers between devices, shards(): lax.ppermute(along_x[d], 'seq', hops(d, 0, 0))  4.9 us
    all_to_all x1, waiting for transfers between devices, shards(): lax.all_to_all(send.reshape(32, 8, N2), 'seq', split_axis=0, concat_axis=...  4.44 us
    pallas_call x1, Pallas kernels, shards(): call(slabs_kernel, out_shape=(pltpu.HBM((8, 2, 32, N2), BF16),) + (rows_o...  1.83 us
    pallas_call x1, Pallas kernels, shards(): call(filter_kernel, out_shape=(jax.ShapeDtypeStruct((2, N1, N2), F32), ja...  1.8 us
  transfers between devices with their start and end apart: 9, of which 3 were waited for; matrix products, arithmetic and copies ran while one was open for 0% of the time, Pallas kernels for 8%

profile of v8, /device:TPU:1, one launch (start us, length us, event | category | flops | bytes accessed | tf_op | source)
XLA Modules:
  0.0 57.3 jit_solution(12388635264808222608)
XLA Ops:
  0.0 1.8 %slabs.1 = (bf16[8,2,32,512]{3,2,1,0:T(8,128)(2,1)}, bf16[64,512]{1,0:T(8,128)(2,1)S(1)}, bf16[64,512]{1,0:T(8,128)(2,1)S(1)}, bf16[64,512]{1,0:T(8,128)(2,1)S(1)}, bf16[64,512]{1,0:T(8,128)(2,1)S(1)}) custom-call(bf16[8,2,32,512]{3,2,1,0:T(8,128)(2,1)} %bitcast.17, f32[32,4096]{1,0:T(8,128)} %taps_hbm.1), custom_call_target="tpu_custom_call" | custom-call | bytes 1048576 | tf_op jit(solution)/shard_map/slabs/pallas_call | solution.py:311
  1.8 11.1 %all-to-all-start = ((bf16[8,2,32,512]{3,2,1,0:T(8,128)(2,1)}), bf16[8,2,32,512]{3,2,1,0:T(8,128)(2,1)S(1)}, u32[]{:S(2)}, u32[]{:S(2)}) async-start(bf16[8,2,32,512]{3,2,1,0:T(8,128)(2,1)} %get-tuple-element.24), calls=%async_computation | async-start | bytes 1048576 | tf_op jit(solution)/shard_map/all_to_all | solution.py:325
  13.0 1.3 %collective-permute-start = (bf16[64,512]{1,0:T(8,128)(2,1)S(1)}, bf16[64,512]{1,0:T(8,128)(2,1)S(1)}, u32[]{:S(2)}, u32[]{:S(2)}) collective-permute-start(bf16[64,512]{1,0:T(8,128)(2,1)S(1)} %get-tuple-element.25), channel_id=1, source_target_pairs={{0,2},{1,3},{2,4},{3,5},{4,6},{5,7},{6,0},{7,1},{8,10},{9,11},{10,... | collective-permute-start | bytes 196616 | tf_op jit(solution)/shard_map/ppermute | solution.py:329
  14.3 2.6 %collective-permute-start.1 = (bf16[64,512]{1,0:T(8,128)(2,1)S(1)}, bf16[64,512]{1,0:T(8,128)(2,1)S(1)}, u32[]{:S(2)}, u32[]{:S(2)}) collective-permute-start(bf16[64,512]{1,0:T(8,128)(2,1)S(1)} %get-tuple-element.26), channel_id=1, source_target_pairs={{0,4},{1,5},{2,6},{3,7},{4,0},{5,1},{6,2},{7,3},{8,12},{9,13},{10,... | collective-permute-start | bytes 196616 | tf_op jit(solution)/shard_map/ppermute | solution.py:329
  16.9 1.1 %collective-permute-start.2 = (bf16[64,512]{1,0:T(8,128)(2,1)S(1)}, bf16[64,512]{1,0:T(8,128)(2,1)S(1)}, u32[]{:S(2)}, u32[]{:S(2)}) collective-permute-start(bf16[64,512]{1,0:T(8,128)(2,1)S(1)} %get-tuple-element.27), channel_id=1, source_target_pairs={{0,6},{1,7},{2,0},{3,1},{4,2},{5,3},{6,4},{7,5},{8,14},{9,15},{10,... | collective-permute-start | bytes 196616 | tf_op jit(solution)/shard_map/ppermute | solution.py:329
  18.6 1.4 %stage.1 = (bf16[256,512]{1,0:T(8,128)(2,1)S(1)}, s32[1,512]{1,0:T(1,128)S(1)}) custom-call(s32[1,8]{1,0:T(1,128)} %owner_hbm.1, s32[1,8]{1,0:T(1,128)} %slot_hbm.1, s32[1]{0:T(128)S(6)} %copy.15.suffix_ref, bf16[32,4096]{1,0:T(8,128)(2,1)} %bitcast.18, bf16[32,4096]{1,0:T(8,128)(2,1)} %bitcast.19, bf16[64,512]{1,0:T(8,128)(2,1)S(1)} %get-tuple-element.21.tie_ref.refs_0_), custom_call_target="tpu_custom_call" | custom-call | bytes 1048576 | tf_op jit(solution)/shard_map/stage/pallas_call | solution.py:331
  20.0 0.0 collective-permute-done.refs_1_
  20.0 0.0 collective-permute-done.1.refs_2_
  20.0 0.6 collective-permute-done.2.refs_3_
  20.6 0.2 taps_x.1
  20.8 1.3 %collective-permute-start.3 = (bf16[64,512]{1,0:T(8,128)(2,1)S(1)}, bf16[64,512]{1,0:T(8,128)(2,1)S(1)}, u32[]{:S(2)}, u32[]{:S(2)}) collective-permute-start(bf16[64,512]{1,0:T(8,128)(2,1)S(1)} %get-tuple-element.29), channel_id=1, source_target_pairs={{0,8},{1,9},{2,10},{3,11},{4,12},{5,13},{6,14},{7,15},{8,16},{9,17... | collective-permute-start | bytes 196616 | tf_op jit(solution)/shard_map/ppermute | solution.py:360
  22.1 2.4 %collective-permute-start.4 = (bf16[64,512]{1,0:T(8,128)(2,1)S(1)}, bf16[64,512]{1,0:T(8,128)(2,1)S(1)}, u32[]{:S(2)}, u32[]{:S(2)}) collective-permute-start(bf16[64,512]{1,0:T(8,128)(2,1)S(1)} %get-tuple-element.30), channel_id=1, source_target_pairs={{0,16},{1,17},{2,18},{3,19},{4,20},{5,21},{6,22},{7,23},{8,24},{9,... | collective-permute-start | bytes 196616 | tf_op jit(solution)/shard_map/ppermute | solution.py:360
  24.6 1.2 %collective-permute-start.5 = (bf16[64,512]{1,0:T(8,128)(2,1)S(1)}, bf16[64,512]{1,0:T(8,128)(2,1)S(1)}, u32[]{:S(2)}, u32[]{:S(2)}) collective-permute-start(bf16[64,512]{1,0:T(8,128)(2,1)S(1)} %get-tuple-element.31), channel_id=1, source_target_pairs={{0,24},{1,25},{2,26},{3,27},{4,28},{5,29},{6,30},{7,31},{8,0},{9,1... | collective-permute-start | bytes 196616 | tf_op jit(solution)/shard_map/ppermute | solution.py:360
  25.7 0.0 all-to-all-done
  25.7 1.0 %select.1 = bf16[256,512]{1,0:T(8,128)(2,1)} custom-call(s32[1,512]{1,0:T(1,128)S(1)} %get-tuple-element.22.row_key_ref.refs_4_, bf16[256,512]{1,0:T(8,128)(2,1)S(1)} %get-tuple-element.23.fresh_ref, bf16[512,512]{1,0:T(8,128)(2,1)S(1)} %bitcast.14), custom_call_target="tpu_custom_call" | custom-call | flops 17179869184 | bytes 268435456 | tf_op jit(solution)/shard_map/select/pallas_call | solution.py:372
  26.7 7.0 %all-to-all-start.1 = ((bf16[32,8,512]{2,1,0:T(8,128)(2,1)}), bf16[32,8,512]{2,1,0:T(8,128)(2,1)S(1)}, u32[]{:S(2)}, u32[]{:S(2)}) async-start(bf16[32,8,512]{2,1,0:T(8,128)(2,1)} %bitcast.4), calls=%async_computation.1 | async-start | bytes 524288 | tf_op jit(solution)/shard_map/all_to_all | solution.py:381
  33.7 0.0 collective-permute-done.3.refs_1_
  33.7 0.0 collective-permute-done.4.refs_2_
  33.7 0.0 collective-permute-done.5.refs_3_
  33.7 0.0 copy-start
  33.7 0.0 copy-start.1
  33.7 0.0 copy-start.2
  33.8 0.2 taps_core.1
  34.0 0.3 collective-permute-start.6
  34.3 1.1 %collective-permute-done.6.refs_1_ = bf16[128,512]{1,0:T(8,128)(2,1)S(1)} collective-permute-done((bf16[128,512]{1,0:T(8,128)(2,1)S(1)}, bf16[128,512]{1,0:T(8,128)(2,1)S(1)}, u32[]{:S(2)}, u32[]{:S(2)}) %collective-permute-start.6) | collective-permute-done | bytes 131104 | tf_op jit(solution)/shard_map/ppermute | solution.py:370
  35.4 0.6 %copy-done.4 = f32[32]{0:T(128)S(1)} copy-done((f32[32]{0:T(128)S(1)}, f32[32]{0:T(128)}, u32[]{:S(2)}) %copy-start.4) | copy-done | bytes 152
  36.1 1.8 %filter.1 = (f32[2,256,512]{2,1,0:T(8,128)S(1)}, bf16[512,256]{1,0:T(8,128)(2,1)S(1)}, f32[1,512]{1,0:T(1,128)S(1)}) custom-call(bf16[128,512]{1,0:T(8,128)(2,1)S(1)} %get-tuple-element.32.refs_0_, bf16[128,512]{1,0:T(8,128)(2,1)S(1)} %collective-permute-done.6.refs_1_, f32[1,32]{1,0:T(1,128)S(1)} %bitcast.16, bf16[512,256]{1,0:T(8,128)(2,1)} %constant.10.clone.refs_3_, ...), custom_call_target="tpu_custom_call" | custom-call | flops 268435456 | bytes 268435456 | tf_op jit(solution)/shard_map/filter/pallas_call | solution.py:386
  37.9 4.4 %all-to-all-done.1 = bf16[32,8,512]{2,1,0:T(8,128)(2,1)S(1)} async-done(((bf16[32,8,512]{2,1,0:T(8,128)(2,1)}), bf16[32,8,512]{2,1,0:T(8,128)(2,1)S(1)}, u32[]{:S(2)}, u32[]{:S(2)}) %all-to-all-start.1) | async-done | bytes 262176 | tf_op jit(solution)/shard_map/all_to_all | solution.py:381
  42.3 1.5 %conv.1 = bf16[256,512]{1,0:T(8,128)(2,1)S(1)} custom-call(bf16[256,512]{1,0:T(8,128)(2,1)S(1)} %bitcast.11, f32[2,256,512]{2,1,0:T(8,128)S(1)} %get-tuple-element.34.filter_ref, f32[1,512]{1,0:T(1,128)S(1)} %get-tuple-element.35.gain_ref, bf16[512,256]{1,0:T(8,128)(2,1)S(1)} %get-tuple-element.36.refs_0_, f32[256,128]{1,0:T(8,128)S(1)} %copy-done.2, ...), custom_call_target="tpu_custom_call" | custom-call | bytes 8388608 | tf_op jit(solution)/shard_map/conv/pallas_call | solution.py:399
  43.9 0.0 copy-start.3
  43.9 12.5 %all_to_all.15 = bf16[32,8,512]{2,1,0:T(8,128)(2,1)S(1)} all-to-all(bf16[32,8,512]{2,1,0:T(8,128)(2,1)S(1)} %bitcast.12), channel_id=1, replica_groups={{0,11,22,1,12,23,2,13,24,3,14,25,4,15,26,5,16,27,6,17,28,7,18,29,8,19,3..., dimensions={0} | all-to-all | bytes 524288 | tf_op jit(solution)/shard_map/all_to_all | solution.py:409
  56.4 0.9 %gate.1 = bf16[32,4096]{1,0:T(8,128)(2,1)} custom-call(bf16[256,512]{1,0:T(8,128)(2,1)S(1)} %bitcast.13, bf16[32,4096]{1,0:T(8,128)(2,1)S(1)} %bitcast.15), custom_call_target="tpu_custom_call" | custom-call | bytes 1048576 | tf_op jit(solution)/shard_map/gate/pallas_call | solution.py:413
  (5 shorter events, 0.0 us)
Async XLA Ops:
  1.8 23.9 %all-to-all-start = ((bf16[8,2,32,512]{3,2,1,0:T(8,128)(2,1)}), bf16[8,2,32,512]{3,2,1,0:T(8,128)(2,1)S(1)}, u32[]{:S(2)}, u32[]{:S(2)}) async-start(bf16[8,2,32,512]{3,2,1,0:T(8,128)(2,1)} %get-tuple-element.24), calls=%async_computation | async-start | bytes 1048576 | tf_op jit(solution)/shard_map/all_to_all | solution.py:325
  13.0 7.0 %collective-permute-start = (bf16[64,512]{1,0:T(8,128)(2,1)S(1)}, bf16[64,512]{1,0:T(8,128)(2,1)S(1)}, u32[]{:S(2)}, u32[]{:S(2)}) collective-permute-start(bf16[64,512]{1,0:T(8,128)(2,1)S(1)} %get-tuple-element.25), channel_id=1, source_target_pairs={{0,2},{1,3},{2,4},{3,5},{4,6},{5,7},{6,0},{7,1},{8,10},{9,11},{10,... | collective-permute-start | bytes 196616 | tf_op jit(solution)/shard_map/ppermute | solution.py:329
  14.3 5.7 %collective-permute-start.1 = (bf16[64,512]{1,0:T(8,128)(2,1)S(1)}, bf16[64,512]{1,0:T(8,128)(2,1)S(1)}, u32[]{:S(2)}, u32[]{:S(2)}) collective-permute-start(bf16[64,512]{1,0:T(8,128)(2,1)S(1)} %get-tuple-element.26), channel_id=1, source_target_pairs={{0,4},{1,5},{2,6},{3,7},{4,0},{5,1},{6,2},{7,3},{8,12},{9,13},{10,... | collective-permute-start | bytes 196616 | tf_op jit(solution)/shard_map/ppermute | solution.py:329
  16.9 3.7 %collective-permute-start.2 = (bf16[64,512]{1,0:T(8,128)(2,1)S(1)}, bf16[64,512]{1,0:T(8,128)(2,1)S(1)}, u32[]{:S(2)}, u32[]{:S(2)}) collective-permute-start(bf16[64,512]{1,0:T(8,128)(2,1)S(1)} %get-tuple-element.27), channel_id=1, source_target_pairs={{0,6},{1,7},{2,0},{3,1},{4,2},{5,3},{6,4},{7,5},{8,14},{9,15},{10,... | collective-permute-start | bytes 196616 | tf_op jit(solution)/shard_map/ppermute | solution.py:329
  20.8 12.9 %collective-permute-start.3 = (bf16[64,512]{1,0:T(8,128)(2,1)S(1)}, bf16[64,512]{1,0:T(8,128)(2,1)S(1)}, u32[]{:S(2)}, u32[]{:S(2)}) collective-permute-start(bf16[64,512]{1,0:T(8,128)(2,1)S(1)} %get-tuple-element.29), channel_id=1, source_target_pairs={{0,8},{1,9},{2,10},{3,11},{4,12},{5,13},{6,14},{7,15},{8,16},{9,17... | collective-permute-start | bytes 196616 | tf_op jit(solution)/shard_map/ppermute | solution.py:360
  22.1 11.6 %collective-permute-start.4 = (bf16[64,512]{1,0:T(8,128)(2,1)S(1)}, bf16[64,512]{1,0:T(8,128)(2,1)S(1)}, u32[]{:S(2)}, u32[]{:S(2)}) collective-permute-start(bf16[64,512]{1,0:T(8,128)(2,1)S(1)} %get-tuple-element.30), channel_id=1, source_target_pairs={{0,16},{1,17},{2,18},{3,19},{4,20},{5,21},{6,22},{7,23},{8,24},{9,... | collective-permute-start | bytes 196616 | tf_op jit(solution)/shard_map/ppermute | solution.py:360
  24.6 9.2 %collective-permute-start.5 = (bf16[64,512]{1,0:T(8,128)(2,1)S(1)}, bf16[64,512]{1,0:T(8,128)(2,1)S(1)}, u32[]{:S(2)}, u32[]{:S(2)}) collective-permute-start(bf16[64,512]{1,0:T(8,128)(2,1)S(1)} %get-tuple-element.31), channel_id=1, source_target_pairs={{0,24},{1,25},{2,26},{3,27},{4,28},{5,29},{6,30},{7,31},{8,0},{9,1... | collective-permute-start | bytes 196616 | tf_op jit(solution)/shard_map/ppermute | solution.py:360
  26.7 15.6 %all-to-all-start.1 = ((bf16[32,8,512]{2,1,0:T(8,128)(2,1)}), bf16[32,8,512]{2,1,0:T(8,128)(2,1)S(1)}, u32[]{:S(2)}, u32[]{:S(2)}) async-start(bf16[32,8,512]{2,1,0:T(8,128)(2,1)} %bitcast.4), calls=%async_computation.1 | async-start | bytes 524288 | tf_op jit(solution)/shard_map/all_to_all | solution.py:381
  33.7 1.7 %copy-start = (bf16[2,256,512]{2,1,0:T(8,128)(2,1)S(1)}, bf16[2,256,512]{2,1,0:T(8,128)(2,1)}, u32[]{:S(2)}) copy-start(bf16[2,256,512]{2,1,0:T(8,128)(2,1)} %constant.13.clone.refs_6_.refs_3_) | copy-start | bytes 1572868
  33.7 1.7 %copy-start.1 = (f32[256,128]{1,0:T(8,128)S(1)}, f32[256,128]{1,0:T(8,128)}, u32[]{:S(2)}) copy-start(f32[256,128]{1,0:T(8,128)} %constant.12.clone.refs_5_.refs_2_) | copy-start | bytes 393220
  33.7 1.7 %copy-start.2 = (f32[256,128]{1,0:T(8,128)S(1)}, f32[256,128]{1,0:T(8,128)}, u32[]{:S(2)}) copy-start(f32[256,128]{1,0:T(8,128)} %constant.11.clone.refs_4_.refs_1_) | copy-start | bytes 393220
  34.0 1.4 %collective-permute-start.6 = (bf16[128,512]{1,0:T(8,128)(2,1)S(1)}, bf16[128,512]{1,0:T(8,128)(2,1)S(1)}, u32[]{:S(2)}, u32[]{:S(2)}) collective-permute-start(bf16[128,512]{1,0:T(8,128)(2,1)S(1)} %get-tuple-element.33), channel_id=1, source_target_pairs={{0,1},{1,0},{2,3},{3,2},{4,5},{5,4},{6,7},{7,6},{8,9},{9,8},{10,11... | collective-permute-start | bytes 393224 | tf_op jit(solution)/shard_map/ppermute | solution.py:370
  35.4 0.7 %copy-start.4 = (f32[32]{0:T(128)S(1)}, f32[32]{0:T(128)}, u32[]{:S(2)}) copy-start(f32[32]{0:T(128)} %param.18) | copy-start | bytes 388
  43.9 12.6 %copy-start.3 = (bf16[1,32,4096]{2,1,0:T(8,128)(2,1)S(1)}, bf16[1,32,4096]{2,1,0:T(8,128)(2,1)}, u32[]{:S(2)}) copy-start(bf16[1,32,4096]{2,1,0:T(8,128)(2,1)} %param.14) | copy-start | bytes 786436
